TPU v7x, 128 devices: a whole 4x4x4 slice. The times are simulated.
128 devices in a mesh: space: 16 (over x_lo, z, core), subj: 8 (over y, x_hi).
Axes of the slice: x: 4 (x_hi: 2, x_lo: 2; x = x_hi * 2 + x_lo), y: 4, z: 4, core: 2. Of those that a mesh axis runs over, the one named last changes fastest.
Arguments:
- template: float32 [128, 64, 256], P('space', 'subj'), may hold values from -6 to 6
- momentum: float32 [32, 3, 128, 64, 256], P('subj', None, 'space'), may hold values from -6 to 6
- targets: float32 [32, 128, 64, 256], P('subj', 'space'), may hold values from -6 to 6
- step_count: int32 [32], P('subj'), may hold values from 1 to 4, as said below
Outputs:
- warped: float32 [32, 128, 64, 256], P('subj', 'space')
- template_gradient: float32 [128, 64, 256], P('space', 'subj')
- momentum_gradient: float32 [32, 3, 128, 64, 256], P('subj', None, 'space')
Inputs may be any that keep to these rules, and one draw needn't show every extreme that they name: `step_count`: each subject takes between 1 and 4 steps; some subject takes 4 and some takes 1.
All inputs are finite; a program needn't handle non-finite values.
Results may differ from a plain program's by a relative error of at most 0.0003.
Values sent between devices are 32-bit elements; how exact they have to be, the bound alone decides.
No kernel may reach another device: no remote copies, remote signals or barrier semaphores. Data moves between devices by JAX's collectives and lax.ppermute only.
A program may use at most 192 MiB of HBM per device.

v0:
```python
import jax
import jax.numpy as jnp
from jax import lax
from jax.sharding import PartitionSpec as P

STEPS = 4


time_step = 0.15
smoothing = 0.1


def with_halo(block, sides, width):
    for axis, dim in sides:
        count = lax.axis_size(axis)
        forward = [(i, i + 1) for i in range(count - 1)]
        backward = [(target, source) for source, target in forward]
        low = lax.ppermute(
            lax.slice_in_dim(block, block.shape[dim] - width, None, axis=dim), axis, forward
        )
        high = lax.ppermute(lax.slice_in_dim(block, 0, width, axis=dim), axis, backward)
        block = jnp.concatenate([low, block, high], axis=dim)
    return block


def central(field, axis):
    size = field.shape[axis]
    widths = [(0, 0)] * field.ndim
    widths[axis] = (1, 1)
    padded = jnp.pad(field, widths)
    upper = lax.slice_in_dim(padded, 2, size + 2, axis=axis)
    lower = lax.slice_in_dim(padded, 0, size, axis=axis)
    return 0.5 * (upper - lower)


def neighbours(field, axis):
    size = field.shape[axis]
    widths = [(0, 0)] * field.ndim
    widths[axis] = (1, 1)
    padded = jnp.pad(field, widths)
    return lax.slice_in_dim(padded, 2, size + 2, axis=axis) + lax.slice_in_dim(
        padded, 0, size, axis=axis
    )


def rim_kernel(padded):
    center = padded[:, :, 1:-1]
    nsum = padded[:, :, 2:] + padded[:, :, :-2] + neighbours(center, 3) + neighbours(center, 4)
    return center + smoothing * (nsum - 6.0 * center)


def shards(template, momentum, targets, step_count):
    whole_tmpl = lax.all_gather(template, "subj", axis=1, tiled=True)
    stored = []
    actives = []
    padded_mom = with_halo(momentum, (("space", 2),), 1)
    velocity = rim_kernel(padded_mom)
    vel_z = velocity[:, 0]
    vel_y = velocity[:, 1]
    vel_x = velocity[:, 2]
    image = jnp.broadcast_to(whole_tmpl[None], targets.shape)
    for step in range(STEPS):
        active = (step < step_count).astype(jnp.float32)[:, None, None, None]
        padded_img = with_halo(image, (("space", 1),), 1)
        diff_z = 0.5 * (padded_img[:, 2:] - padded_img[:, :-2])
        diff_y = central(image, 2)
        diff_x = central(image, 3)
        stored.append((diff_z, diff_y, diff_x))
        actives.append(active)
        image = image - time_step * active * (vel_z * diff_z + vel_y * diff_y + vel_x * diff_x)
    adjoint = image - targets
    grad_z = jnp.zeros_like(adjoint)
    grad_y = jnp.zeros_like(adjoint)
    grad_x = jnp.zeros_like(adjoint)
    for step in reversed(range(STEPS)):
        active = actives[step]
        diff_z, diff_y, diff_x = stored[step]
        scaled = -time_step * active * adjoint
        grad_z = grad_z + scaled * diff_z
        grad_y = grad_y + scaled * diff_y
        grad_x = grad_x + scaled * diff_x
        padded_flux = with_halo(vel_z * adjoint, (("space", 1),), 1)
        spread = 0.5 * (padded_flux[:, 2:] - padded_flux[:, :-2])
        spread = spread + central(vel_y * adjoint, 2) + central(vel_x * adjoint, 3)
        adjoint = adjoint + time_step * active * spread
    local_sum = jnp.sum(adjoint, axis=0)
    total = lax.psum(local_sum, "subj")
    rows = template.shape[1]
    start = lax.axis_index("subj") * rows
    template_gradient = lax.dynamic_slice_in_dim(total, start, rows, 1)
    velocity_grad = jnp.stack([grad_z, grad_y, grad_x], axis=1)
    padded_grad = with_halo(velocity_grad, (("space", 2),), 1)
    momentum_gradient = rim_kernel(padded_grad)
    return (image, template_gradient, momentum_gradient)


def solution(mesh):
    in_specs = (
        P("space", "subj", None),
        P("subj", None, "space", None, None),
        P("subj", "space", None, None),
        P("subj"),
    )
    out_specs = (
        P("subj", "space", None, None),
        P("space", "subj", None),
        P("subj", None, "space", None, None),
    )
    return jax.shard_map(shards, mesh=mesh, in_specs=in_specs, out_specs=out_specs, check_vma=False)
```

profile of v0, /device:TPU:6, one launch (start us, length us, event | category | flops | bytes accessed | tf_op | source)
XLA Modules:
  0.0 347.6 jit_solution(16976377590490229920)
XLA Ops:
  7.2 1.5 fusion.94
  8.8 1.9 collective-permute-start.1
  10.7 5.8 %collective-permute-start = (f32[4,3,1,64,256]{4,3,2,0,1:T(8,128)S(1)}, f32[4,3,1,64,256]{4,3,2,0,1:T(8,128)}, u32[]{:S(2)}, u32[]{:S(2)}) collective-permute-start(f32[4,3,1,64,256]{4,3,2,0,1:T(8,128)S(1)} %get-tuple-element.25), channel_id=1, source_target_pairs={{8,0},{16,8},{24,16},{32,24},{40,32},{48,40},{56,48},{64,56},{72,6... | collective-permute-start | bytes 2359304 | tf_op jit(solution)/shard_map/ppermute | solution.py:21
  16.5 42.4 %all_gather.3 = f32[8,64,256]{2,1,0:T(8,128)S(1)} all-gather(f32[8,8,256]{2,1,0:T(8,128)S(1)} %copy-done.24), channel_id=1, replica_groups=mesh['space'=16,'subj'=8] {'subj'}, dimensions={1}, use_global_device_ids=true | all-gather | bytes 589824 | tf_op jit(solution)/shard_map/all_gather | solution.py:53
  59.7 1.9 collective-permute-start.3
  62.3 6.0 %collective-permute-start.2 = (f32[4,1,64,256]{3,2,1,0:T(8,128)}, f32[4,1,64,256]{3,2,1,0:T(8,128)}, u32[]{:S(2)}, u32[]{:S(2)}) collective-permute-start(f32[4,1,64,256]{3,2,1,0:T(8,128)} %broadcast_in_dim.7), channel_id=1, source_target_pairs={{8,0},{16,8},{24,16},{32,24},{40,32},{48,40},{56,48},{64,56},{72,6... | collective-permute-start | bytes 786440 | tf_op jit(solution)/shard_map/ppermute | solution.py:21
  68.3 6.3 %copy.8 = f32[4,3,8,64,256]{4,3,2,0,1:T(8,128)} copy(f32[4,3,8,64,256]{4,3,2,1,0:T(8,128)} %param.5) | data formatting | bytes 12582912 | tf_op args[1]
  75.6 20.9 %fusion.12 = f32[4,3,8,64,256]{4,3,2,1,0:T(8,128)S(1)} fusion(f32[4,3,8,64,256]{4,3,2,1,0:T(8,128)S(1)} %bitcast.72, f32[4,3,8,64,256]{4,3,2,0,1:T(8,128)} %copy.8, f32[4,3,1,64,256]{4,3,2,0,1:T(8,128)} %copy-done.21, f32[4,3,1,64,256]{4,3,2,0,1:T(8,128)} %collective-permute-done), kind=kLoop, calls=%fused_computation.32 | loop fusion | flops 17301504 | bytes 20447232 | tf_op jit(solution)/shard_map/add | solution.py:49
  96.5 1.4 broadcast_in_dim.6
  97.9 3.5 %fusion.47 = f32[4,8,64,256]{3,2,1,0:T(8,128)S(1)} fusion(f32[4,8,64,256]{3,2,1,0:T(8,128)S(1)} %broadcast_in_dim.6, f32[4,1,64,256]{3,2,1,0:T(8,128)S(1)} %collective-permute-done.3, f32[4,1,64,256]{3,2,1,0:T(8,128)} %collective-permute-done.2, f32[4,3,8,64,256]{4,3,2,1,0:T(8,128)S(1)} %fusion.12, f32[4]{0:T(128)S(1)} %get-tuple-element.55), kind=kLoop, calls=%fused_computation.99 | loop fusion | flops 7864320 | bytes 11010064 | tf_op jit(solution)/shard_map/sub | solution.py:70
  101.6 1.9 collective-permute-start.5
  103.5 5.8 %collective-permute-start.4 = (f32[4,1,64,256]{3,2,1,0:T(8,128)S(1)}, f32[4,1,64,256]{3,2,1,0:T(8,128)S(1)}, u32[]{:S(2)}, u32[]{:S(2)}) collective-permute-start(f32[4,1,64,256]{3,2,1,0:T(8,128)S(1)} %get-tuple-element.42), channel_id=1, source_target_pairs={{8,0},{16,8},{24,16},{32,24},{40,32},{48,40},{56,48},{64,56},{72,6... | collective-permute-start | bytes 786440 | tf_op jit(solution)/shard_map/ppermute | solution.py:21
  109.3 2.1 collective-permute-done.5
  111.4 1.8 collective-permute-done.4
  113.1 2.5 multiply_subtract_fusion.2
  115.7 1.9 collective-permute-start.7
  117.6 5.9 %collective-permute-start.6 = (f32[4,1,64,256]{3,2,1,0:T(8,128)S(1)}, f32[4,1,64,256]{3,2,1,0:T(8,128)S(1)}, u32[]{:S(2)}, u32[]{:S(2)}) collective-permute-start(f32[4,1,64,256]{3,2,1,0:T(8,128)S(1)} %get-tuple-element.40), channel_id=1, source_target_pairs={{8,0},{16,8},{24,16},{32,24},{40,32},{48,40},{56,48},{64,56},{72,6... | collective-permute-start | bytes 786440 | tf_op jit(solution)/shard_map/ppermute | solution.py:21
  123.5 2.1 collective-permute-done.7
  125.6 1.8 collective-permute-done.6
  127.4 2.5 multiply_subtract_fusion.1
  129.9 1.9 collective-permute-start.9
  131.9 5.9 %collective-permute-start.8 = (f32[4,1,64,256]{3,2,1,0:T(8,128)S(1)}, f32[4,1,64,256]{3,2,1,0:T(8,128)S(1)}, u32[]{:S(2)}, u32[]{:S(2)}) collective-permute-start(f32[4,1,64,256]{3,2,1,0:T(8,128)S(1)} %get-tuple-element.38), channel_id=1, source_target_pairs={{8,0},{16,8},{24,16},{32,24},{40,32},{48,40},{56,48},{64,56},{72,6... | collective-permute-start | bytes 786440 | tf_op jit(solution)/shard_map/ppermute | solution.py:21
  137.8 2.1 collective-permute-done.9
  139.9 1.8 collective-permute-done.8
  141.7 3.8 %fusion.81 = (f32[4,8,64,256]{3,2,1,0:T(8,128)S(1)}, f32[4,8,64,256]{3,2,1,0:T(8,128)S(1)}, f32[4,8,64,256]{3,2,1,0:T(8,128)}) fusion(f32[4,3,8,64,256]{4,3,2,1,0:T(8,128)S(1)} %fusion.12, f32[4,8,64,256]{3,2,1,0:T(8,128)S(1)} %copy-done.14, f32[4,8,64,256]{3,2,1,0:T(8,128)S(1)} %multiply_subtract_fusion.1, ...), kind=kLoop, calls=%fused_computation.156 | loop fusion | flops 8912896 | bytes 17301520 | tf_op jit(solution)/shard_map/mul | solution.py:82
  145.6 1.9 collective-permute-start.11
  147.5 5.9 %collective-permute-start.10 = (f32[4,1,64,256]{3,2,1,0:T(8,128)S(1)}, f32[4,1,64,256]{3,2,1,0:T(8,128)S(1)}, u32[]{:S(2)}, u32[]{:S(2)}) collective-permute-start(f32[4,1,64,256]{3,2,1,0:T(8,128)S(1)} %get-tuple-element.36), channel_id=1, source_target_pairs={{8,0},{16,8},{24,16},{32,24},{40,32},{48,40},{56,48},{64,56},{72,6... | collective-permute-start | bytes 786440 | tf_op jit(solution)/shard_map/ppermute | solution.py:21
  154.0 1.5 collective-permute-done.11
  155.5 1.8 collective-permute-done.10
  157.3 1.9 fusion.80
  159.3 1.9 collective-permute-start.13
  161.2 6.1 %collective-permute-start.12 = (f32[4,1,64,256]{3,2,1,0:T(8,128)S(1)}, f32[4,1,64,256]{3,2,1,0:T(8,128)S(1)}, u32[]{:S(2)}, u32[]{:S(2)}) collective-permute-start(f32[4,1,64,256]{3,2,1,0:T(8,128)S(1)} %get-tuple-element.34), channel_id=1, source_target_pairs={{8,0},{16,8},{24,16},{32,24},{40,32},{48,40},{56,48},{64,56},{72,6... | collective-permute-start | bytes 786440 | tf_op jit(solution)/shard_map/ppermute | solution.py:21
  169.2 1.8 collective-permute-done.12
  171.0 2.0 fusion.79
  173.1 1.9 collective-permute-start.15
  175.0 5.9 %collective-permute-start.14 = (f32[4,1,64,256]{3,2,1,0:T(8,128)S(1)}, f32[4,1,64,256]{3,2,1,0:T(8,128)S(1)}, u32[]{:S(2)}, u32[]{:S(2)}) collective-permute-start(f32[4,1,64,256]{3,2,1,0:T(8,128)S(1)} %get-tuple-element.32), channel_id=1, source_target_pairs={{8,0},{16,8},{24,16},{32,24},{40,32},{48,40},{56,48},{64,56},{72,6... | collective-permute-start | bytes 786440 | tf_op jit(solution)/shard_map/ppermute | solution.py:21
  181.0 2.8 fusion.83
  185.5 13.6 %add_bitcast_fusion = (f32[4,1,8,64,256]{4,3,2,0,1:T(8,128)}, f32[4,8,64,256]{3,2,1,0:T(8,128)}) fusion(f32[4,8,64,256]{3,2,1,0:T(8,128)} %copy-done.3, f32[4,1,64,256]{3,2,1,0:T(8,128)} %copy-done.16, f32[4,1,64,256]{3,2,1,0:T(8,128)} %collective-permute-done.2, f32[4,8,64,256]{3,2,1,0:T(8,128)} %copy-done.4, f32[4,8,64,256]{3,2,1,0:T(8,128)S(1)} %get-tuple-element.8, ...), kind=kLoop, calls=%fused_computation.149 | loop fusion | flops 18874368 | bytes 27787344 | tf_op jit(solution)/shard_map/stack | solution.py:91
  199.2 17.0 %fusion.49 = (f32[4,1,8,64,256]{4,3,2,0,1:T(8,128)S(1)}, f32[4,1,8,64,256]{4,3,2,0,1:T(8,128)S(1)}, f32[4,8,64,256]{3,2,1,0:T(8,128)}, f32[4,8,64,256]{3,2,1,0:T(8,128)}, f32[4,8,64,256]{3,2,1,0:T(8,128)S(1)}) fusion(f32[4,8,64,256]{3,2,1,0:T(8,128)} %copy-done.3, f32[4,8,64,256]{3,2,1,0:T(8,128)} %get-tuple-element.4, f32[4,8,64,256]{3,2,1,0:T(8,128)} %copy-done.4, ...), kind=kLoop, calls=%fused_computation.101 | loop fusion | flops 19398656 | bytes 33554496 | tf_op jit(solution)/shard_map/stack | solution.py:91
  216.3 1.9 collective-permute-start.17
  218.2 5.9 %collective-permute-start.16 = (f32[4,1,64,256]{3,2,1,0:T(8,128)S(1)}, f32[4,1,64,256]{3,2,1,0:T(8,128)S(1)}, u32[]{:S(2)}, u32[]{:S(2)}) collective-permute-start(f32[4,1,64,256]{3,2,1,0:T(8,128)S(1)} %get-tuple-element.30), channel_id=1, source_target_pairs={{8,0},{16,8},{24,16},{32,24},{40,32},{48,40},{56,48},{64,56},{72,6... | collective-permute-start | bytes 786440 | tf_op jit(solution)/shard_map/ppermute | solution.py:21
  224.7 3.0 copy-done
  229.0 1.9 collective-permute-start.19
  230.9 5.8 %collective-permute-start.18 = (f32[4,3,1,64,256]{4,3,2,0,1:T(8,128)}, f32[4,3,1,64,256]{4,3,2,0,1:T(8,128)}, u32[]{:S(2)}, u32[]{:S(2)}) collective-permute-start(f32[4,3,1,64,256]{4,3,2,0,1:T(8,128)} %get-tuple-element.23), channel_id=1, source_target_pairs={{8,0},{16,8},{24,16},{32,24},{40,32},{48,40},{56,48},{64,56},{72,6... | collective-permute-start | bytes 2359304 | tf_op jit(solution)/shard_map/ppermute | solution.py:21
  236.7 2.6 fusion.39
  239.4 81.3 %all-reduce.22.cloned.1.call-done = f32[8,64,256]{2,1,0:T(8,128)} async-done(((f32[8,64,256]{2,1,0:T(8,128)}), f32[8,64,256]{2,1,0:T(8,128)}) %all-reduce.22.cloned.1.call-update) | async-done | bytes 524304 | tf_op jit(solution)/shard_map/psum | solution.py:87
  320.7 1.5 constant_dynamic-slice_fusion
  322.2 18.6 %copy_add_fusion = f32[4,3,8,64,256]{4,3,2,1,0:T(8,128)} fusion(f32[4,3,8,64,256]{4,3,2,0,1:T(8,128)} %copy-done, f32[4,3,1,64,256]{4,3,2,0,1:T(8,128)S(1)} %collective-permute-done.19, f32[4,1,8,64,256]{4,3,2,0,1:T(8,128)} %copy-done.9, f32[4,1,8,64,256]{4,3,2,0,1:T(8,128)} %copy-done.8, f32[4,1,8,64,256]{4,3,2,0,1:T(8,128)S(1)} %copy-done.7, ...), kind=kLoop, calls=%fused_computation.29 | loop fusion | flops 23592960 | bytes 26738688 | tf_op jit(solution)/shard_map/add | solution.py:49
  (84 shorter events, 8.9 us)
Async XLA Ops:
  7.2 9.3 %copy-start.24 = (f32[8,8,256]{2,1,0:T(8,128)S(1)}, f32[8,8,256]{2,1,0:T(8,128)}, u32[]{:S(2)}) copy-start(f32[8,8,256]{2,1,0:T(8,128)} %param.4) | copy-start | bytes 196612
  7.2 313.5 %all-reduce.22.cloned.1.call-start = ((), (), s32[]{:S(2)}) async-start(), calls=%async_computation | async-start | bytes 1048576 | tf_op jit(solution)/shard_map/psum | solution.py:87
  8.8 65.9 %collective-permute-start.1 = (f32[4,3,1,64,256]{4,3,2,0,1:T(8,128)S(1)}, f32[4,3,1,64,256]{4,3,2,0,1:T(8,128)S(1)}, u32[]{:S(2)}, u32[]{:S(2)}) collective-permute-start(f32[4,3,1,64,256]{4,3,2,0,1:T(8,128)S(1)} %get-tuple-element.26), channel_id=1, source_target_pairs={{0,8},{8,16},{16,24},{24,32},{32,40},{40,48},{48,56},{56,64},{64,7... | collective-permute-start | bytes 2359304 | tf_op jit(solution)/shard_map/ppermute | solution.py:18
  10.7 64.9 %collective-permute-start = (f32[4,3,1,64,256]{4,3,2,0,1:T(8,128)S(1)}, f32[4,3,1,64,256]{4,3,2,0,1:T(8,128)}, u32[]{:S(2)}, u32[]{:S(2)}) collective-permute-start(f32[4,3,1,64,256]{4,3,2,0,1:T(8,128)S(1)} %get-tuple-element.25), channel_id=1, source_target_pairs={{8,0},{16,8},{24,16},{32,24},{40,32},{48,40},{56,48},{64,56},{72,6... | collective-permute-start | bytes 2359304 | tf_op jit(solution)/shard_map/ppermute | solution.py:21
  58.9 2.7 copy-start.13
  59.7 36.9 %collective-permute-start.3 = (f32[4,1,64,256]{3,2,1,0:T(8,128)}, f32[4,1,64,256]{3,2,1,0:T(8,128)S(1)}, u32[]{:S(2)}, u32[]{:S(2)}) collective-permute-start(f32[4,1,64,256]{3,2,1,0:T(8,128)} %broadcast_in_dim.16), channel_id=1, source_target_pairs={{0,8},{8,16},{16,24},{24,32},{32,40},{40,48},{48,56},{56,64},{64,7... | collective-permute-start | bytes 786440 | tf_op jit(solution)/shard_map/ppermute | solution.py:18
  61.6 14.0 %slice-start = ((s8[6291456]{0:T(1024)(128)(4,1)}), s8[4194304]{0:T(1024)(128)(4,1)S(1)}, s32[]{:S(2)}) async-start(s8[6291456]{0:T(1024)(128)(4,1)} %bitcast.71), calls=%async_computation.1 | async-start | bytes 8388608
  62.3 12.3 %copy-start.25 = (s32[4]{0:T(128)S(1)}, s32[4]{0:T(128)}, u32[]{:S(2)}) copy-start(s32[4]{0:T(128)} %param.7) | copy-start | bytes 52
  62.3 13.2 %slice-start.1 = ((s8[6291456]{0:T(1024)(128)(4,1)}), s8[2097152]{0:T(1024)(128)(4,1)S(1)}, s32[]{:S(2)}) async-start(s8[6291456]{0:T(1024)(128)(4,1)} %bitcast.71), calls=%async_computation.2 | async-start | bytes 4194304
  62.3 34.2 %collective-permute-start.2 = (f32[4,1,64,256]{3,2,1,0:T(8,128)}, f32[4,1,64,256]{3,2,1,0:T(8,128)}, u32[]{:S(2)}, u32[]{:S(2)}) collective-permute-start(f32[4,1,64,256]{3,2,1,0:T(8,128)} %broadcast_in_dim.7), channel_id=1, source_target_pairs={{8,0},{16,8},{24,16},{32,24},{40,32},{48,40},{56,48},{64,56},{72,6... | collective-permute-start | bytes 786440 | tf_op jit(solution)/shard_map/ppermute | solution.py:21
  74.7 0.9 copy-start.21
  96.5 5.0 %copy-start.16 = (f32[4,1,64,256]{3,2,1,0:T(8,128)}, f32[4,1,64,256]{3,2,1,0:T(8,128)S(1)}, u32[]{:S(2)}) copy-start(f32[4,1,64,256]{3,2,1,0:T(8,128)S(1)} %collective-permute-done.3) | copy-start | bytes 786436
  97.9 3.6 %copy-start.3 = (f32[4,8,64,256]{3,2,1,0:T(8,128)}, f32[4,8,64,256]{3,2,1,0:T(8,128)S(1)}, u32[]{:S(2)}) copy-start(f32[4,8,64,256]{3,2,1,0:T(8,128)S(1)} %broadcast_in_dim.6) | copy-start | bytes 6291460
  101.5 14.1 %copy-start.1 = (f32[4,8,64,256]{3,2,1,0:T(8,128)}, f32[4,8,64,256]{3,2,1,0:T(8,128)S(1)}, u32[]{:S(2)}) copy-start(f32[4,8,64,256]{3,2,1,0:T(8,128)S(1)} %fusion.47) | copy-start | bytes 6291460
  101.6 9.8 %collective-permute-start.5 = (f32[4,1,64,256]{3,2,1,0:T(8,128)S(1)}, f32[4,1,64,256]{3,2,1,0:T(8,128)S(1)}, u32[]{:S(2)}, u32[]{:S(2)}) collective-permute-start(f32[4,1,64,256]{3,2,1,0:T(8,128)S(1)} %get-tuple-element.43), channel_id=1, source_target_pairs={{0,8},{8,16},{16,24},{24,32},{32,40},{40,48},{48,56},{56,64},{64,7... | collective-permute-start | bytes 786440 | tf_op jit(solution)/shard_map/ppermute | solution.py:18
  103.5 9.6 %collective-permute-start.4 = (f32[4,1,64,256]{3,2,1,0:T(8,128)S(1)}, f32[4,1,64,256]{3,2,1,0:T(8,128)S(1)}, u32[]{:S(2)}, u32[]{:S(2)}) collective-permute-start(f32[4,1,64,256]{3,2,1,0:T(8,128)S(1)} %get-tuple-element.42), channel_id=1, source_target_pairs={{8,0},{16,8},{24,16},{32,24},{40,32},{48,40},{56,48},{64,56},{72,6... | collective-permute-start | bytes 786440 | tf_op jit(solution)/shard_map/ppermute | solution.py:21
  111.4 4.2 %copy-start.17 = (f32[4,1,64,256]{3,2,1,0:T(8,128)}, f32[4,1,64,256]{3,2,1,0:T(8,128)S(1)}, u32[]{:S(2)}) copy-start(f32[4,1,64,256]{3,2,1,0:T(8,128)S(1)} %collective-permute-done.5) | copy-start | bytes 786436
  113.1 2.5 copy-start.18
  115.6 14.2 %copy-start.2 = (f32[4,8,64,256]{3,2,1,0:T(8,128)}, f32[4,8,64,256]{3,2,1,0:T(8,128)S(1)}, u32[]{:S(2)}) copy-start(f32[4,8,64,256]{3,2,1,0:T(8,128)S(1)} %multiply_subtract_fusion.2) | copy-start | bytes 6291460
  115.7 10.0 %collective-permute-start.7 = (f32[4,1,64,256]{3,2,1,0:T(8,128)S(1)}, f32[4,1,64,256]{3,2,1,0:T(8,128)S(1)}, u32[]{:S(2)}, u32[]{:S(2)}) collective-permute-start(f32[4,1,64,256]{3,2,1,0:T(8,128)S(1)} %get-tuple-element.41), channel_id=1, source_target_pairs={{0,8},{8,16},{16,24},{24,32},{32,40},{40,48},{48,56},{56,64},{64,7... | collective-permute-start | bytes 786440 | tf_op jit(solution)/shard_map/ppermute | solution.py:18
  117.6 9.8 %collective-permute-start.6 = (f32[4,1,64,256]{3,2,1,0:T(8,128)S(1)}, f32[4,1,64,256]{3,2,1,0:T(8,128)S(1)}, u32[]{:S(2)}, u32[]{:S(2)}) collective-permute-start(f32[4,1,64,256]{3,2,1,0:T(8,128)S(1)} %get-tuple-element.40), channel_id=1, source_target_pairs={{8,0},{16,8},{24,16},{32,24},{40,32},{48,40},{56,48},{64,56},{72,6... | collective-permute-start | bytes 786440 | tf_op jit(solution)/shard_map/ppermute | solution.py:21
  125.6 4.2 %copy-start.19 = (f32[4,1,64,256]{3,2,1,0:T(8,128)}, f32[4,1,64,256]{3,2,1,0:T(8,128)S(1)}, u32[]{:S(2)}) copy-start(f32[4,1,64,256]{3,2,1,0:T(8,128)S(1)} %collective-permute-done.7) | copy-start | bytes 786436
  127.4 2.5 copy-start.20
  127.4 14.3 %copy-start.14 = (f32[4,8,64,256]{3,2,1,0:T(8,128)S(1)}, f32[4,8,64,256]{3,2,1,0:T(8,128)}, u32[]{:S(2)}) copy-start(f32[4,8,64,256]{3,2,1,0:T(8,128)} %param.6) | copy-start | bytes 6291460
  129.9 10.0 %collective-permute-start.9 = (f32[4,1,64,256]{3,2,1,0:T(8,128)S(1)}, f32[4,1,64,256]{3,2,1,0:T(8,128)S(1)}, u32[]{:S(2)}, u32[]{:S(2)}) collective-permute-start(f32[4,1,64,256]{3,2,1,0:T(8,128)S(1)} %get-tuple-element.39), channel_id=1, source_target_pairs={{0,8},{8,16},{16,24},{24,32},{32,40},{40,48},{48,56},{56,64},{64,7... | collective-permute-start | bytes 786440 | tf_op jit(solution)/shard_map/ppermute | solution.py:18
  131.9 9.8 %collective-permute-start.8 = (f32[4,1,64,256]{3,2,1,0:T(8,128)S(1)}, f32[4,1,64,256]{3,2,1,0:T(8,128)S(1)}, u32[]{:S(2)}, u32[]{:S(2)}) collective-permute-start(f32[4,1,64,256]{3,2,1,0:T(8,128)S(1)} %get-tuple-element.38), channel_id=1, source_target_pairs={{8,0},{16,8},{24,16},{32,24},{40,32},{48,40},{56,48},{64,56},{72,6... | collective-permute-start | bytes 786440 | tf_op jit(solution)/shard_map/ppermute | solution.py:21
  141.7 3.9 %copy-start.15 = (f32[4,1,64,256]{3,2,1,0:T(8,128)}, f32[4,1,64,256]{3,2,1,0:T(8,128)S(1)}, u32[]{:S(2)}) copy-start(f32[4,1,64,256]{3,2,1,0:T(8,128)S(1)} %collective-permute-done.8) | copy-start | bytes 786436
  145.6 10.0 %collective-permute-start.11 = (f32[4,1,64,256]{3,2,1,0:T(8,128)S(1)}, f32[4,1,64,256]{3,2,1,0:T(8,128)S(1)}, u32[]{:S(2)}, u32[]{:S(2)}) collective-permute-start(f32[4,1,64,256]{3,2,1,0:T(8,128)S(1)} %get-tuple-element.37), channel_id=1, source_target_pairs={{0,8},{8,16},{16,24},{24,32},{32,40},{40,48},{48,56},{56,64},{64,7... | collective-permute-start | bytes 786440 | tf_op jit(solution)/shard_map/ppermute | solution.py:18
  147.5 9.8 %collective-permute-start.10 = (f32[4,1,64,256]{3,2,1,0:T(8,128)S(1)}, f32[4,1,64,256]{3,2,1,0:T(8,128)S(1)}, u32[]{:S(2)}, u32[]{:S(2)}) collective-permute-start(f32[4,1,64,256]{3,2,1,0:T(8,128)S(1)} %get-tuple-element.36), channel_id=1, source_target_pairs={{8,0},{16,8},{24,16},{32,24},{40,32},{48,40},{56,48},{64,56},{72,6... | collective-permute-start | bytes 786440 | tf_op jit(solution)/shard_map/ppermute | solution.py:21
  159.3 10.0 %collective-permute-start.13 = (f32[4,1,64,256]{3,2,1,0:T(8,128)S(1)}, f32[4,1,64,256]{3,2,1,0:T(8,128)S(1)}, u32[]{:S(2)}, u32[]{:S(2)}) collective-permute-start(f32[4,1,64,256]{3,2,1,0:T(8,128)S(1)} %get-tuple-element.35), channel_id=1, source_target_pairs={{0,8},{8,16},{16,24},{24,32},{32,40},{40,48},{48,56},{56,64},{64,7... | collective-permute-start | bytes 786440 | tf_op jit(solution)/shard_map/ppermute | solution.py:18
  161.2 9.8 %collective-permute-start.12 = (f32[4,1,64,256]{3,2,1,0:T(8,128)S(1)}, f32[4,1,64,256]{3,2,1,0:T(8,128)S(1)}, u32[]{:S(2)}, u32[]{:S(2)}) collective-permute-start(f32[4,1,64,256]{3,2,1,0:T(8,128)S(1)} %get-tuple-element.34), channel_id=1, source_target_pairs={{8,0},{16,8},{24,16},{32,24},{40,32},{48,40},{56,48},{64,56},{72,6... | collective-permute-start | bytes 786440 | tf_op jit(solution)/shard_map/ppermute | solution.py:21
  173.0 10.7 %copy-start.4 = (f32[4,8,64,256]{3,2,1,0:T(8,128)}, f32[4,8,64,256]{3,2,1,0:T(8,128)S(1)}, u32[]{:S(2)}) copy-start(f32[4,8,64,256]{3,2,1,0:T(8,128)S(1)} %get-tuple-element.6) | copy-start | bytes 6291460
  173.1 10.7 %copy-start.10 = (f32[4,8,64,256]{3,2,1,0:T(8,128)}, f32[4,8,64,256]{3,2,1,0:T(8,128)S(1)}, u32[]{:S(2)}) copy-start(f32[4,8,64,256]{3,2,1,0:T(8,128)S(1)} %get-tuple-element.5) | copy-start | bytes 6291460
  173.1 10.7 %collective-permute-start.15 = (f32[4,1,64,256]{3,2,1,0:T(8,128)S(1)}, f32[4,1,64,256]{3,2,1,0:T(8,128)S(1)}, u32[]{:S(2)}, u32[]{:S(2)}) collective-permute-start(f32[4,1,64,256]{3,2,1,0:T(8,128)S(1)} %get-tuple-element.33), channel_id=1, source_target_pairs={{0,8},{8,16},{16,24},{24,32},{32,40},{40,48},{48,56},{56,64},{64,7... | collective-permute-start | bytes 786440 | tf_op jit(solution)/shard_map/ppermute | solution.py:18
  175.0 9.8 %collective-permute-start.14 = (f32[4,1,64,256]{3,2,1,0:T(8,128)S(1)}, f32[4,1,64,256]{3,2,1,0:T(8,128)S(1)}, u32[]{:S(2)}, u32[]{:S(2)}) collective-permute-start(f32[4,1,64,256]{3,2,1,0:T(8,128)S(1)} %get-tuple-element.32), channel_id=1, source_target_pairs={{8,0},{16,8},{24,16},{32,24},{40,32},{48,40},{56,48},{64,56},{72,6... | collective-permute-start | bytes 786440 | tf_op jit(solution)/shard_map/ppermute | solution.py:21
  183.8 0.7 copy-start.22
  199.2 25.0 %copy-start.6 = (f32[4,1,8,64,256]{4,3,2,0,1:T(8,128)S(1)}, f32[4,1,8,64,256]{4,3,2,0,1:T(8,128)}, u32[]{:S(2)}) copy-start(f32[4,1,8,64,256]{4,3,2,0,1:T(8,128)} %get-tuple-element.3) | copy-start | bytes 6291460
  216.2 8.4 %copy-start.8 = (f32[4,1,8,64,256]{4,3,2,0,1:T(8,128)}, f32[4,1,8,64,256]{4,3,2,0,1:T(8,128)S(1)}, u32[]{:S(2)}) copy-start(f32[4,1,8,64,256]{4,3,2,0,1:T(8,128)S(1)} %get-tuple-element.12) | copy-start | bytes 6291460
  216.2 8.4 %copy-start.9 = (f32[4,1,8,64,256]{4,3,2,0,1:T(8,128)}, f32[4,1,8,64,256]{4,3,2,0,1:T(8,128)S(1)}, u32[]{:S(2)}) copy-start(f32[4,1,8,64,256]{4,3,2,0,1:T(8,128)S(1)} %get-tuple-element.13) | copy-start | bytes 6291460
  216.3 20.4 %collective-permute-start.17 = (f32[4,1,64,256]{3,2,1,0:T(8,128)S(1)}, f32[4,1,64,256]{3,2,1,0:T(8,128)S(1)}, u32[]{:S(2)}, u32[]{:S(2)}) collective-permute-start(f32[4,1,64,256]{3,2,1,0:T(8,128)S(1)} %get-tuple-element.31), channel_id=1, source_target_pairs={{0,8},{8,16},{16,24},{24,32},{32,40},{40,48},{48,56},{56,64},{64,7... | collective-permute-start | bytes 786440 | tf_op jit(solution)/shard_map/ppermute | solution.py:18
  218.2 18.4 %collective-permute-start.16 = (f32[4,1,64,256]{3,2,1,0:T(8,128)S(1)}, f32[4,1,64,256]{3,2,1,0:T(8,128)S(1)}, u32[]{:S(2)}, u32[]{:S(2)}) collective-permute-start(f32[4,1,64,256]{3,2,1,0:T(8,128)S(1)} %get-tuple-element.30), channel_id=1, source_target_pairs={{8,0},{16,8},{24,16},{32,24},{40,32},{48,40},{56,48},{64,56},{72,6... | collective-permute-start | bytes 786440 | tf_op jit(solution)/shard_map/ppermute | solution.py:21
  224.2 12.5 %copy-start.11 = (f32[4,8,64,256]{3,2,1,0:T(8,128)S(1)}, f32[4,8,64,256]{3,2,1,0:T(8,128)}, u32[]{:S(2)}) copy-start(f32[4,8,64,256]{3,2,1,0:T(8,128)} %get-tuple-element.27) | copy-start | bytes 6291460
  224.2 12.5 %copy-start.12 = (f32[4,8,64,256]{3,2,1,0:T(8,128)S(1)}, f32[4,8,64,256]{3,2,1,0:T(8,128)}, u32[]{:S(2)}) copy-start(f32[4,8,64,256]{3,2,1,0:T(8,128)} %get-tuple-element.28) | copy-start | bytes 6291460
  224.7 3.0 copy-start
  227.7 9.0 %copy-start.5 = (f32[4,8,64,256]{3,2,1,0:T(8,128)S(1)}, f32[4,8,64,256]{3,2,1,0:T(8,128)}, u32[]{:S(2)}) copy-start(f32[4,8,64,256]{3,2,1,0:T(8,128)} %get-tuple-element.4) | copy-start | bytes 6291460
  229.0 93.2 %collective-permute-start.19 = (f32[4,3,1,64,256]{4,3,2,0,1:T(8,128)}, f32[4,3,1,64,256]{4,3,2,0,1:T(8,128)S(1)}, u32[]{:S(2)}, u32[]{:S(2)}) collective-permute-start(f32[4,3,1,64,256]{4,3,2,0,1:T(8,128)} %get-tuple-element.24), channel_id=1, source_target_pairs={{0,8},{8,16},{16,24},{24,32},{32,40},{40,48},{48,56},{56,64},{64,7... | collective-permute-start | bytes 2359304 | tf_op jit(solution)/shard_map/ppermute | solution.py:18
  230.9 91.2 %collective-permute-start.18 = (f32[4,3,1,64,256]{4,3,2,0,1:T(8,128)}, f32[4,3,1,64,256]{4,3,2,0,1:T(8,128)}, u32[]{:S(2)}, u32[]{:S(2)}) collective-permute-start(f32[4,3,1,64,256]{4,3,2,0,1:T(8,128)} %get-tuple-element.23), channel_id=1, source_target_pairs={{8,0},{16,8},{24,16},{32,24},{40,32},{48,40},{56,48},{64,56},{72,6... | collective-permute-start | bytes 2359304 | tf_op jit(solution)/shard_map/ppermute | solution.py:21
  236.7 85.4 %copy-start.7 = (f32[4,1,8,64,256]{4,3,2,0,1:T(8,128)S(1)}, f32[4,1,8,64,256]{4,3,2,0,1:T(8,128)}, u32[]{:S(2)}) copy-start(f32[4,1,8,64,256]{4,3,2,0,1:T(8,128)} %get-tuple-element.3) | copy-start | bytes 6291460
  (1 other events, 0.7 us)
Sparse Core Ops, SparseCore 0:
  239.5 81.1 all-reduce.21
where the time goes:
time: 352 us; the launch traced here: 348 us
  waiting for transfers between devices  99.6 us (28%)
  other arithmetic  93.6 us (27%)
  starting transfers between devices  78.2 us (22%)
  blocking collectives  42.4 us (12%)
  local copies, waits for them, and re-layouts  19.2 us (5%)
  between operations  14.7 us (4%)
    psum x1, waiting for transfers between devices, shards(): total = lax.psum(local_sum, 'subj')  81.3 us
    ppermute x10, starting transfers between devices, with_halo(): lax.ppermute(lax.slice_in_dim(block, 0, width, axis=dim), axis, backward)  59 us
    all_gather x1, blocking collectives, shards(): whole_tmpl = lax.all_gather(template, 'subj', axis=1, tiled=True)  42.4 us
    add x2, other arithmetic, rim_kernel(): return center + smoothing * (nsum - 6.0 * center)  39.5 us
    another operation x3, other arithmetic, shards(): velocity_grad = jnp.stack([grad_z, grad_y, grad_x], axis=1)  31.1 us
    ppermute x10, starting transfers between devices, with_halo(): lax.ppermute(lax.slice_in_dim(block, block.shape[dim] - width, None, axis...  19.2 us
    unnamed x57, local copies, waits for them, and re-layouts  11.7 us
    ppermute x10, waiting for transfers between devices, with_halo(): lax.ppermute(lax.slice_in_dim(block, block.shape[dim] - width, None, axis...  9.15 us
  transfers between devices with their start and end apart: 21, of which 12 were waited for; matrix products, arithmetic and copies ran while one was open for 11% of the time, Pallas kernels for 0%

commit v1 on v0

v1 whole, which is shorter than its diff:
```python
import jax
import jax.numpy as jnp
from jax import lax
from jax.experimental import pallas as pl
from jax.experimental.pallas import tpu as pltpu
from jax.sharding import PartitionSpec as P

time_step = 0.15
smoothing = 0.1
half = 0.5 * time_step
centre = 1.0 - 6.0 * smoothing
f32 = jnp.float32


def load(ref, *at):
    at = at + (slice(None),)
    rows = ref.shape[-2] // 8
    return tuple(ref[at + (pl.ds(128 * h, 128),)].reshape(rows, 8, 128) for h in (0, 1))


def store(ref, plane, *at):
    at = at + (slice(None),)
    for h in (0, 1):
        ref[at + (pl.ds(128 * h, 128),)] = plane[h].reshape(-1, 128)


def load_t(ref, p):
    return tuple(ref[:, p, :, pl.ds(128 * h, 128)] for h in (0, 1))


def each(fn, *planes):
    return tuple(fn(*x) for x in zip(*planes))


def add(*planes):
    total = planes[0]
    for plane in planes[1:]:
        total = each(lambda a, b: a + b, total, plane)
    return total


def sub(a, b):
    return each(lambda x, y: x - y, a, b)


def mul(a, b):
    return each(lambda x, y: x * y, a, b)


def scale(a, factor):
    return each(lambda x: x * factor, a)


def y_sides(x):
    row = lax.broadcasted_iota(jnp.int32, (1, 8, 128), 1)
    down, up = pltpu.roll(x, 1, axis=1), pltpu.roll(x, 7, axis=1)
    none = jnp.zeros((1, 8, 128), f32)
    before = jnp.where(row == 0, jnp.concatenate([none, down[:-1]], axis=0), down)
    after = jnp.where(row == 7, jnp.concatenate([up[1:], none], axis=0), up)
    return before, after


def x_sides(plane):
    lane = lax.broadcasted_iota(jnp.int32, (1, 8, 128), 2)
    right = each(lambda x: pltpu.roll(x, 1, axis=2), plane)
    left = each(lambda x: pltpu.roll(x, 127, axis=2), plane)
    before = (jnp.where(lane == 0, 0.0, right[0]), jnp.where(lane == 0, right[0], right[1]))
    after = (jnp.where(lane == 127, left[1], left[0]), jnp.where(lane == 127, 0.0, left[1]))
    return before, after


def dy(plane):
    def one(x):
        before, after = y_sides(x)
        return after - before

    return each(one, plane)


def dx(plane):
    before, after = x_sides(plane)
    return sub(after, before)


def smooth(mid, inner, outer, a, b):
    def ysum(x):
        before, after = y_sides(x)
        return after + before

    before, after = x_sides(mid)
    total = add(inner, outer, each(ysum, mid), add(before, after))
    return each(lambda m, t: a * m + b * t, mid, total)


def dz(inner, outer, toward):
    return sub(inner, outer) if toward > 0 else sub(outer, inner)


def forward(mid, inner, outer, w, toward=1):
    change = add(mul(w[0], dz(inner, outer, toward)), mul(w[1], dy(mid)), mul(w[2], dx(mid)))
    return sub(mid, change)


def backward(mid, flux_inner, flux_outer, wy, wx, toward=1, active=None):
    change = add(dz(flux_inner, flux_outer, toward), dy(mul(wy, mid)), dx(mul(wx, mid)))
    return add(mid, change if active is None else scale(change, active))


def grads(adj, mid, inner, outer, toward=1):
    return [mul(adj, dz(inner, outer, toward)), mul(adj, dy(mid)), mul(adj, dx(mid))]


def natural(odd, j):
    return j + odd * (7 - 2 * j)


ROLES = (0, 1)
TOWARD = (1, -1)


def t_side(odd, role):
    if role == 0:
        return odd, 1 - odd, 2 + 7 * odd, 2 + odd * 5 + 1
    return 11 - odd, 10 + odd, 9 - 7 * odd, 8 - 5 * odd


def inner_1(info, m, t, w_in, i1_in, i2_in):
    s = pl.program_id(0)
    odd = info[4]
    sign = (1 - 2 * odd).astype(f32)

    def first(j, _):
        w = []
        for c in range(3):
            turn = sign if c == 0 else 1.0
            v = smooth(
                load(m, 0, c, natural(odd, j)),
                load(m, 0, c, natural(odd, j + 1)),
                load(m, 0, c, natural(odd, j - 1)),
                half * centre * turn,
                half * smoothing * turn,
            )
            store(w_in, v, 0, c, j - 1)
            w.append(v)
        at = lambda i: load_t(t, 2 + natural(odd, i))
        store(i1_in, forward(at(j), at(j + 1), at(j - 1), w), 0, j - 1)
        return 0

    lax.fori_loop(1, 7, first, 0)
    active = info[s] > 1

    @pl.when(active)
    def _():
        def second(j, _):
            at = lambda i: load(i1_in, 0, i - 1)
            w = [load(w_in, 0, c, j - 1) for c in range(3)]
            store(i2_in, forward(at(j), at(j + 1), at(j - 1), w), 0, j - 2)
            return 0

        lax.fori_loop(2, 6, second, 0)

    @pl.when(jnp.logical_not(active))
    def _():
        i2_in[...] = i1_in[:, 1:5]


def outer_1(info, *refs):
    ms, mr, t, wp, i1p = refs[0:2], refs[2:4], refs[4], refs[5:7], refs[7:9]
    w_out, i1_out, send = refs[9:11], refs[11:13], refs[13:15]
    s = pl.program_id(0)
    odd = info[4]
    sign = (1 - 2 * odd).astype(f32)
    for r in ROLES:
        to = TOWARD[r]
        p0 = odd if r == 0 else 1 - odd
        p1 = 1 - p0
        h1, h2 = p1, p0
        near = r * 1
        far = 1 - near
        inside = info[5].astype(f32) if r == 0 else 1.0
        ws = [[], []]
        for c in range(3):
            turn = sign if c == 0 else 1.0
            m_h1, m_p0 = load(mr[r], 0, c, h1), load(ms[r], 0, c, p0)
            a, b = half * centre * turn, half * smoothing * turn
            wh = smooth(m_h1, m_p0, load(mr[r], 0, c, h2), a * inside, b * inside)
            w0 = smooth(m_p0, load(ms[r], 0, c, p1), m_h1, a, b)
            store(w_out[r], wh, 0, c, 0)
            store(w_out[r], w0, 0, c, 1)
            ws[0].append(wh)
            ws[1].append(w0)
        th2, th1, tp0, tp1 = (load_t(t, at) for at in t_side(odd, r))
        i_h1 = forward(th1, tp0, th2, ws[0], to)
        i_p0 = forward(tp0, tp1, th1, ws[1], to)
        store(i1_out[r], i_h1, 0, 0)
        store(i1_out[r], i_p0, 0, 1)

        @pl.when(info[s] > 1)
        def _():
            i_p1, i_p2 = load(i1p[r], 0, near), load(i1p[r], 0, far)
            i_h1, i_p0 = load(i1_out[r], 0, 0), load(i1_out[r], 0, 1)
            w0 = [load(w_out[r], 0, c, 1) for c in range(3)]
            w1 = [load(wp[r], 0, c, near) for c in range(3)]
            store(send[r], forward(i_p0, i_p1, i_h1, w0, to), 0, 0)
            store(send[r], forward(i_p1, i_p2, i_p0, w1, to), 0, 1)

        @pl.when(info[s] <= 1)
        def _():
            store(send[r], load(i1_out[r], 0, 1), 0, 0)
            store(send[r], load(i1p[r], 0, near), 0, 1)


def gather_planes(x, sides, inner):
    x[0] = sides[0][0, 0]
    x[1] = sides[0][0, 1]
    x[7] = sides[1][0, 0]
    x[6] = sides[1][0, 1]
    x[2:6] = inner[0]


def inner_2(info, w_in, i2_in, s1z, s1c, targets, i3_in, a4_in, i4_in, x):
    s = pl.program_id(0)
    odd = info[4]
    gather_planes(x, (s1z, s1c), i2_in)

    @pl.when(info[s] > 2)
    def _():
        def step(j, _):
            w = [load(w_in, 0, c, j - 1) for c in range(3)]
            store(i3_in, forward(load(x, j), load(x, j + 1), load(x, j - 1), w), 0, j - 1)
            return 0

        lax.fori_loop(1, 7, step, 0)

    @pl.when(info[s] <= 2)
    def _():
        i3_in[0] = x[1:7]

    @pl.when(info[s] > 3)
    def _():
        def step(j, _):
            at = lambda i: load(i3_in, 0, i - 1)
            w = [load(w_in, 0, c, j - 1) for c in range(3)]
            image = forward(at(j), at(j + 1), at(j - 1), w)
            store(i4_in, image, 0, j - 2)
            store(a4_in, sub(image, load(targets, 0, natural(odd, j))), 0, j - 2)
            return 0

        lax.fori_loop(2, 6, step, 0)

    @pl.when(info[s] <= 3)
    def _():
        def step(j, _):
            image = load(i3_in, 0, j - 1)
            store(i4_in, image, 0, j - 2)
            store(a4_in, sub(image, load(targets, 0, natural(odd, j))), 0, j - 2)
            return 0

        lax.fori_loop(2, 6, step, 0)


def outer_2(info, *refs):
    r1, wb, wp, s1, i2p, i3p, tg = (refs[2 * i : 2 * i + 2] for i in range(7))
    i3_out, i4_out, a4_out, send = (refs[14 + 2 * i : 16 + 2 * i] for i in range(4))
    s = pl.program_id(0)
    odd = info[4]
    for r in ROLES:
        to, near, far = TOWARD[r], r, 1 - r
        p0 = odd if r == 0 else 1 - odd

        @pl.when(info[s] > 2)
        def _():
            i_h1, i_h2 = load(r1[r], 0, 0), load(r1[r], 0, 1)
            i_p0, i_p1 = load(s1[r], 0, 0), load(s1[r], 0, 1)
            wh = [load(wb[r], 0, c, 0) for c in range(3)]
            w0 = [load(wb[r], 0, c, 1) for c in range(3)]
            store(i3_out[r], forward(i_h1, i_p0, i_h2, wh, to), 0, 0)
            store(i3_out[r], forward(i_p0, i_p1, i_h1, w0, to), 0, 1)

        @pl.when(info[s] <= 2)
        def _():
            i3_out[r][0, 0] = r1[r][0, 0]
            i3_out[r][0, 1] = s1[r][0, 0]

        @pl.when(info[s] > 3)
        def _():
            i_h1, i_p0 = load(i3_out[r], 0, 0), load(i3_out[r], 0, 1)
            i_p1, i_p2 = load(i3p[r], 0, near), load(i3p[r], 0, far)
            w0 = [load(wb[r], 0, c, 1) for c in range(3)]
            w1 = [load(wp[r], 0, c, near) for c in range(3)]
            store(i4_out[r], forward(i_p0, i_p1, i_h1, w0, to), 0, 0)
            store(i4_out[r], forward(i_p1, i_p2, i_p0, w1, to), 0, 1)

        @pl.when(info[s] <= 3)
        def _():
            i4_out[r][0, 0] = i3_out[r][0, 1]
            i4_out[r][0, 1] = i3p[r][0, near]

        store(send[r], sub(load(i4_out[r], 0, 0), load(tg[r], 0, p0)), 0, 0)
        a_p1 = sub(load(i4_out[r], 0, 1), load(tg[r], 0, 1 - p0))
        store(a4_out[r], a_p1, 0, 0)
        store(send[r], mul(load(wp[r], 0, 0, near), a_p1), 0, 1)


def inner_3(info, *refs):
    w_in, wbz, wbc, s2z, s2c, a4z, a4c, a4_in, i3_in, i3z, i3c, i2_in, s1z, s1c, i1_in, i4_in, i4z, i4c = refs[:18]
    a3_in, a2_in, g_in, warped, a, f, x = refs[18:]
    s = pl.program_id(0)
    odd = info[4]
    a[0], a[7] = s2z[0, 0], s2c[0, 0]
    a[1], a[6] = a4z[0, 0], a4c[0, 0]
    a[2:6] = a4_in[0]
    for r, side in ((0, i4z), (1, i4c)):
        p0, p1 = (0, 1) if r == 0 else (7, 6)
        warped[0, natural(odd, p0)] = side[0, 0]
        warped[0, natural(odd, p1)] = side[0, 1]

    def copy(j, _):
        warped[0, natural(odd, j)] = i4_in[0, j - 2]
        return 0

    lax.fori_loop(2, 6, copy, 0)

    @pl.when(info[s] > 3)
    def _():
        x[0], x[7] = i3z[0, 0], i3c[0, 0]
        x[1:7] = i3_in[0]
        f[0] = wbz[0, 0, 0] * a[0]
        f[7] = wbc[0, 0, 0] * a[7]
        f[1:7] = w_in[0, 0] * a[1:7]

        def step(j, _):
            mid = load(a, j)
            wy, wx = (load(w_in, 0, c, j - 1) for c in (1, 2))
            store(a3_in, backward(mid, load(f, j + 1), load(f, j - 1), wy, wx), 0, j - 1)
            for c, g in enumerate(grads(mid, load(x, j), load(x, j + 1), load(x, j - 1))):
                store(g_in, g, 0, c, j - 1)
            return 0

        lax.fori_loop(1, 7, step, 0)

    @pl.when(info[s] <= 3)
    def _():
        a3_in[0] = a[1:7]
        g_in[...] = jnp.zeros(g_in.shape, f32)

    @pl.when(info[s] > 2)
    def _():
        gather_planes(x, (s1z, s1c), i2_in)
        f[1:7] = w_in[0, 0] * a3_in[0]

        def gradient(j):
            adj = load(a3_in, 0, j - 1)
            for c, g in enumerate(grads(adj, load(x, j), load(x, j + 1), load(x, j - 1))):
                store(g_in, add(load(g_in, 0, c, j - 1), g), 0, c, j - 1)
            return adj

        gradient(1)
        gradient(6)

        def step(j, _):
            mid = gradient(j)
            wy, wx = (load(w_in, 0, c, j - 1) for c in (1, 2))
            store(a2_in, backward(mid, load(f, j + 1), load(f, j - 1), wy, wx), 0, j - 2)
            return 0

        lax.fori_loop(2, 6, step, 0)

    @pl.when(info[s] <= 2)
    def _():
        a2_in[0] = a3_in[0, 1:5]

    @pl.when(info[s] > 1)
    def _():
        def step(j, _):
            at = lambda i: load(i1_in, 0, i - 1)
            for c, g in enumerate(grads(load(a2_in, 0, j - 2), at(j), at(j + 1), at(j - 1))):
                store(g_in, add(load(g_in, 0, c, j - 1), g), 0, c, j - 1)
            return 0

        lax.fori_loop(2, 6, step, 0)


def outer_3(info, *refs):
    r2, wb, wp, s2, a3p, i3b, i3p, r1, s1, i1b, i1p = (refs[2 * i : 2 * i + 2] for i in range(11))
    a2_out, g_out, send, a3 = (refs[22 + 2 * i : 24 + 2 * i] for i in range(4))
    s = pl.program_id(0)
    for r in ROLES:
        to, near, far = TOWARD[r], r, 1 - r
        g = g_out[r]

        @pl.when(info[s] > 3)
        def _():
            a_h1, a_p0 = load(r2[r], 0, 0), load(s2[r], 0, 0)
            f_h2, f_p1 = scale(load(r2[r], 0, 1), -1.0), load(s2[r], 0, 1)
            wh = [load(wb[r], 0, c, 0) for c in range(3)]
            w0 = [load(wb[r], 0, c, 1) for c in range(3)]
            store(a3[r], backward(a_h1, mul(w0[0], a_p0), f_h2, wh[1], wh[2], to), 0)
            store(a3[r], backward(a_p0, f_p1, mul(wh[0], a_h1), w0[1], w0[2], to), 1)
            i_h1, i_p0, i_p1 = load(i3b[r], 0, 0), load(i3b[r], 0, 1), load(i3p[r], 0, near)
            store(g, mul(a_h1, dy(i_h1)), 0, 1, 0)
            store(g, mul(a_h1, dx(i_h1)), 0, 2, 0)
            for c, value in enumerate(grads(a_p0, i_p0, i_p1, i_h1, to)):
                store(g, value, 0, c, 1)

        @pl.when(info[s] <= 3)
        def _():
            a3[r][0] = r2[r][0, 0]
            a3[r][1] = s2[r][0, 0]
            g[...] = jnp.zeros(g.shape, f32)

        @pl.when(info[s] > 2)
        def _():
            a_h1, a_p0 = load(a3[r], 0), load(a3[r], 1)
            a_p1, a_p2 = load(a3p[r], 0, near), load(a3p[r], 0, far)
            wh0 = load(wb[r], 0, 0, 0)
            w0 = [load(wb[r], 0, c, 1) for c in range(3)]
            w1 = [load(wp[r], 0, c, near) for c in range(3)]
            store(a2_out[r], backward(a_p0, mul(w1[0], a_p1), mul(wh0, a_h1), w0[1], w0[2], to), 0, 0)
            f_p2 = mul(load(wp[r], 0, 0, far), a_p2)
            store(a2_out[r], backward(a_p1, f_p2, mul(w0[0], a_p0), w1[1], w1[2], to), 0, 1)
            i_h1, i_p0, i_p1 = load(r1[r], 0, 0), load(s1[r], 0, 0), load(s1[r], 0, 1)
            store(g, add(load(g, 0, 1, 0), mul(a_h1, dy(i_h1))), 0, 1, 0)
            store(g, add(load(g, 0, 2, 0), mul(a_h1, dx(i_h1))), 0, 2, 0)
            for c, value in enumerate(grads(a_p0, i_p0, i_p1, i_h1, to)):
                store(g, add(load(g, 0, c, 1), value), 0, c, 1)

        @pl.when(info[s] <= 2)
        def _():
            a2_out[r][0, 0] = a3[r][1]
            a2_out[r][0, 1] = a3p[r][0, near]

        @pl.when(info[s] > 1)
        def _():
            i_h1, i_p0 = load(i1b[r], 0, 0), load(i1b[r], 0, 1)
            i_p1, i_p2 = load(i1p[r], 0, near), load(i1p[r], 0, far)
            for c, value in enumerate(grads(load(a2_out[r], 0, 0), i_p0, i_p1, i_h1, to)):
                store(g, add(load(g, 0, c, 1), value), 0, c, 1)
            for c, value in enumerate(grads(load(a2_out[r], 0, 1), i_p1, i_p2, i_p0, to)):
                store(g, value, 0, c, 2)

        @pl.when(info[s] <= 1)
        def _():
            g[0, :, 2] = jnp.zeros(g.shape[1:2] + g.shape[3:], f32)

        send[r][0, 0] = a2_out[r][0, 0]
        send[r][0, 1] = wp[r][0, 0, near] * a2_out[r][0, 1]
        send[r][0, 2] = g[0, 0, 1]


def final(mid, inner, outer, turn):
    return smooth(mid, inner, outer, -half * centre * turn, -half * smoothing * turn)


def inner_4(info, *refs):
    w_in, wbz, wbc, a2_in, a2z, a2c, t, g_in, gz, gc = refs[:10]
    a1_in, g_full, total, mg, a, f = refs[10:]
    s = pl.program_id(0)
    odd = info[4]
    sign = (1 - 2 * odd).astype(f32)
    gather_planes(a, (a2z, a2c), a2_in)
    f[0] = wbz[0, 0, 0] * a[0]
    f[7] = wbc[0, 0, 0] * a[7]
    f[1:7] = w_in[0, 0] * a[1:7]
    @pl.when(s == 0)
    def _():
        total[...] = jnp.zeros(total.shape, f32)

    def gradient(j, adj):
        at = lambda i: load_t(t, 2 + natural(odd, i))
        for c, g in enumerate(grads(adj, at(j), at(j + 1), at(j - 1))):
            store(g_full, add(load(g_in, 0, c, j - 1), g), 0, c, j - 1)

    @pl.when(info[s] > 1)
    def _():
        def step(j, _):
            mid = load(a, j)
            wy, wx = (load(w_in, 0, c, j - 1) for c in (1, 2))
            adj = backward(mid, load(f, j + 1), load(f, j - 1), wy, wx)
            store(a1_in, adj, 0, j - 1)
            gradient(j, adj)
            return 0

        lax.fori_loop(1, 7, step, 0)

    @pl.when(info[s] <= 1)
    def _():
        def step(j, _):
            adj = load(a, j)
            store(a1_in, adj, 0, j - 1)
            gradient(j, adj)
            return 0

        lax.fori_loop(1, 7, step, 0)

    g_full[0, :, 0] += gz[0, :, 0]
    g_full[0, :, 5] += gc[0, :, 0]
    f[1:7] = w_in[0, 0] * a1_in[0]

    def last(j, _):
        mid = load(a1_in, 0, j - 1)
        wy, wx = (load(w_in, 0, c, j - 1) for c in (1, 2))
        adj = backward(mid, load(f, j + 1), load(f, j - 1), wy, wx)
        for h in (0, 1):
            total[:, j - 2, :, pl.ds(128 * h, 128)] += adj[h]
        for c in range(3):
            at = lambda i: load(g_full, 0, c, i - 1)
            store(mg, final(at(j), at(j + 1), at(j - 1), sign if c == 0 else 1.0), 0, c, natural(odd, j))
        return 0

    lax.fori_loop(2, 6, last, 0)


def outer_4(info, *refs):
    r3, wb, wp, s3, a1p, gb, gp, i1b = (refs[2 * i : 2 * i + 2] for i in range(8))
    t, total_in, mg_in = refs[16:19]
    total, mg, made, sems = refs[19:]
    s = pl.program_id(0)
    odd = info[4]
    sign = (1 - 2 * odd).astype(f32)
    slot = lax.rem(s, 2)

    def copies(which, at):
        z_first, c_first = 6 * odd, 6 - 6 * odd
        return [
            pltpu.make_async_copy(made.at[which, r], mg.at[at, :, pl.ds(first, 2)], sems.at[which, r])
            for r, first in ((0, z_first), (1, c_first))
        ]

    @pl.when(s == 0)
    def _():
        total[...] = jnp.zeros(total.shape, f32)

        def copy(j, _):
            total[:, natural(odd, j)] = total_in[:, j - 2]
            return 0

        lax.fori_loop(2, 6, copy, 0)

    @pl.when(s >= 2)
    def _():
        for copy in copies(slot, s - 2):
            copy.wait()

    for r in ROLES:
        to, near, far = TOWARD[r], r, 1 - r
        p0 = odd if r == 0 else 1 - odd
        n0, n1 = (natural(odd, 0), natural(odd, 1)) if r == 0 else (natural(odd, 7), natural(odd, 6))
        inside = info[5].astype(f32) if r == 0 else 1.0
        a_h1, a_p0 = load(r3[r], 0, 0), load(s3[r], 0, 0)
        f_h2, f_p1 = scale(load(r3[r], 0, 1), -1.0), load(s3[r], 0, 1)
        wh = [load(wb[r], 0, c, 0) for c in range(3)]
        w0 = [load(wb[r], 0, c, 1) for c in range(3)]
        w1 = [load(wp[r], 0, c, near) for c in range(3)]
        step_one = (info[s] > 1).astype(f32)
        b_h1 = backward(a_h1, mul(w0[0], a_p0), f_h2, wh[1], wh[2], to, step_one)
        b_p0 = backward(a_p0, f_p1, mul(wh[0], a_h1), w0[1], w0[2], to, step_one)
        b_p1, b_p2 = load(a1p[r], 0, near), load(a1p[r], 0, far)
        c_p0 = backward(b_p0, mul(w1[0], b_p1), mul(wh[0], b_h1), w0[1], w0[2], to)
        c_p1 = backward(b_p1, mul(load(wp[r], 0, 0, far), b_p2), mul(w0[0], b_p0), w1[1], w1[2], to)
        for n, value in ((n0, c_p0), (n1, c_p1)):
            for h in (0, 1):
                total[:, n, :, pl.ds(128 * h, 128)] += value[h]
        th2, th1, tp0, tp1 = (load_t(t, at) for at in t_side(odd, r))
        i_h1 = load(i1b[r], 0, 0)
        a_one = scale(a_h1, step_one)
        g_h1 = [
            add(scale(load(r3[r], 0, 2), -1.0), mul(b_h1, dz(tp0, th2, to))),
            add(load(gb[r], 0, 1, 0), mul(a_one, dy(i_h1)), mul(b_h1, dy(th1))),
            add(load(gb[r], 0, 2, 0), mul(a_one, dx(i_h1)), mul(b_h1, dx(th1))),
        ]
        g_p0 = grads(b_p0, tp0, tp1, th1, to)
        for c in range(3):
            turn = sign if c == 0 else 1.0
            g0 = add(load(gb[r], 0, c, 1), g_p0[c])
            g1, g2 = load(gp[r], 0, c, near), load(gp[r], 0, c, far)
            store(made, final(g0, g1, scale(g_h1[c], inside), turn), slot, r, c, p0)
            store(made, final(g1, g2, g0, turn), slot, r, c, 1 - p0)

    for copy in copies(slot, s):
        copy.start()

    @pl.when(s == 3)
    def _():
        for copy in copies(1 - slot, s - 1) + copies(slot, s):
            copy.wait()


ROWS, COLS = 64, 256
PLANE = (ROWS, COLS)


def planes(count, at=0):
    return pl.BlockSpec((1, count) + PLANE, lambda s, info: (s, at, 0, 0))


def vec(count, at=0):
    return pl.BlockSpec((1, 3, count) + PLANE, lambda s, info: (s, 0, at, 0, 0))


def vec_z(at):
    return pl.BlockSpec((1, 1, 1) + PLANE, lambda s, info: (s, 0, at, 0, 0))


def whole(shape):
    return pl.BlockSpec(shape, lambda s, info: (0,) * len(shape))


def call(kernel, info, ins, outs, scratch=(), alias={}, work=1.0, name=None):
    arrays, in_specs = zip(*ins)
    shapes, out_specs = zip(*outs)
    moved = 4 * sum(a.size for a in arrays) // 2
    return pl.pallas_call(
        kernel,
        grid_spec=pltpu.PrefetchScalarGridSpec(
            num_scalar_prefetch=1,
            grid=(4,),
            in_specs=list(in_specs),
            out_specs=list(out_specs),
            scratch_shapes=list(scratch),
        ),
        out_shape=[jax.ShapeDtypeStruct(shape, f32) for shape in shapes],
        input_output_aliases=alias,
        compiler_params=pltpu.CompilerParams(vmem_limit_bytes=32 * 1024 * 1024),
        cost_estimate=pl.CostEstimate(flops=int(work * 1e7), bytes_accessed=moved, transcendentals=0),
        name=name,
    )(info, *arrays)


def shards(template, momentum, targets, step_count):
    count = lax.axis_size("space")
    groups = lax.axis_size("subj")
    place = lax.axis_index("space")
    odd = place % 2
    core_pairs = [(i, i ^ 1) for i in range(count)]
    chip_pairs = [(i, ((i + 1) ^ 1) - 1) for i in range(1, count - 1)]

    def swap(pair):
        return lax.ppermute(pair[0], "space", chip_pairs), lax.ppermute(pair[1], "space", core_pairs)

    inside = jnp.logical_and(place > 0, place < count - 1).astype(jnp.int32)
    info = jnp.concatenate([step_count, jnp.stack([odd, inside]).astype(jnp.int32)])

    def ends(array, dim):
        return tuple(lax.dynamic_slice_in_dim(array, at, 2, dim) for at in (6 * odd, 6 - 6 * odd))

    subjects = step_count.shape[0]

    def shape(*lead):
        return (subjects,) + lead + PLANE

    t_halo = swap(ends(template, 0))
    ms = ends(momentum, 2)
    mr = swap(ms)
    wide = jnp.concatenate([t_halo[0], template, t_halo[1]], axis=0)
    t = lax.all_to_all(jnp.broadcast_to(wide[None], (groups,) + wide.shape), "subj", 0, 0)
    t_spec = (t, whole(t.shape))

    def both(pair, *specs):
        return [(pair[0], specs[0]), (pair[1], specs[-1])]

    w_in, i1_in, i2_in = call(
        inner_1,
        info,
        [(momentum, vec(8)), t_spec],
        [(shape(3, 6), vec(6)), (shape(6), planes(6)), (shape(4), planes(4))],
        name="inner_1",
    )
    wp = both((w_in, w_in), vec(2, 0), vec(2, 2))
    i1p = both((i1_in, i1_in), planes(2, 0), planes(2, 2))
    two = [(shape(2), planes(2))] * 2
    three = [(shape(3), planes(3))] * 2
    *rest, s1z, s1c = call(
        outer_1,
        info,
        both(ms, vec(2)) + both(mr, vec(2)) + [t_spec] + wp + i1p,
        [(shape(3, 2), vec(2))] * 2 + two + two,
        name="outer_1",
    )
    wb, i1b, s1 = rest[0:2], rest[2:4], (s1z, s1c)

    r1 = swap(s1)
    i3_in, a4_in, i4_in = call(
        inner_2,
        info,
        [(w_in, vec(6)), (i2_in, planes(4))] + both(s1, planes(2)) + [(targets, planes(8))],
        [(shape(6), planes(6)), (shape(4), planes(4)), (shape(4), planes(4))],
        [pltpu.VMEM((8,) + PLANE, f32)],
        name="inner_2",
    )
    i3p = both((i3_in, i3_in), planes(2, 0), planes(2, 2))
    z_end = pl.BlockSpec((1, 2) + PLANE, lambda s, info: (s, 3 * info[4], 0, 0))
    c_end = pl.BlockSpec((1, 2) + PLANE, lambda s, info: (s, 3 - 3 * info[4], 0, 0))
    out = call(
        outer_2,
        info,
        both(r1, planes(2))
        + both(wb, vec(2))
        + wp
        + both(s1, planes(2))
        + both((i2_in, i2_in), planes(1, 0), planes(1, 3))
        + i3p
        + both((targets, targets), z_end, c_end),
        two + two + [(shape(1), planes(1))] * 2 + two,
        name="outer_2",
    )
    i3b, i4b, a4b, s2 = (out[2 * i : 2 * i + 2] for i in range(4))

    r2 = swap(s2)
    wb_z = both(wb, vec_z(1))
    a3_in, a2_in, g_in, warped = call(
        inner_3,
        info,
        [(w_in, vec(6))]
        + wb_z
        + both(s2, planes(1))
        + both(a4b, planes(1))
        + [(a4_in, planes(4)), (i3_in, planes(6))]
        + both(i3b, planes(1, 1))
        + [(i2_in, planes(4))]
        + both(s1, planes(2))
        + [(i1_in, planes(6)), (i4_in, planes(4))]
        + both(i4b, planes(2)),
        [(shape(6), planes(6)), (shape(4), planes(4)), (shape(3, 6), vec(6)), (shape(8), planes(8))],
        [pltpu.VMEM((8,) + PLANE, f32)] * 3,
        name="inner_3",
    )
    out = call(
        outer_3,
        info,
        both(r2, planes(2))
        + both(wb, vec(2))
        + wp
        + both(s2, planes(2))
        + both((a3_in, a3_in), planes(2, 0), planes(2, 2))
        + both(i3b, planes(2))
        + i3p
        + both(r1, planes(2))
        + both(s1, planes(2))
        + both(i1b, planes(2))
        + i1p,
        two + [(shape(3, 3), vec(3))] * 2 + three,
        [pltpu.VMEM((2,) + PLANE, f32)] * 2,
        name="outer_3",
    )
    a2b, gb, s3 = (out[2 * i : 2 * i + 2] for i in range(3))

    r3 = swap(s3)
    tile = (groups, 8, 8, COLS)
    small = (groups, 4, 8, COLS)
    a1_in, g_full, total, mg = call(
        inner_4,
        info,
        [(w_in, vec(6))]
        + wb_z
        + [(a2_in, planes(4))]
        + both(a2b, planes(2))
        + [t_spec, (g_in, vec(6))]
        + both(gb, vec(1, 2)),
        [(shape(6), planes(6)), (shape(3, 6), vec(6)), (small, whole(small)), (shape(3, 8), vec(8))],
        [pltpu.VMEM((8,) + PLANE, f32)] * 2,
        name="inner_4",
    )
    anywhere = pl.BlockSpec(memory_space=pl.ANY)
    total, momentum_gradient = call(
        outer_4,
        info,
        both(r3, planes(3))
        + both(wb, vec(2))
        + wp
        + both(s3, planes(3))
        + both((a1_in, a1_in), planes(2, 0), planes(2, 2))
        + both(gb, vec(3))
        + both((g_full, g_full), vec(2, 0), vec(2, 2))
        + both(i1b, planes(2))
        + [t_spec, (total, whole(small)), (mg, anywhere)],
        [(tile, whole(tile)), (shape(3, 8), anywhere)],
        [pltpu.VMEM((2, 2, 3, 2) + PLANE, f32), pltpu.SemaphoreType.DMA((2, 2))],
        alias={19: 1},
        name="outer_4",
    )
    parts = lax.all_to_all(total, "subj", 0, 0)
    template_gradient = jnp.sum(parts, axis=0)
    return (warped, template_gradient, momentum_gradient)


def solution(mesh):
    in_specs = (
        P("space", "subj", None),
        P("subj", None, "space", None, None),
        P("subj", "space", None, None),
        P("subj"),
    )
    out_specs = (
        P("subj", "space", None, None),
        P("space", "subj", None),
        P("subj", None, "space", None, None),
    )
    return jax.shard_map(shards, mesh=mesh, in_specs=in_specs, out_specs=out_specs, check_vma=False)
```

time: 352 us -> 149 us (0.42)
  other arithmetic: 93.6 us -> 0.75 us
  waiting for transfers between devices: 99.6 us -> 31 us
  Pallas kernels: 0 us -> 48.1 us
  starting transfers between devices: 78.2 us -> 30.3 us
  blocking collectives: 42.4 us -> 19.9 us
  between operations: 14.7 us -> 1 us
    psum x1 -> x0, waiting for transfers between devices: 81.3 us -> none  [shards(): total = lax.psum(local_sum, 'subj')]
    ppermute x20 -> x10, starting transfers between devices: 78.2 us -> 22.9 us  [the longest x5 22.5 us: swap(): lax.ppermute(pair[0], 'space', chip_pairs)]
    pallas_call x0 -> x8, Pallas kernels: none -> 48.1 us  [call(): pl.pallas_call(kernel, grid_spec=pltpu.PrefetchScalarGridSpec(num_scalar_...]
    all_gather x1 -> x0, blocking collectives: 42.4 us -> none  [shards(): whole_tmpl = lax.all_gather(template, 'subj', axis=1, tiled=True)]
    add x2 -> x0, other arithmetic: 39.5 us -> none  [rim_kernel(): return center + smoothing * (nsum - 6.0 * center)]
    another operation x3 -> x0, other arithmetic: 31.1 us -> none  [shards(): velocity_grad = jnp.stack([grad_z, grad_y, grad_x], axis=1)]
    all_to_all x0 -> x1, blocking collectives: none -> 19.9 us  [shards(): parts = lax.all_to_all(total, 'subj', 0, 0)]
    mul x7 -> x0, other arithmetic: 11.8 us -> none  [the longest x3 7.81 us: shards(): padded_flux = with_halo(vel_z * adjoint, (('space', 1),), 1)]
  transfers between devices with their start and end apart: 21 -> 11, of which waited for: 12 -> 3; matrix products, arithmetic and copies ran while one was open for 11% -> 1% of each run, Pallas kernels for 0% -> 19%
where the time goes in v1:
time: 149 us; the launch traced here: 148 us
  Pallas kernels  48.1 us (32%)
  waiting for transfers between devices  31 us (21%)
  starting transfers between devices  30.3 us (20%)
  blocking collectives  19.9 us (13%)
  local copies, waits for them, and re-layouts  16.7 us (11%)
    pallas_call x8, Pallas kernels, call(): pl.pallas_call(kernel, grid_spec=pltpu.PrefetchScalarGridSpec(num_scalar_...  48.1 us
    ppermute x5, starting transfers between devices, swap(): lax.ppermute(pair[0], 'space', chip_pairs)  22.5 us
    ppermute x5, waiting for transfers between devices, swap(): lax.ppermute(pair[0], 'space', chip_pairs)  21 us
    all_to_all x1, blocking collectives, shards(): parts = lax.all_to_all(total, 'subj', 0, 0)  19.9 us
    unnamed x42, local copies, waits for them, and re-layouts  12.4 us
    all_to_all x1, waiting for transfers between devices, shards(): lax.all_to_all(jnp.broadcast_to(wide[None], (groups,) + wide.shape), 'sub...  10 us
    all_to_all x1, starting transfers between devices, shards(): lax.all_to_all(jnp.broadcast_to(wide[None], (groups,) + wide.shape), 'sub...  7.43 us
    dynamic_slice x2, local copies, waits for them, and re-layouts, ends(): lax.dynamic_slice_in_dim(array, at, 2, dim)  3.37 us
  transfers between devices with their start and end apart: 11, of which 3 were waited for; matrix products, arithmetic and copies ran while one was open for 1% of the time, Pallas kernels for 19%

profile of v1, /device:TPU:6, one launch (start us, length us, event | category | flops | bytes accessed | tf_op | source)
XLA Modules:
  0.0 147.8 jit_solution(3615573560467267111)
XLA Ops:
  0.7 3.4 %constant_dynamic-slice_fusion = (f32[4,3,2,64,256]{4,3,2,1,0:T(8,128)S(1)}, f32[4,3,2,64,256]{4,3,2,1,0:T(8,128)}) fusion(f32[4,3,8,64,256]{4,3,2,1,0:T(8,128)} %m.1, s32[]{:T(128)S(6)} %select_n.17, s32[]{:T(128)S(6)} %select_n.16), kind=kLoop, calls=%fused_computation.1 | loop fusion | bytes 6291464 | tf_op jit(solution)/shard_map/dynamic_slice | solution.py:645
  4.0 0.0 collective-permute-start.3
  4.0 6.3 %collective-permute-start.2 = (f32[4,3,2,64,256]{4,3,2,1,0:T(8,128)}, f32[4,3,2,64,256]{4,3,2,1,0:T(8,128)}, u32[]{:S(2)}, u32[]{:S(2)}) collective-permute-start(f32[4,3,2,64,256]{4,3,2,1,0:T(8,128)} %get-tuple-element.76.refs_0_), channel_id=1, source_target_pairs={{8,16},{16,8},{24,32},{32,24},{40,48},{48,40},{56,64},{64,56},{72,... | collective-permute-start | bytes 4718600 | tf_op jit(solution)/shard_map/ppermute | solution.py:639
  10.4 0.0 copy-done.17
  10.4 1.9 %collective-permute-start = (f32[2,8,256]{2,1,0:T(8,128)S(1)}, f32[2,8,256]{2,1,0:T(8,128)S(1)}, u32[]{:S(2)}, u32[]{:S(2)}) collective-permute-start(f32[2,8,256]{2,1,0:T(8,128)S(1)} %get-tuple-element.77), channel_id=1, source_target_pairs={{8,16},{16,8},{24,32},{32,24},{40,48},{48,40},{56,64},{64,56},{72,... | collective-permute-start | bytes 49160 | tf_op jit(solution)/shard_map/ppermute | solution.py:639
  12.3 0.1 collective-permute-start.1
  12.4 16.4 %collective-permute-done = f32[2,8,256]{2,1,0:T(8,128)S(1)} collective-permute-done((f32[2,8,256]{2,1,0:T(8,128)S(1)}, f32[2,8,256]{2,1,0:T(8,128)S(1)}, u32[]{:S(2)}, u32[]{:S(2)}) %collective-permute-start) | collective-permute-done | bytes 16416 | tf_op jit(solution)/shard_map/ppermute | solution.py:639
  28.8 0.0 collective-permute-done.1
  28.8 0.9 broadcast_in_dim.2
  29.8 7.4 %all-to-all-start = ((f32[8,12,8,256]{3,2,1,0:T(8,128)}), f32[8,12,8,256]{3,2,1,0:T(8,128)S(1)}, u32[]{:S(2)}, u32[]{:S(2)}) async-start(f32[8,12,8,256]{3,2,1,0:T(8,128)} %broadcast_in_dim.2), calls=%async_computation | async-start | bytes 1572864 | tf_op jit(solution)/shard_map/all_to_all | solution.py:656
  37.2 0.1 pad_add_fusion.info
  37.3 10.0 %all-to-all-done.t.refs_4_.refs_6_.refs_16_ = f32[8,12,8,256]{3,2,1,0:T(8,128)S(1)} async-done(((f32[8,12,8,256]{3,2,1,0:T(8,128)}), f32[8,12,8,256]{3,2,1,0:T(8,128)S(1)}, u32[]{:S(2)}, u32[]{:S(2)}) %all-to-all-start) | async-done | bytes 786464 | tf_op jit(solution)/shard_map/all_to_all | solution.py:656
  47.3 2.8 %copy-done.3 = f32[4,3,8,64,256]{4,3,2,1,0:T(8,128)S(1)} copy-done((f32[4,3,8,64,256]{4,3,2,1,0:T(8,128)S(1)}, f32[4,3,8,64,256]{4,3,2,1,0:T(8,128)}, u32[]{:S(2)}) %copy-start.3) | copy-done | bytes 6291480
  50.1 7.3 %inner_1.1 = (f32[4,3,6,64,256]{4,3,2,1,0:T(8,128)S(1)}, f32[4,6,64,256]{3,2,1,0:T(8,128)S(1)}, f32[4,4,64,256]{3,2,1,0:T(8,128)S(1)}) custom-call(s32[6]{0:T(128)S(1)} %pad_add_fusion.info, f32[4,3,8,64,256]{4,3,2,1,0:T(8,128)S(1)} %copy-done.3, f32[8,12,8,256]{3,2,1,0:T(8,128)S(1)} %all-to-all-done.t.refs_4_.refs_6_.refs_16_), custom_call_target="tpu_custom_call" | custom-call | flops 10000000 | bytes 3538944 | tf_op jit(solution)/shard_map/inner_1/pallas_call | solution.py:613
  57.4 0.0 copy-done.4
  57.4 0.0 copy-start
  57.4 0.0 collective-permute-done.3.refs_3_
  57.4 0.0 collective-permute-done.2.refs_2_
  57.4 2.6 %copy-done.5 = f32[4,3,2,64,256]{4,3,2,1,0:T(8,128)S(1)} copy-done((f32[4,3,2,64,256]{4,3,2,1,0:T(8,128)S(1)}, f32[4,3,2,64,256]{4,3,2,1,0:T(8,128)}, u32[]{:S(2)}) %copy-start.5) | copy-done | bytes 1572888
  60.0 5.9 %outer_1.1 = (f32[4,3,2,64,256]{4,3,2,1,0:T(8,128)S(1)}, f32[4,3,2,64,256]{4,3,2,1,0:T(8,128)S(1)}, f32[4,2,64,256]{3,2,1,0:T(8,128)S(1)}, f32[4,2,64,256]{3,2,1...) custom-call(s32[6]{0:T(128)S(1)} %pad_add_fusion.info, ...), custom_call_target="tpu_custom_call" | custom-call | flops 10000000 | bytes 9830400 | tf_op jit(solution)/shard_map/outer_1/pallas_call | solution.py:613
  66.0 6.0 %collective-permute-start.4 = (f32[4,2,64,256]{3,2,1,0:T(8,128)S(1)}, f32[4,2,64,256]{3,2,1,0:T(8,128)S(1)}, u32[]{:S(2)}, u32[]{:S(2)}) collective-permute-start(f32[4,2,64,256]{3,2,1,0:T(8,128)S(1)} %get-tuple-element.43.s1z.refs_6_.refs_12_.refs_16_), channel_id=1, source_target_pairs={{8,16},{16,8},{24,32},{32,24},{40,48},{48,40},{56,64},{64,56},{72,... | collective-permute-start | bytes 1572872 | tf_op jit(solution)/shard_map/ppermute | solution.py:639
  72.0 0.1 collective-permute-start.5
  72.1 2.2 %inner_2.1 = (f32[4,6,64,256]{3,2,1,0:T(8,128)S(1)}, f32[4,4,64,256]{3,2,1,0:T(8,128)S(1)}, f32[4,4,64,256]{3,2,1,0:T(8,128)S(1)}) custom-call(s32[6]{0:T(128)S(1)} %pad_add_fusion.info, f32[4,3,6,64,256]{4,3,2,1,0:T(8,128)S(1)} %get-tuple-element.39.refs_5_.refs_6_.w_in.refs_4_.refs_0_, ...), custom_call_target="tpu_custom_call" | custom-call | flops 10000000 | bytes 4456448 | tf_op jit(solution)/shard_map/inner_2/pallas_call | solution.py:613
  74.3 0.0 copy-done.7
  74.3 0.0 copy-done.10
  74.3 4.6 %collective-permute-done.4.refs_0_.refs_14_ = f32[4,2,64,256]{3,2,1,0:T(8,128)S(1)} collective-permute-done((f32[4,2,64,256]{3,2,1,0:T(8,128)S(1)}, f32[4,2,64,256]{3,2,1,0:T(8,128)S(1)}, u32[]{:S(2)}, u32[]{:S(2)}) %collective-permute-start.4) | collective-permute-done | bytes 524320 | tf_op jit(solution)/shard_map/ppermute | solution.py:639
  78.8 0.0 collective-permute-done.5.refs_1_.refs_15_
  78.8 2.0 %outer_2.1 = (f32[4,2,64,256]{3,2,1,0:T(8,128)S(1)}, f32[4,2,64,256]{3,2,1,0:T(8,128)S(1)}, f32[4,2,64,256]{3,2,1,0:T(8,128)S(1)}, f32[4,2,64,256]{3,2,1,0:T(8,1...) custom-call(s32[6]{0:T(128)S(1)} %pad_add_fusion.info, ...), custom_call_target="tpu_custom_call" | custom-call | flops 10000000 | bytes 12058624 | tf_op jit(solution)/shard_map/outer_2/pallas_call | solution.py:613
  80.8 5.8 %collective-permute-start.6 = (f32[4,2,64,256]{3,2,1,0:T(8,128)S(1)}, f32[4,2,64,256]{3,2,1,0:T(8,128)S(1)}, u32[]{:S(2)}, u32[]{:S(2)}) collective-permute-start(f32[4,2,64,256]{3,2,1,0:T(8,128)S(1)} %get-tuple-element.47.refs_3_.refs_6_), channel_id=1, source_target_pairs={{8,16},{16,8},{24,32},{32,24},{40,48},{48,40},{56,64},{64,56},{72,... | collective-permute-start | bytes 1572872 | tf_op jit(solution)/shard_map/ppermute | solution.py:639
  86.6 0.1 collective-permute-start.7
  86.7 7.5 %inner_3.1 = (f32[4,6,64,256]{3,2,1,0:T(8,128)S(1)}, f32[4,4,64,256]{3,2,1,0:T(8,128)S(1)}, f32[4,3,6,64,256]{4,3,2,1,0:T(8,128)S(1)}, f32[4,8,64,256]{3,2,1,0:T(8,128)}) custom-call(s32[6]{0:T(128)S(1)} %pad_add_fusion.info, f32[4,3,6,64,256]{4,3,2,1,0:T(8,128)} %copy-done, f32[4,3,2,64,256]{4,3,2,1,0:T(8,128)S(1)} %get-tuple-element.41.refs_2_.refs_1_, ...), custom_call_target="tpu_custom_call" | custom-call | flops 10000000 | bytes 9437184 | tf_op jit(solution)/shard_map/inner_3/pallas_call | solution.py:613
  94.2 2.1 %copy-done.6 = f32[4,3,6,64,256]{4,3,2,1,0:T(8,128)} copy-done((f32[4,3,6,64,256]{4,3,2,1,0:T(8,128)}, f32[4,3,6,64,256]{4,3,2,1,0:T(8,128)S(1)}, u32[]{:S(2)}) %copy-start.6) | copy-done | bytes 4718616
  96.4 0.0 collective-permute-done.6.refs_0_
  96.4 0.0 collective-permute-done.7.refs_1_
  96.4 0.0 slice-start
  96.4 1.4 copy-done.14
  97.9 4.8 %outer_3.1 = (f32[4,2,64,256]{3,2,1,0:T(8,128)S(1)}, f32[4,2,64,256]{3,2,1,0:T(8,128)S(1)}, f32[4,3,3,64,256]{4,3,2,1,0:T(8,128)S(1)}, f32[4,3,3,64,256]{4,3,2,1...) custom-call(s32[6]{0:T(128)S(1)} %pad_add_fusion.info, ...), custom_call_target="tpu_custom_call" | custom-call | flops 10000000 | bytes 14155776 | tf_op jit(solution)/shard_map/outer_3/pallas_call | solution.py:613
  102.7 2.5 %collective-permute-start.8 = (f32[4,3,64,256]{3,2,1,0:T(8,128)S(1)}, f32[4,3,64,256]{3,2,1,0:T(8,128)S(1)}, u32[]{:S(2)}, u32[]{:S(2)}) collective-permute-start(f32[4,3,64,256]{3,2,1,0:T(8,128)S(1)} %get-tuple-element.61.refs_6_), channel_id=1, source_target_pairs={{8,16},{16,8},{24,32},{32,24},{40,48},{48,40},{56,64},{64,56},{72,... | collective-permute-start | bytes 2359304 | tf_op jit(solution)/shard_map/ppermute | solution.py:639
  105.2 0.1 collective-permute-start.9
  105.3 0.0 slice-done
  105.4 1.2 copy-done.16
  106.6 10.6 %inner_4.1 = (f32[4,6,64,256]{3,2,1,0:T(8,128)S(1)}, f32[4,3,6,64,256]{4,3,2,1,0:T(8,128)S(1)}, f32[8,4,8,256]{3,2,1,0:T(8,128)S(1)}, f32[4,3,8,64,256]{4,3,2,1,0:T(8,128)}) custom-call(s32[6]{0:T(128)S(1)} %pad_add_fusion.info, f32[4,3,6,64,256]{4,3,2,1,0:T(8,128)S(1)} %bitcast.3, f32[4,3,2,64,256]{4,3,2,1,0:T(8,128)S(1)} %get-tuple-element.41.refs_2_.refs_1_, ...), custom_call_target="tpu_custom_call" | custom-call | flops 10000000 | bytes 10092544 | tf_op jit(solution)/shard_map/inner_4/pallas_call | solution.py:613
  117.1 2.1 %copy-done.1 = f32[4,3,6,64,256]{4,3,2,1,0:T(8,128)} copy-done((f32[4,3,6,64,256]{4,3,2,1,0:T(8,128)}, f32[4,3,6,64,256]{4,3,2,1,0:T(8,128)S(1)}, u32[]{:S(2)}) %copy-start.1) | copy-done | bytes 4718616
  119.3 0.0 collective-permute-done.8.refs_0_
  119.3 0.0 collective-permute-done.9.refs_1_
  119.3 7.9 %outer_4.1 = (f32[8,8,8,256]{3,2,1,0:T(8,128)S(1)}, f32[4,3,8,64,256]{4,3,2,1,0:T(8,128)}) custom-call(s32[6]{0:T(128)S(1)} %pad_add_fusion.info, f32[4,3,64,256]{3,2,1,0:T(8,128)S(1)} %collective-permute-done.8.refs_0_, f32[4,3,64,256]{3,2,1,0:T(8,128)S(1)} %collective-permute-done.9.refs_1_, ...), custom_call_target="tpu_custom_call", output_to_operand_aliasing={{1}: (19, {})} | custom-call | flops 10000000 | bytes 20709376 | tf_op jit(solution)/shard_map/outer_4/pallas_call | solution.py:613
  127.2 19.9 %all_to_all.10 = f32[8,8,8,256]{3,2,1,0:T(8,128)S(1)} all-to-all(f32[8,8,8,256]{3,2,1,0:T(8,128)S(1)} %get-tuple-element.73), channel_id=1, replica_groups=mesh['space'=16,'subj'=8] {'subj'}, dimensions={0} | all-to-all | bytes 1048576 | tf_op jit(solution)/shard_map/all_to_all | solution.py:782
  147.1 0.7 reduce_sum.9
  (32 shorter events, 0.1 us)
Async XLA Ops:
  0.7 9.7 %copy-start.17 = (f32[8,8,256]{2,1,0:T(8,128)S(1)}, f32[8,8,256]{2,1,0:T(8,128)}, u32[]{:S(2)}) copy-start(f32[8,8,256]{2,1,0:T(8,128)} %param.4) | copy-start | bytes 196612
  4.0 53.4 %copy-start.4 = (f32[4,3,2,64,256]{4,3,2,1,0:T(8,128)}, f32[4,3,2,64,256]{4,3,2,1,0:T(8,128)S(1)}, u32[]{:S(2)}) copy-start(f32[4,3,2,64,256]{4,3,2,1,0:T(8,128)S(1)} %get-tuple-element.75.refs_1_) | copy-start | bytes 4718596
  4.0 33.2 %copy-start.18 = (s32[4]{0:T(128)S(1)}, s32[4]{0:T(128)}, u32[]{:S(2)}) copy-start(s32[4]{0:T(128)} %param.7) | copy-start | bytes 52
  4.0 53.4 %collective-permute-start.3 = (f32[4,3,2,64,256]{4,3,2,1,0:T(8,128)S(1)}, f32[4,3,2,64,256]{4,3,2,1,0:T(8,128)}, u32[]{:S(2)}, u32[]{:S(2)}) collective-permute-start(f32[4,3,2,64,256]{4,3,2,1,0:T(8,128)S(1)} %get-tuple-element.75.refs_1_), channel_id=1, source_target_pairs={{0,8},{8,0},{16,24},{24,16},{32,40},{40,32},{48,56},{56,48},{64,72... | collective-permute-start | bytes 4718600 | tf_op jit(solution)/shard_map/ppermute | solution.py:639
  4.0 53.4 %collective-permute-start.2 = (f32[4,3,2,64,256]{4,3,2,1,0:T(8,128)}, f32[4,3,2,64,256]{4,3,2,1,0:T(8,128)}, u32[]{:S(2)}, u32[]{:S(2)}) collective-permute-start(f32[4,3,2,64,256]{4,3,2,1,0:T(8,128)} %get-tuple-element.76.refs_0_), channel_id=1, source_target_pairs={{8,16},{16,8},{24,32},{32,24},{40,48},{48,40},{56,64},{64,56},{72,... | collective-permute-start | bytes 4718600 | tf_op jit(solution)/shard_map/ppermute | solution.py:639
  10.4 18.4 %collective-permute-start = (f32[2,8,256]{2,1,0:T(8,128)S(1)}, f32[2,8,256]{2,1,0:T(8,128)S(1)}, u32[]{:S(2)}, u32[]{:S(2)}) collective-permute-start(f32[2,8,256]{2,1,0:T(8,128)S(1)} %get-tuple-element.77), channel_id=1, source_target_pairs={{8,16},{16,8},{24,32},{32,24},{40,48},{48,40},{56,64},{64,56},{72,... | collective-permute-start | bytes 49160 | tf_op jit(solution)/shard_map/ppermute | solution.py:639
  12.3 16.5 %collective-permute-start.1 = (f32[2,8,256]{2,1,0:T(8,128)S(1)}, f32[2,8,256]{2,1,0:T(8,128)S(1)}, u32[]{:S(2)}, u32[]{:S(2)}) collective-permute-start(f32[2,8,256]{2,1,0:T(8,128)S(1)} %get-tuple-element.78), channel_id=1, source_target_pairs={{0,8},{8,0},{16,24},{24,16},{32,40},{40,32},{48,56},{56,48},{64,72... | collective-permute-start | bytes 49160 | tf_op jit(solution)/shard_map/ppermute | solution.py:639
  29.8 17.6 %all-to-all-start = ((f32[8,12,8,256]{3,2,1,0:T(8,128)}), f32[8,12,8,256]{3,2,1,0:T(8,128)S(1)}, u32[]{:S(2)}, u32[]{:S(2)}) async-start(f32[8,12,8,256]{3,2,1,0:T(8,128)} %broadcast_in_dim.2), calls=%async_computation | async-start | bytes 1572864 | tf_op jit(solution)/shard_map/all_to_all | solution.py:656
  47.3 2.8 %copy-start.3 = (f32[4,3,8,64,256]{4,3,2,1,0:T(8,128)S(1)}, f32[4,3,8,64,256]{4,3,2,1,0:T(8,128)}, u32[]{:S(2)}) copy-start(f32[4,3,8,64,256]{4,3,2,1,0:T(8,128)} %m.1) | copy-start | bytes 18874372
  57.4 21.4 %copy-start = (f32[4,3,6,64,256]{4,3,2,1,0:T(8,128)}, f32[4,3,6,64,256]{4,3,2,1,0:T(8,128)S(1)}, u32[]{:S(2)}) copy-start(f32[4,3,6,64,256]{4,3,2,1,0:T(8,128)S(1)} %get-tuple-element.39.refs_5_.refs_6_.w_in.refs_4_.refs_0_) | copy-start | bytes 14155780
  57.4 2.6 %copy-start.5 = (f32[4,3,2,64,256]{4,3,2,1,0:T(8,128)S(1)}, f32[4,3,2,64,256]{4,3,2,1,0:T(8,128)}, u32[]{:S(2)}) copy-start(f32[4,3,2,64,256]{4,3,2,1,0:T(8,128)} %copy-done.4) | copy-start | bytes 4718596
  60.0 12.1 %copy-start.2 = (f32[4,8,64,256]{3,2,1,0:T(8,128)S(1)}, f32[4,8,64,256]{3,2,1,0:T(8,128)}, u32[]{:S(2)}) copy-start(f32[4,8,64,256]{3,2,1,0:T(8,128)} %refs_13_.1) | copy-start | bytes 6291460
  66.0 8.3 %copy-start.7 = (f32[4,2,64,256]{3,2,1,0:T(8,128)}, f32[4,2,64,256]{3,2,1,0:T(8,128)S(1)}, u32[]{:S(2)}) copy-start(f32[4,2,64,256]{3,2,1,0:T(8,128)S(1)} %get-tuple-element.59.refs_18_.refs_14_) | copy-start | bytes 1572868
  66.0 8.3 %copy-start.10 = (f32[4,2,64,256]{3,2,1,0:T(8,128)}, f32[4,2,64,256]{3,2,1,0:T(8,128)S(1)}, u32[]{:S(2)}) copy-start(f32[4,2,64,256]{3,2,1,0:T(8,128)S(1)} %get-tuple-element.60.refs_19_.refs_15_) | copy-start | bytes 1572868
  66.0 12.9 %collective-permute-start.4 = (f32[4,2,64,256]{3,2,1,0:T(8,128)S(1)}, f32[4,2,64,256]{3,2,1,0:T(8,128)S(1)}, u32[]{:S(2)}, u32[]{:S(2)}) collective-permute-start(f32[4,2,64,256]{3,2,1,0:T(8,128)S(1)} %get-tuple-element.43.s1z.refs_6_.refs_12_.refs_16_), channel_id=1, source_target_pairs={{8,16},{16,8},{24,32},{32,24},{40,48},{48,40},{56,64},{64,56},{72,... | collective-permute-start | bytes 1572872 | tf_op jit(solution)/shard_map/ppermute | solution.py:639
  72.0 6.9 %collective-permute-start.5 = (f32[4,2,64,256]{3,2,1,0:T(8,128)S(1)}, f32[4,2,64,256]{3,2,1,0:T(8,128)S(1)}, u32[]{:S(2)}, u32[]{:S(2)}) collective-permute-start(f32[4,2,64,256]{3,2,1,0:T(8,128)S(1)} %get-tuple-element.44.s1c.refs_7_.refs_13_.refs_17_), channel_id=1, source_target_pairs={{0,8},{8,0},{16,24},{24,16},{32,40},{40,32},{48,56},{56,48},{64,72... | collective-permute-start | bytes 1572872 | tf_op jit(solution)/shard_map/ppermute | solution.py:639
  80.8 13.4 %copy-start.13 = (f32[4,2,64,256]{3,2,1,0:T(8,128)}, f32[4,2,64,256]{3,2,1,0:T(8,128)S(1)}, u32[]{:S(2)}) copy-start(f32[4,2,64,256]{3,2,1,0:T(8,128)S(1)} %get-tuple-element.52.refs_9_.refs_10_) | copy-start | bytes 1572868
  80.8 15.5 %collective-permute-start.6 = (f32[4,2,64,256]{3,2,1,0:T(8,128)S(1)}, f32[4,2,64,256]{3,2,1,0:T(8,128)S(1)}, u32[]{:S(2)}, u32[]{:S(2)}) collective-permute-start(f32[4,2,64,256]{3,2,1,0:T(8,128)S(1)} %get-tuple-element.47.refs_3_.refs_6_), channel_id=1, source_target_pairs={{8,16},{16,8},{24,32},{32,24},{40,48},{48,40},{56,64},{64,56},{72,... | collective-permute-start | bytes 1572872 | tf_op jit(solution)/shard_map/ppermute | solution.py:639
  86.6 9.8 %collective-permute-start.7 = (f32[4,2,64,256]{3,2,1,0:T(8,128)S(1)}, f32[4,2,64,256]{3,2,1,0:T(8,128)S(1)}, u32[]{:S(2)}, u32[]{:S(2)}) collective-permute-start(f32[4,2,64,256]{3,2,1,0:T(8,128)S(1)} %get-tuple-element.48.refs_4_.refs_7_), channel_id=1, source_target_pairs={{0,8},{8,0},{16,24},{24,16},{32,40},{40,32},{48,56},{56,48},{64,72... | collective-permute-start | bytes 1572872 | tf_op jit(solution)/shard_map/ppermute | solution.py:639
  86.7 9.7 %copy-start.8 = (f32[4,2,64,256]{3,2,1,0:T(8,128)S(1)}, f32[4,2,64,256]{3,2,1,0:T(8,128)}, u32[]{:S(2)}) copy-start(f32[4,2,64,256]{3,2,1,0:T(8,128)} %copy-done.7) | copy-start | bytes 1572868
  86.7 9.7 %copy-start.11 = (f32[4,2,64,256]{3,2,1,0:T(8,128)S(1)}, f32[4,2,64,256]{3,2,1,0:T(8,128)}, u32[]{:S(2)}) copy-start(f32[4,2,64,256]{3,2,1,0:T(8,128)} %copy-done.10) | copy-start | bytes 1572868
  94.2 2.1 %copy-start.6 = (f32[4,3,6,64,256]{4,3,2,1,0:T(8,128)}, f32[4,3,6,64,256]{4,3,2,1,0:T(8,128)S(1)}, u32[]{:S(2)}) copy-start(f32[4,3,6,64,256]{4,3,2,1,0:T(8,128)S(1)} %get-tuple-element.66.refs_7_) | copy-start | bytes 14155780
  96.4 6.3 %copy-start.15 = (f32[4,4,64,256]{3,2,1,0:T(8,128)}, f32[4,4,64,256]{3,2,1,0:T(8,128)S(1)}, u32[]{:S(2)}) copy-start(f32[4,4,64,256]{3,2,1,0:T(8,128)S(1)} %get-tuple-element.63.refs_3_) | copy-start | bytes 3145732
  96.4 9.0 %slice-start = ((s8[4718592]{0:T(1024)(128)(4,1)}), s8[4194304]{0:T(1024)(128)(4,1)S(1)}, s32[]{:S(2)}) async-start(s8[4718592]{0:T(1024)(128)(4,1)} %bitcast.2), calls=%async_computation.2 | async-start | bytes 8388608
  96.4 1.4 copy-start.14
  97.9 7.5 %slice-start.1 = ((s8[4718592]{0:T(1024)(128)(4,1)}), s8[524288]{0:T(1024)(128)(4,1)S(1)}, s32[]{:S(2)}) async-start(s8[4718592]{0:T(1024)(128)(4,1)} %bitcast.2), calls=%async_computation.3 | async-start | bytes 1048576
  102.7 16.6 %collective-permute-start.8 = (f32[4,3,64,256]{3,2,1,0:T(8,128)S(1)}, f32[4,3,64,256]{3,2,1,0:T(8,128)S(1)}, u32[]{:S(2)}, u32[]{:S(2)}) collective-permute-start(f32[4,3,64,256]{3,2,1,0:T(8,128)S(1)} %get-tuple-element.61.refs_6_), channel_id=1, source_target_pairs={{8,16},{16,8},{24,32},{32,24},{40,48},{48,40},{56,64},{64,56},{72,... | collective-permute-start | bytes 2359304 | tf_op jit(solution)/shard_map/ppermute | solution.py:639
  105.2 14.0 %collective-permute-start.9 = (f32[4,3,64,256]{3,2,1,0:T(8,128)S(1)}, f32[4,3,64,256]{3,2,1,0:T(8,128)S(1)}, u32[]{:S(2)}, u32[]{:S(2)}) collective-permute-start(f32[4,3,64,256]{3,2,1,0:T(8,128)S(1)} %get-tuple-element.62.refs_7_), channel_id=1, source_target_pairs={{0,8},{8,0},{16,24},{24,16},{32,40},{40,32},{48,56},{56,48},{64,72... | collective-permute-start | bytes 2359304 | tf_op jit(solution)/shard_map/ppermute | solution.py:639
  105.4 1.2 copy-start.16
  106.6 12.7 %copy-start.9 = (f32[4,2,64,256]{3,2,1,0:T(8,128)S(1)}, f32[4,2,64,256]{3,2,1,0:T(8,128)}, u32[]{:S(2)}) copy-start(f32[4,2,64,256]{3,2,1,0:T(8,128)} %copy-done.7) | copy-start | bytes 1572868
  106.6 12.7 %copy-start.12 = (f32[4,2,64,256]{3,2,1,0:T(8,128)S(1)}, f32[4,2,64,256]{3,2,1,0:T(8,128)}, u32[]{:S(2)}) copy-start(f32[4,2,64,256]{3,2,1,0:T(8,128)} %copy-done.10) | copy-start | bytes 1572868
  117.1 2.1 %copy-start.1 = (f32[4,3,6,64,256]{4,3,2,1,0:T(8,128)}, f32[4,3,6,64,256]{4,3,2,1,0:T(8,128)S(1)}, u32[]{:S(2)}) copy-start(f32[4,3,6,64,256]{4,3,2,1,0:T(8,128)S(1)} %get-tuple-element.70.refs_12_.refs_13_) | copy-start | bytes 14155780

commit v2 on v0

v2 whole, which is shorter than its diff:
```python
import jax
import jax.numpy as jnp
from jax import lax
from jax.experimental import pallas as pl
from jax.experimental.pallas import tpu as pltpu
from jax.sharding import PartitionSpec as P

time_step = 0.15
smoothing = 0.1
half = 0.5 * time_step
centre = 1.0 - 6.0 * smoothing
f32 = jnp.float32


class Plane:
    def __init__(self, rows):
        self.rows, self.known, self.rolled = rows, {}, {}

    def at(self, b):
        if b not in self.known:
            self.known[b] = tuple(self.rows(b))
        return self.known[b]

    def turned(self, b, by):
        if (b, by) not in self.rolled:
            self.rolled[b, by] = tuple(pltpu.roll(x, by, axis=0) for x in self.at(b))
        return self.rolled[b, by]


BLOCKS = 8


def halves(h):
    return pl.ds(128 * h, 128)


def load(ref, *at):
    return Plane(lambda b: [ref[at + (pl.ds(8 * b, 8), halves(h))] for h in (0, 1)])


def store(ref, plane, *at):
    store_all([(ref, plane, at)])


def store_all(targets):
    for b in range(BLOCKS):
        for ref, plane, at in targets:
            for h, value in enumerate(plane.at(b)):
                ref[at + (pl.ds(8 * b, 8), halves(h))] = value


def add_t(ref, plane, p):
    for b in range(BLOCKS):
        for h, value in enumerate(plane.at(b)):
            ref[b, p, :, halves(h)] += value


def each(fn, *planes):
    return Plane(lambda b: [fn(*x) for x in zip(*(plane.at(b) for plane in planes))])


def add(*planes):
    total = planes[0]
    for plane in planes[1:]:
        total = each(lambda a, b: a + b, total, plane)
    return total


def sub(a, b):
    return each(lambda x, y: x - y, a, b)


def mul(a, b):
    return each(lambda x, y: x * y, a, b)


def scale(a, factor):
    return each(lambda x: x * factor, a)


def y_sides(plane):
    def rows(b, by, edge, step):
        row = lax.broadcasted_iota(jnp.int32, (8, 128), 0)
        here, there = plane.turned(b, by), b + step
        over = plane.turned(there, by) if 0 <= there < BLOCKS else (0.0, 0.0)
        return [jnp.where(row == edge, o, x) for o, x in zip(over, here)]

    return Plane(lambda b: rows(b, 1, 0, -1)), Plane(lambda b: rows(b, 7, 7, 1))


def x_sides(plane):
    def before(b):
        lane = lax.broadcasted_iota(jnp.int32, (8, 128), 1)
        left, right = (pltpu.roll(x, 1, axis=1) for x in plane.at(b))
        return jnp.where(lane == 0, 0.0, left), jnp.where(lane == 0, left, right)

    def after(b):
        lane = lax.broadcasted_iota(jnp.int32, (8, 128), 1)
        left, right = (pltpu.roll(x, 127, axis=1) for x in plane.at(b))
        return jnp.where(lane == 127, right, left), jnp.where(lane == 127, 0.0, right)

    return Plane(before), Plane(after)


def dy(plane):
    before, after = y_sides(plane)
    return sub(after, before)


def dx(plane):
    before, after = x_sides(plane)
    return sub(after, before)


def smooth(mid, inner, outer, a, b):
    total = add(*(plane for plane in (inner, outer) if plane is not None), *y_sides(mid), *x_sides(mid))
    return each(lambda m, t: a * m + b * t, mid, total)


def dz(inner, outer, toward):
    return sub(inner, outer) if toward > 0 else sub(outer, inner)


def forward(mid, inner, outer, w, toward=1):
    change = add(mul(w[0], dz(inner, outer, toward)), mul(w[1], dy(mid)), mul(w[2], dx(mid)))
    return sub(mid, change)


def forward_by(mid, inner, outer, slopes, w, toward=1):
    change = add(mul(w[0], dz(inner, outer, toward)), mul(w[1], slopes[0]), mul(w[2], slopes[1]))
    return sub(mid, change)


def backward(mid, flux_inner, flux_outer, wy, wx, toward=1, active=None):
    change = add(dz(flux_inner, flux_outer, toward), dy(mul(wy, mid)), dx(mul(wx, mid)))
    return add(mid, change if active is None else scale(change, active))


def grads(adj, mid, inner, outer, toward=1, slopes=None):
    sy, sx = slopes or (dy(mid), dx(mid))
    return [mul(adj, dz(inner, outer, toward)), mul(adj, sy), mul(adj, sx)]


def natural(odd, j):
    return j + odd * (7 - 2 * j)


def unrolled(low, high, step):
    for j in range(low, high):
        step(j, 0)


ROLES = (0, 1)
TOWARD = (1, -1)


def t_load(t, k, role=0):
    return load(t, 2 + k if role == 0 else 9 - k)


def t_slopes(dt, k, role=0):
    return [load(dt, c, 1 + k if role == 0 else 8 - k) for c in (0, 1)]


def template_planes(info, s, *refs):
    *sources, t, dt = refs
    odd, me = info[4], info[6]

    @pl.when(s == 0)
    def _():
        for j in range(-2, 10):
            at = 2 + natural(odd, j)
            if j < 0:
                at = 1 - odd if j == -1 else odd
            if j > 7:
                at = 10 + odd if j == 8 else 11 - odd
            for i, source in enumerate(sources):
                for x in (0, 1):
                    row = pl.multiple_of(8 * jnp.bitwise_xor(me, 2 * i + x), 8)
                    t[j + 2, pl.ds(row, 8)] = source[x, at]
        for j in range(-1, 9):
            mid = load(t, j + 2)
            store_all([(dt, dy(mid), (0, j + 1)), (dt, dx(mid), (1, j + 1))])


def velocity_inner(info, s, m, w_in, w_edge, m_edge):
    odd = info[4]
    sign = (1 - 2 * odd).astype(f32)
    for j in range(8):
        for c in range(3):
            turn = sign if c == 0 else 1.0
            v = smooth(
                load(m, 0, c, natural(odd, j)),
                load(m, 0, c, natural(odd, j + 1)) if j < 7 else None,
                load(m, 0, c, natural(odd, j - 1)) if j > 0 else None,
                half * centre * turn,
                half * smoothing * turn,
            )
            if 0 < j < 7:
                store(w_in, v, 0, c, j - 1)
            else:
                store(w_edge, v, 0, c, j // 7)
                m_edge[0, c, j // 7] = m[0, c, natural(odd, j)]


def inner_1(info, s, w_in, t, dt, i1_in, i2_in):
    def first(j, _):
        w = [load(w_in, 0, c, j - 1) for c in range(3)]
        image = forward_by(t_load(t, j), t_load(t, j + 1), t_load(t, j - 1), t_slopes(dt, j), w)
        store(i1_in, image, 0, j - 1)
        return 0

    unrolled(1, 7, first)

    @pl.when(info[s] > 1)
    def _():
        def second(j, _):
            at = lambda i: load(i1_in, 0, i - 1)
            w = [load(w_in, 0, c, j - 1) for c in range(3)]
            store(i2_in, forward(at(j), at(j + 1), at(j - 1), w), 0, j - 2)
            return 0

        unrolled(2, 6, second)

    @pl.when(info[s] <= 1)
    def _():
        i2_in[0] = i1_in[0, 1:5]


def outer_1(info, s, *refs):
    mr, m_edge, w_edge, t, dt, wp, i1p = refs[0:2], *refs[2:6], refs[6:8], refs[8:10]
    w_out, i1_out, send = refs[10:12], refs[12:14], refs[14:16]
    odd = info[4]
    sign = (1 - 2 * odd).astype(f32)
    for r in ROLES:
        to = TOWARD[r]
        h1 = 1 - odd if r == 0 else odd
        inside = info[5].astype(f32) if r == 0 else 1.0
        wh, w0 = [], []
        for c in range(3):
            turn = sign if c == 0 else 1.0
            m_h1, m_p0 = load(mr[r], 0, c, h1), load(m_edge, 0, c, r)
            a, b = half * centre * turn, half * smoothing * turn
            wh.append(smooth(m_h1, m_p0, load(mr[r], 0, c, 1 - h1), a * inside, b * inside))
            w0.append(add(load(w_edge, 0, c, r), scale(m_h1, b)))
        at = lambda k: t_load(t, k, r)
        i_h1 = forward_by(at(-1), at(0), at(-2), t_slopes(dt, -1, r), wh, to)
        i_p0 = forward_by(at(0), at(1), at(-1), t_slopes(dt, 0, r), w0, to)
        targets = [(i1_out[r], i_h1, (0, 0)), (i1_out[r], i_p0, (0, 1))]
        targets += [(w_out[r], w[c], (0, c, i)) for i, w in enumerate((wh, w0)) for c in range(3)]
        store_all(targets)

    @pl.when(info[s] > 1)
    def _():
        for r in ROLES:
            to, near, far = TOWARD[r], r, 1 - r
            i_h1, i_p0 = load(i1_out[r], 0, 0), load(i1_out[r], 0, 1)
            i_p1, i_p2 = load(i1p[r], 0, near), load(i1p[r], 0, far)
            w0 = [load(w_out[r], 0, c, 1) for c in range(3)]
            w1 = [load(wp[r], 0, c, near) for c in range(3)]
            store(send[r], forward(i_p0, i_p1, i_h1, w0, to), 0, 0)
            store(send[r], forward(i_p1, i_p2, i_p0, w1, to), 0, 1)

    @pl.when(info[s] <= 1)
    def _():
        for r in ROLES:
            send[r][0, 0] = i1_out[r][0, 1]
            send[r][0, 1] = i1p[r][0, r]


def gather_planes(x, sides, inner):
    x[0] = sides[0][0, 0]
    x[1] = sides[0][0, 1]
    x[7] = sides[1][0, 0]
    x[6] = sides[1][0, 1]
    x[2:6] = inner[0]


def inner_2(info, s, w_in, i2_in, s1z, s1c, targets, i3_in, i4_in, a4_in, x):
    odd = info[4]
    gather_planes(x, (s1z, s1c), i2_in)

    @pl.when(info[s] > 2)
    def _():
        def step(j, _):
            w = [load(w_in, 0, c, j - 1) for c in range(3)]
            store(i3_in, forward(load(x, j), load(x, j + 1), load(x, j - 1), w), 0, j - 1)
            return 0

        unrolled(1, 7, step)

    @pl.when(info[s] <= 2)
    def _():
        i3_in[0] = x[1:7]

    @pl.when(info[s] > 3)
    def _():
        def step(j, _):
            at = lambda i: load(i3_in, 0, i - 1)
            w = [load(w_in, 0, c, j - 1) for c in range(3)]
            image = forward(at(j), at(j + 1), at(j - 1), w)
            late = sub(image, load(targets, 0, natural(odd, j)))
            store_all([(i4_in, image, (0, j - 2)), (a4_in, late, (0, j - 2))])
            return 0

        unrolled(2, 6, step)

    @pl.when(info[s] <= 3)
    def _():
        def step(j, _):
            image = load(i3_in, 0, j - 1)
            late = sub(image, load(targets, 0, natural(odd, j)))
            store_all([(i4_in, image, (0, j - 2)), (a4_in, late, (0, j - 2))])
            return 0

        unrolled(2, 6, step)


def outer_2(info, s, *refs):
    r1, wb, wp, s1, i3p = (refs[2 * i : 2 * i + 2] for i in range(5))
    targets = refs[10]
    i3_out, i4_out, a4_out, send = (refs[11 + 2 * i : 13 + 2 * i] for i in range(4))
    odd = info[4]

    @pl.when(info[s] > 2)
    def _():
        for r in ROLES:
            i_h1, i_h2 = load(r1[r], 0, 0), load(r1[r], 0, 1)
            i_p0, i_p1 = load(s1[r], 0, 0), load(s1[r], 0, 1)
            wh = [load(wb[r], 0, c, 0) for c in range(3)]
            w0 = [load(wb[r], 0, c, 1) for c in range(3)]
            store(i3_out[r], forward(i_h1, i_p0, i_h2, wh, TOWARD[r]), 0, 0)
            store(i3_out[r], forward(i_p0, i_p1, i_h1, w0, TOWARD[r]), 0, 1)

    @pl.when(info[s] <= 2)
    def _():
        for r in ROLES:
            i3_out[r][0, 0] = r1[r][0, 0]
            i3_out[r][0, 1] = s1[r][0, 0]

    def late(r, i4_p0, i4_p1):
        n = [natural(odd, k if r == 0 else 7 - k) for k in (0, 1)]
        a_p0, a_p1 = sub(i4_p0, load(targets, 0, n[0])), sub(i4_p1, load(targets, 0, n[1]))
        store_all([(i4_out[r], i4_p0, (0, 0)), (send[r], a_p0, (0, 0))])
        f_p1 = mul(load(wp[r], 0, 0, r), a_p1)
        store_all([(i4_out[r], i4_p1, (0, 1)), (a4_out[r], a_p1, (0, 0)), (send[r], f_p1, (0, 1))])

    @pl.when(info[s] > 3)
    def _():
        for r in ROLES:
            to, near, far = TOWARD[r], r, 1 - r
            i_h1, i_p0 = load(i3_out[r], 0, 0), load(i3_out[r], 0, 1)
            i_p1, i_p2 = load(i3p[r], 0, near), load(i3p[r], 0, far)
            w0 = [load(wb[r], 0, c, 1) for c in range(3)]
            w1 = [load(wp[r], 0, c, near) for c in range(3)]
            late(r, forward(i_p0, i_p1, i_h1, w0, to), forward(i_p1, i_p2, i_p0, w1, to))

    @pl.when(info[s] <= 3)
    def _():
        for r in ROLES:
            late(r, load(i3_out[r], 0, 1), load(i3p[r], 0, r))


def inner_3(info, s, *refs):
    w_in, wbz, wbc, s2z, s2c, a4z, a4c, a4_in, i3_in, i3z, i3c, i2_in, s1z, s1c, i1_in, i4_in, i4z, i4c = refs[:18]
    a3_in, a2_in, g_in, warped, a, f, x, sems = refs[18:]
    odd = info[4]

    def copies():
        def one(source, j):
            return pltpu.make_async_copy(source, warped.at[s, natural(odd, j)], sems.at[j])

        pairs = [(i4z.at[0, 0], 0), (i4z.at[0, 1], 1), (i4c.at[0, 1], 6), (i4c.at[0, 0], 7)]
        pairs += [(i4_in.at[0, j - 2], j) for j in range(2, 6)]
        return [one(source, j) for source, j in pairs]

    for copy in copies():
        copy.start()
    a[0], a[7] = s2z[0, 0], s2c[0, 0]
    a[1], a[6] = a4z[0, 0], a4c[0, 0]
    a[2:6] = a4_in[0]

    @pl.when(info[s] > 3)
    def _():
        x[0], x[7] = i3z[0, 1], i3c[0, 1]
        x[1:7] = i3_in[0]
        f[0] = wbz[0, 0, 1] * a[0]
        f[7] = wbc[0, 0, 1] * a[7]
        f[1:7] = w_in[0, 0] * a[1:7]

        def step(j, _):
            mid = load(a, j)
            wy, wx = (load(w_in, 0, c, j - 1) for c in (1, 2))
            adj = backward(mid, load(f, j + 1), load(f, j - 1), wy, wx)
            g = grads(mid, load(x, j), load(x, j + 1), load(x, j - 1))
            store_all([(a3_in, adj, (0, j - 1))] + [(g_in, g[c], (0, c, j - 1)) for c in range(3)])
            return 0

        unrolled(1, 7, step)

    @pl.when(info[s] <= 3)
    def _():
        a3_in[0] = a[1:7]
        g_in[...] = jnp.zeros(g_in.shape, f32)

    @pl.when(info[s] > 2)
    def _():
        gather_planes(x, (s1z, s1c), i2_in)
        f[1:7] = w_in[0, 0] * a3_in[0]

        def gradient(j, adj):
            g = grads(adj, load(x, j), load(x, j + 1), load(x, j - 1))
            return [(g_in, add(load(g_in, 0, c, j - 1), g[c]), (0, c, j - 1)) for c in range(3)]

        def end(i, _):
            j = 1 + 5 * i
            store_all(gradient(j, load(a3_in, 0, j - 1)))
            return 0

        unrolled(0, 2, end)

        def step(j, _):
            mid = load(a3_in, 0, j - 1)
            wy, wx = (load(w_in, 0, c, j - 1) for c in (1, 2))
            adj = backward(mid, load(f, j + 1), load(f, j - 1), wy, wx)
            store_all([(a2_in, adj, (0, j - 2))] + gradient(j, mid))
            return 0

        unrolled(2, 6, step)

    @pl.when(info[s] <= 2)
    def _():
        a2_in[0] = a3_in[0, 1:5]

    @pl.when(info[s] > 1)
    def _():
        def step(j, _):
            at = lambda i: load(i1_in, 0, i - 1)
            g = grads(load(a2_in, 0, j - 2), at(j), at(j + 1), at(j - 1))
            store_all([(g_in, add(load(g_in, 0, c, j - 1), g[c]), (0, c, j - 1)) for c in range(3)])
            return 0

        unrolled(2, 6, step)

    for copy in copies():
        copy.wait()


def outer_3(info, s, *refs):
    r2, wb, wp, s2, a3p, i3b, i3p, r1, s1, i1b, i1p = (refs[2 * i : 2 * i + 2] for i in range(11))
    a3, a2_out, send = (refs[22 + 2 * i : 24 + 2 * i] for i in range(3))

    def gz(r, adj, inner, outer):
        return (send[r], add(load(send[r], 0, 2), mul(adj, dz(inner, outer, TOWARD[r]))), (0, 2))


    @pl.when(info[s] > 3)
    def _():
        for r in ROLES:
            to = TOWARD[r]
            a_h1, a_p0 = load(r2[r], 0, 0), load(s2[r], 0, 0)
            f_h2, f_p1 = scale(load(r2[r], 0, 1), -1.0), load(s2[r], 0, 1)
            wh = [load(wb[r], 0, c, 0) for c in range(3)]
            w0 = [load(wb[r], 0, c, 1) for c in range(3)]
            store(a3[r], backward(a_h1, mul(w0[0], a_p0), f_h2, wh[1], wh[2], to), 0, 0)
            b_p0 = backward(a_p0, f_p1, mul(wh[0], a_h1), w0[1], w0[2], to)
            g = mul(a_p0, dz(load(i3p[r], 0, r), load(i3b[r], 0, 0), to))
            store_all([(a3[r], b_p0, (0, 1)), (send[r], g, (0, 2))])

    @pl.when(info[s] <= 3)
    def _():
        for r in ROLES:
            a3[r][0, 0] = r2[r][0, 0]
            a3[r][0, 1] = s2[r][0, 0]
            send[r][0, 2] = jnp.zeros(send[r].shape[2:], f32)

    def late(r, a2_p0, a2_p1):
        f_p1 = mul(load(wp[r], 0, 0, r), a2_p1)
        store_all([(a2_out[r], a2_p0, (0, 0)), (send[r], a2_p0, (0, 0))])
        store_all([(a2_out[r], a2_p1, (0, 1)), (send[r], f_p1, (0, 1))])

    @pl.when(info[s] > 2)
    def _():
        for r in ROLES:
            to, near, far = TOWARD[r], r, 1 - r
            a_h1, a_p0 = load(a3[r], 0, 0), load(a3[r], 0, 1)
            a_p1, a_p2 = load(a3p[r], 0, near), load(a3p[r], 0, far)
            wh0 = load(wb[r], 0, 0, 0)
            w0 = [load(wb[r], 0, c, 1) for c in range(3)]
            w1 = [load(wp[r], 0, c, near) for c in range(3)]
            f_p2 = mul(load(wp[r], 0, 0, far), a_p2)
            store_all([gz(r, a_p0, load(s1[r], 0, 1), load(r1[r], 0, 0))])
            late(
                r,
                backward(a_p0, mul(w1[0], a_p1), mul(wh0, a_h1), w0[1], w0[2], to),
                backward(a_p1, f_p2, mul(w0[0], a_p0), w1[1], w1[2], to),
            )

    @pl.when(info[s] <= 2)
    def _():
        for r in ROLES:
            late(r, load(a3[r], 0, 1), load(a3p[r], 0, r))

    @pl.when(info[s] > 1)
    def _():
        for r in ROLES:
            store_all([gz(r, load(a2_out[r], 0, 0), load(i1p[r], 0, r), load(i1b[r], 0, 0))])


def inner_4(info, s, *refs):
    w_in, wbz, wbc, a2_in, a2z, a2c, *rest, a1_in, total, g_full, gbz, gbc, a, f = refs
    gather_planes(a, (a2z, a2c), a2_in)

    @pl.when(s == 0)
    def _():
        total[...] = jnp.zeros(total.shape, f32)

    @pl.when(info[s] > 1)
    def _():
        f[0] = wbz[0, 0, 1] * a[0]
        f[7] = wbc[0, 0, 1] * a[7]
        f[1:7] = w_in[0, 0] * a[1:7]

        def step(j, _):
            mid = load(a, j)
            wy, wx = (load(w_in, 0, c, j - 1) for c in (1, 2))
            store(a1_in, backward(mid, load(f, j + 1), load(f, j - 1), wy, wx), 0, j - 1)
            return 0

        unrolled(1, 7, step)

    @pl.when(info[s] <= 1)
    def _():
        a1_in[0] = a[1:7]

    f[1:7] = w_in[0, 0] * a1_in[0]

    def last(j, _):
        mid = load(a1_in, 0, j - 1)
        wy, wx = (load(w_in, 0, c, j - 1) for c in (1, 2))
        adj = backward(mid, load(f, j + 1), load(f, j - 1), wy, wx)
        add_t(total, adj, j - 2)
        return 0

    unrolled(2, 6, last)
    r2, a3, s2, s3, i3b, i3p, r1, s1, i1b, i1p = (rest[2 * i : 2 * i + 2] for i in range(10))
    t, dt, g_in = rest[20:23]
    a2b, gb = (a2z, a2c), (gbz, gbc)

    def step(j, _):
        adj = load(a1_in, 0, j - 1)
        g = grads(adj, None, t_load(t, j + 1), t_load(t, j - 1), slopes=t_slopes(dt, j))
        store_all([(g_full, add(load(g_in, 0, c, j - 1), g[c]), (0, c, j - 1)) for c in range(3)])
        return 0

    unrolled(1, 7, step)
    for r in ROLES:
        to, near, far = TOWARD[r], r, 1 - r
        p1 = 0 if r == 0 else 5
        g = gb[r]

        def more(plane, parts, first=False):
            values = [(g, value if first else add(load(g, 0, c, plane), value), (0, c, plane)) for c, value in parts]
            store_all(values)

        def at_h1(adj, image):
            return [(1, mul(adj, dy(image))), (2, mul(adj, dx(image)))]

        def at_p0(adj, *images):
            return list(enumerate(grads(adj, *images, to)))[1:]

        @pl.when(info[s] > 3)
        def _():
            i_h1, i_p0 = load(i3b[r], 0, 0), load(i3b[r], 0, 1)
            more(0, at_h1(load(r2[r], 0, 0), i_h1), True)
            more(1, at_p0(load(s2[r], 0, 0), i_p0, load(i3p[r], 0, near), i_h1), True)

        @pl.when(info[s] <= 3)
        def _():
            g[...] = jnp.zeros(g.shape, f32)

        @pl.when(info[s] > 2)
        def _():
            i_h1, i_p0 = load(r1[r], 0, 0), load(s1[r], 0, 0)
            more(0, at_h1(load(a3[r], 0, 0), i_h1))
            more(1, at_p0(load(a3[r], 0, 1), i_p0, load(s1[r], 0, 1), i_h1))

        @pl.when(info[s] > 1)
        def _():
            i_h1, i_p0 = load(i1b[r], 0, 0), load(i1b[r], 0, 1)
            i_p1, i_p2 = load(i1p[r], 0, near), load(i1p[r], 0, far)
            more(1, at_p0(load(a2b[r], 0, 0), i_p0, i_p1, i_h1))
            g1 = grads(load(a2b[r], 0, 1), i_p1, i_p2, i_p0, to)
            store_all([(g_full, add(load(g_full, 0, c, p1), g1[c]), (0, c, p1)) for c in range(3)])

        g[0, 0, 1] = s3[r][0, 2]


def outer_4(info, s, *refs):
    r3, wb, wp, s3, a1p = (refs[2 * i : 2 * i + 2] for i in range(5))
    total_in, total_out, *outs = refs[10:14]
    total, a1s, sems = refs[14:]
    odd = info[4]

    def sent(r):
        return pltpu.make_async_copy(a1s.at[s, r], outs[r].at[s], sems.at[s, r])

    @pl.when(s == 0)
    def _():
        for j in range(2, 6):
            total[:, natural(odd, j)] = total_in[:, j - 2]
        for j in (0, 1, 6, 7):
            total[:, j] = jnp.zeros((8, 8, COLS), f32)

    for r in ROLES:
        to, near, far = TOWARD[r], r, 1 - r

        active = (info[s] > 1).astype(f32)
        a_h1, a_p0 = load(r3[r], 0, 0), load(s3[r], 0, 0)
        f_h2, f_p1 = scale(load(r3[r], 0, 1), -1.0), load(s3[r], 0, 1)
        wh = [load(wb[r], 0, c, 0) for c in range(3)]
        w0 = [load(wb[r], 0, c, 1) for c in range(3)]
        b_h1 = backward(a_h1, mul(w0[0], a_p0), f_h2, wh[1], wh[2], to, active)
        b_p0 = backward(a_p0, f_p1, mul(wh[0], a_h1), w0[1], w0[2], to, active)
        store_all([(a1s, b_h1, (s, r, 0)), (a1s, b_p0, (s, r, 1))])
        w1 = [load(wp[r], 0, c, near) for c in range(3)]
        b_p1, b_p2 = load(a1p[r], 0, near), load(a1p[r], 0, far)
        c_p0 = backward(b_p0, mul(w1[0], b_p1), mul(wh[0], b_h1), w0[1], w0[2], to)
        c_p1 = backward(b_p1, mul(load(wp[r], 0, 0, far), b_p2), mul(w0[0], b_p0), w1[1], w1[2], to)
        for k, value in enumerate((c_p0, c_p1)):
            add_t(total, value, natural(odd, k if r == 0 else 7 - k))
        sent(r).start()

    @pl.when(s == 3)
    def _():
        last = pltpu.make_async_copy(total, total_out, sems.at[4, 0])
        last.start()
        for at in range(4):
            for r in ROLES:
                pltpu.make_async_copy(a1s.at[at, r], outs[r].at[at], sems.at[at, r]).wait()
        last.wait()


def final(mid, inner, outer, turn):
    return smooth(mid, inner, outer, -half * centre * turn, -half * smoothing * turn)


def finish(info, s, *refs):
    r3, a1b, gb, i1b = (refs[2 * i : 2 * i + 2] for i in range(4))
    t, dt, g_full, mg, made, sems = refs[8:]
    odd = info[4]
    sign = (1 - 2 * odd).astype(f32)
    slot = lax.rem(s, 2)

    def copy_out(which, at):
        return pltpu.make_async_copy(made.at[which], mg.at[at], sems.at[which])

    @pl.when(s >= 2)
    def _():
        copy_out(slot, s - 2).wait()

    def step(j, _):
        for c in range(3):
            at = lambda i: load(g_full, 0, c, i - 1)
            store(made, final(at(j), at(j + 1), at(j - 1), sign if c == 0 else 1.0), slot, c, natural(odd, j))
        return 0

    unrolled(2, 6, step)
    for r in ROLES:
        to = TOWARD[r]
        p1, p2 = (0, 1) if r == 0 else (5, 4)
        n0, n1 = (natural(odd, k if r == 0 else 7 - k) for k in (0, 1))
        inside = info[5].astype(f32) if r == 0 else 1.0
        step_one = (info[s] > 1).astype(f32)
        th2, th1, tp0, tp1 = (t_load(t, k, r) for k in (-2, -1, 0, 1))
        slopes = t_slopes(dt, -1, r)
        a_one = scale(load(r3[r], 0, 0), step_one)
        i_h1 = load(i1b[r], 0, 0)
        b_h1, b_p0 = load(a1b[r], 0, 0), load(a1b[r], 0, 1)
        g_h1 = [
            add(scale(load(r3[r], 0, 2), -1.0), mul(b_h1, dz(tp0, th2, to))),
            add(load(gb[r], 0, 1, 0), mul(a_one, dy(i_h1)), mul(b_h1, slopes[0])),
            add(load(gb[r], 0, 2, 0), mul(a_one, dx(i_h1)), mul(b_h1, slopes[1])),
        ]
        g_p0 = grads(b_p0, tp0, tp1, th1, to, t_slopes(dt, 0, r))
        for c in range(3):
            turn = sign if c == 0 else 1.0
            g0 = add(load(gb[r], 0, c, 1), g_p0[c])
            g1, g2 = load(g_full, 0, c, p1), load(g_full, 0, c, p2)
            store(made, final(g0, g1, scale(g_h1[c], inside), turn), slot, c, n0)
            store(made, final(g1, g2, g0, turn), slot, c, n1)

    copy_out(slot, s).start()

    @pl.when(s == 3)
    def _():
        copy_out(1 - slot, s - 1).wait()
        copy_out(slot, s).wait()


ROWS, COLS = 64, 256
PLANE = (ROWS, COLS)


def one(ref, s):
    return ref.at[pl.ds(s, 1)]


def whole(ref, s):
    return ref


def stream(ref, s):
    return ref


def flows(view):
    return view is stream or getattr(view, "streamed", False)


def pair(at, streamed=False):
    def view(ref, s):
        subject = pl.ds(0 if streamed else s, 1)
        if len(ref.shape) == 5:
            return ref.at[subject, :, pl.ds(at, 2)]
        return ref.at[subject, pl.ds(at, 2)]

    view.streamed = streamed
    return view


def call(kernel, info, ins, outs, scratch=(), us=1.0, mib=5):
    arrays, places = [], []
    streams = any(flows(view) for _, view in list(ins) + list(outs))
    for array, _ in ins:
        known = [i for i, other in enumerate(arrays) if other is array]
        if not known:
            arrays.append(array)
        places.append(known[0] if known else len(arrays) - 1)
    subjects = 4

    def body(info_ref, *refs):
        given, made = refs[: len(arrays)], refs[len(arrays) : len(arrays) + len(outs)]

        def per(s, _):
            views = [view(given[at], s) for at, (_, view) in zip(places, ins)]
            views += [view(ref, s) if view else ref for ref, (_, view) in zip(made, outs)]
            kernel(info_ref, s, *views, *refs[len(arrays) + len(outs) :])
            return 0

        if streams:
            per(pl.program_id(0), 0)
        else:
            lax.fori_loop(0, subjects, per, 0)

    vmem = pl.BlockSpec(memory_space=pltpu.VMEM)

    def block(dims):
        return pl.BlockSpec((1,) + dims[1:], lambda s: (s,) + (0,) * (len(dims) - 1))

    def made_of(dims, view):
        if view is stream:
            return block(dims), pltpu.HBM(dims, f32)
        if view is None:
            return pl.BlockSpec(memory_space=pl.ANY), pltpu.HBM(dims, f32)
        return vmem, jax.ShapeDtypeStruct(dims, f32)

    streamed = [any(flows(view) for other, view in ins if other is array) for array in arrays]
    operands = [pltpu.with_memory_space_constraint(a, pltpu.HBM) if st else a for a, st in zip(arrays, streamed)]
    out_specs, out_shapes = zip(*(made_of(*o) for o in outs))

    return pl.pallas_call(
        body,
        grid=(subjects,) if streams else (),
        in_specs=[pl.BlockSpec(memory_space=pltpu.SMEM)] + [block(a.shape) if st else vmem for a, st in zip(arrays, streamed)],
        out_specs=list(out_specs),
        out_shape=list(out_shapes),
        scratch_shapes=list(scratch),
        compiler_params=pltpu.CompilerParams(vmem_limit_bytes=mib * 1024 * 1024),
        cost_estimate=pl.CostEstimate(flops=0, bytes_accessed=int(us * 3.3e6), transcendentals=0),
        name=kernel.__name__,
    )(info, *operands)


def shards(template, momentum, targets, step_count):
    count = lax.axis_size("space")
    groups = lax.axis_size("subj")
    place = lax.axis_index("space")
    odd = place % 2
    core_pairs = [(i, i ^ 1) for i in range(count)]
    chip_pairs = [(i, ((i + 1) ^ 1) - 1) for i in range(1, count - 1)]

    def swap(sides):
        return lax.ppermute(sides[0], "space", chip_pairs), lax.ppermute(sides[1], "space", core_pairs)

    group = lax.axis_index("subj")
    inside = jnp.logical_and(place > 0, place < count - 1)
    info = jnp.concatenate([step_count, jnp.stack([odd, inside, group]).astype(jnp.int32)])

    def ends(array, dim):
        return tuple(lax.dynamic_slice_in_dim(array, at, 2, dim) for at in (6 * odd, 6 - 6 * odd))

    def shape(*lead):
        return (step_count.shape[0],) + lead + PLANE

    def both(arrays, *views):
        return [(arrays[0], views[0]), (arrays[1], views[-1])]

    def near(array, streamed=False):
        return both((array, array), pair(0, streamed), pair(4, streamed))

    def out(*lead):
        return (shape(*lead), one)

    def out2(*lead):
        return [out(*lead)] * 2

    def planes(n):
        return pltpu.VMEM((n,) + PLANE, f32)

    def partner(array, by):
        return lax.ppermute(array, "subj", [(i, i ^ by) for i in range(groups)])

    across, ms = lax.optimization_barrier((partner(template, 1), ends(momentum, 2)))
    own = jnp.stack([template, across])
    t_halo, ms = lax.optimization_barrier((swap(ends(own, 1)), ms))
    mr = swap(ms)
    wide = jnp.concatenate([t_halo[0], own, t_halo[1]], axis=1)
    wide, late_info = lax.optimization_barrier((wide, info))
    rows = [wide] + [partner(wide, by) for by in (2, 4, 6)]
    w_in, w_edge, m_edge = call(
        velocity_inner, late_info, [(momentum, stream)], [out(3, 6), out(3, 2), out(3, 2)], us=5
    )
    t, dt = call(
        template_planes, info, [(x, whole) for x in rows], [((12,) + PLANE, whole), ((2, 10) + PLANE, whole)], us=1
    )
    tdt = [(t, whole), (dt, whole)]
    i1_in, i2_in = call(inner_1, info, [(w_in, one)] + tdt, [out(6), out(4)], us=3)
    *made, s1z, s1c = call(
        outer_1,
        info,
        both(mr, stream) + [(m_edge, one), (w_edge, one)] + tdt + near(w_in) + near(i1_in),
        out2(3, 2) + out2(2) + out2(2),
        us=5,
    )
    wb, i1b = made[:2], made[2:]
    s1 = (s1z, s1c)
    r1 = swap(s1)
    i3_in, i4_in, a4_in = call(
        inner_2,
        info,
        [(w_in, one), (i2_in, one)] + both(s1, one) + [(targets, one)],
        [out(6), out(4), out(4)],
        [planes(8)],
        us=4,
    )
    made = call(
        outer_2,
        info,
        both(r1, one) + both(wb, one) + near(w_in) + both(s1, one) + near(i3_in) + [(targets, one)],
        out2(2) + out2(2) + out2(1) + out2(2),
        us=3,
    )
    i3b, i4b, a4b, s2 = (made[2 * i : 2 * i + 2] for i in range(4))
    r2 = swap(s2)
    a3_in, a2_in, g_in, warped = call(
        inner_3,
        info,
        [(w_in, one)]
        + both(wb, one)
        + both(s2, one)
        + both(a4b, one)
        + [(a4_in, one), (i3_in, one)]
        + both(i3b, one)
        + [(i2_in, one)]
        + both(s1, one)
        + [(i1_in, one), (i4_in, one)]
        + both(i4b, one),
        [out(6), out(4), out(3, 6), (shape(8), None)],
        [planes(8)] * 3 + [pltpu.SemaphoreType.DMA((8,))],
        us=7,
    )
    images = both(i3b, one) + near(i3_in) + both(r1, one) + both(s1, one) + both(i1b, one) + near(i1_in)
    made = call(
        outer_3,
        info,
        both(r2, one) + both(wb, one) + near(w_in) + both(s2, one) + near(a3_in) + images,
        out2(2) + out2(2) + out2(3),
        us=2,
    )
    a3b, a2b, s3 = (made[2 * i : 2 * i + 2] for i in range(3))
    r3 = swap(s3)
    small, tile = (groups, 4, 8, COLS), (groups, 8, 8, COLS)
    a1_in, total, g_full, *gb = call(
        inner_4,
        info,
        [(w_in, one)]
        + both(wb, one)
        + [(a2_in, one)]
        + both(a2b, one)
        + both(r2, one)
        + both(a3b, one)
        + both(s2, one)
        + both(s3, one)
        + images
        + tdt
        + [(g_in, one)],
        [out(6), (small, whole), out(3, 6)] + out2(3, 2),
        [planes(8)] * 2,
        us=5,
    )
    total, *a1b = call(
        outer_4,
        info,
        both(r3, one) + both(wb, one) + near(w_in) + both(s3, one) + near(a1_in) + [(total, whole)],
        [(tile, None)] + [(shape(2), None)] * 2,
        [pltpu.VMEM(tile, f32), pltpu.VMEM((4, 2, 2) + PLANE, f32), pltpu.SemaphoreType.DMA((5, 2))],
        us=3,
    )
    parts = lax.all_to_all(total, "subj", 0, 0)
    (momentum_gradient,) = call(
        finish,
        info,
        both(r3, stream) + both(a1b, stream) + both(gb, stream) + both(i1b, stream) + tdt + [(g_full, stream)],
        [(shape(3, 8), None)],
        [pltpu.VMEM((2, 3, 8) + PLANE, f32), pltpu.SemaphoreType.DMA((2,))],
        us=6,
        mib=14,
    )
    template_gradient = jnp.sum(parts, axis=0)
    return (warped, template_gradient, momentum_gradient)


def solution(mesh):
    in_specs = (
        P("space", "subj", None),
        P("subj", None, "space", None, None),
        P("subj", "space", None, None),
        P("subj"),
    )
    out_specs = (
        P("subj", "space", None, None),
        P("space", "subj", None),
        P("subj", None, "space", None, None),
    )
    return jax.shard_map(shards, mesh=mesh, in_specs=in_specs, out_specs=out_specs, check_vma=False)
```

time: 352 us -> 108 us (0.31); the launches traced: 348 us -> 108 us
  other arithmetic: 93.6 us -> 0.76 us
  waiting for transfers between devices: 99.6 us -> 20.6 us
  blocking collectives: 42.4 us -> 0 us
  Pallas kernels: 0 us -> 36.1 us
  starting transfers between devices: 78.2 us -> 44.1 us
  local copies, waits for them, and re-layouts: 19.2 us -> 5.16 us
  between operations: 14.7 us -> 0.93 us
    psum x1 -> x0, waiting for transfers between devices: 81.3 us -> none  [shards(): total = lax.psum(local_sum, 'subj')]
    ppermute x20 -> x14, starting transfers between devices: 78.2 us -> 35.4 us  [the longest x5 29.3 us: swap(): lax.ppermute(sides[0], 'space', chip_pairs)]
    all_gather x1 -> x0, blocking collectives: 42.4 us -> none  [shards(): whole_tmpl = lax.all_gather(template, 'subj', axis=1, tiled=True)]
    add x2 -> x0, other arithmetic: 39.5 us -> none  [rim_kernel(): return center + smoothing * (nsum - 6.0 * center)]
    pallas_call x0 -> x11, Pallas kernels: none -> 36.1 us  [call(): pl.pallas_call(body, grid=(subjects,) if streams else (), in_specs=[pl.Bl...]
    another operation x3 -> x1, other arithmetic: 31.1 us -> 0.01 us  [shards(): own = jnp.stack([template, across])]
    mul x7 -> x0, other arithmetic: 11.8 us -> none  [the longest x3 7.81 us: shards(): padded_flux = with_halo(vel_z * adjoint, (('space', 1),), 1)]
    unnamed x57 -> x20, local copies, waits for them, and re-layouts: 11.7 us -> 1.23 us
  transfers between devices with their start and end apart: 21 -> 15, of which waited for: 12 -> 8; matrix products, arithmetic and copies ran while one was open for 11% -> 4% of each run, Pallas kernels for 0% -> 25%
where the time goes in v2:
time: 108 us
  starting transfers between devices  44.1 us (41%)
  Pallas kernels  36.1 us (33%)
  waiting for transfers between devices  20.6 us (19%)
  local copies, waits for them, and re-layouts  5.16 us (5%)
    pallas_call x11, Pallas kernels, call(): pl.pallas_call(body, grid=(subjects,) if streams else (), in_specs=[pl.Bl...  36.1 us
    ppermute x5, starting transfers between devices, swap(): lax.ppermute(sides[0], 'space', chip_pairs)  29.3 us
    ppermute x5, waiting for transfers between devices, swap(): lax.ppermute(sides[0], 'space', chip_pairs)  16.2 us
    all_to_all x1, starting transfers between devices, shards(): parts = lax.all_to_all(total, 'subj', 0, 0)  8.67 us
    ppermute x4, starting transfers between devices, partner(): return lax.ppermute(array, 'subj', [(i, i ^ by) for i in range(groups)])  5.66 us
    ppermute x4, waiting for transfers between devices, partner(): return lax.ppermute(array, 'subj', [(i, i ^ by) for i in range(groups)])  4.34 us
    dynamic_slice x1, local copies, waits for them, and re-layouts, ends(): lax.dynamic_slice_in_dim(array, at, 2, dim)  3.93 us
  transfers between devices with their start and end apart: 15, of which 8 were waited for; matrix products, arithmetic and copies ran while one was open for 4% of the time, Pallas kernels for 25%

profile of v2, /device:TPU:6, one launch (start us, length us, event | category | flops | bytes accessed | tf_op | source)
XLA Modules:
  0.0 107.6 jit_solution(12109346355029203978)
XLA Ops:
  0.6 1.5 %collective-permute-start = (f32[8,8,256]{2,1,0:T(8,128)}, f32[8,8,256]{2,1,0:T(8,128)S(1)}, u32[]{:S(2)}, u32[]{:S(2)}) collective-permute-start(f32[8,8,256]{2,1,0:T(8,128)} %param.4), channel_id=1, source_target_pairs={{0,1},{1,0},{2,3},{3,2},{4,5},{5,4},{6,7},{7,6},{8,9},{9,8},{10,11... | collective-permute-start | bytes 196616 | tf_op jit(solution)/shard_map/ppermute | solution.py:822
  2.1 3.9 %constant_dynamic-slice_fusion = (f32[4,3,2,64,256]{4,3,2,1,0:T(8,128)}, f32[4,3,2,64,256]{4,3,2,1,0:T(8,128)}) fusion(f32[4,3,8,64,256]{4,3,2,1,0:T(8,128)} %refs_0_.1, s32[]{:T(128)S(6)} %select_n.17, s32[]{:T(128)S(6)} %select_n.16), kind=kLoop, calls=%fused_computation.7 | loop fusion | bytes 6291464 | tf_op jit(solution)/shard_map/dynamic_slice | solution.py:801
  6.0 0.6 collective-permute-done
  6.7 0.0 copy-done.8
  6.7 0.1 collective-permute-start.2
  6.8 6.3 %collective-permute-start.1 = (f32[2,2,8,256]{3,2,1,0:T(8,128)S(1)}, f32[2,2,8,256]{3,2,1,0:T(8,128)S(1)}, u32[]{:S(2)}, u32[]{:S(2)}) collective-permute-start(f32[2,2,8,256]{3,2,1,0:T(8,128)S(1)} %get-tuple-element.108), channel_id=1, source_target_pairs={{8,16},{16,8},{24,32},{32,24},{40,48},{48,40},{56,64},{64,56},{72,... | collective-permute-start | bytes 98312 | tf_op jit(solution)/shard_map/ppermute | solution.py:794
  13.1 0.0 collective-permute-done.2
  13.1 1.6 %collective-permute-done.1 = f32[2,2,8,256]{3,2,1,0:T(8,128)S(1)} collective-permute-done((f32[2,2,8,256]{3,2,1,0:T(8,128)S(1)}, f32[2,2,8,256]{3,2,1,0:T(8,128)S(1)}, u32[]{:S(2)}, u32[]{:S(2)}) %collective-permute-start.1) | collective-permute-done | bytes 32800 | tf_op jit(solution)/shard_map/ppermute | solution.py:794
  14.7 5.7 %collective-permute-start.3 = (f32[4,3,2,64,256]{4,3,2,1,0:T(8,128)}, f32[4,3,2,64,256]{4,3,2,1,0:T(8,128)}, u32[]{:S(2)}, u32[]{:S(2)}) collective-permute-start(f32[4,3,2,64,256]{4,3,2,1,0:T(8,128)} %get-tuple-element.61), channel_id=1, source_target_pairs={{8,16},{16,8},{24,32},{32,24},{40,48},{48,40},{56,64},{64,56},{72,... | collective-permute-start | bytes 4718600 | tf_op jit(solution)/shard_map/ppermute | solution.py:794
  20.4 0.1 collective-permute-start.4
  20.5 0.0 copy-done.9
  20.6 0.1 pad_add_fusion.info_ref
  20.7 3.1 %collective-permute-start.7 = (f32[2,12,8,256]{3,2,1,0:T(8,128)S(1)}, f32[2,12,8,256]{3,2,1,0:T(8,128)S(1)}, u32[]{:S(2)}, u32[]{:S(2)}) collective-permute-start(f32[2,12,8,256]{3,2,1,0:T(8,128)S(1)} %pad_maximum_fusion.refs_0_), channel_id=1, source_target_pairs={{0,6},{1,7},{2,4},{3,5},{4,2},{5,3},{6,0},{7,1},{8,14},{9,15},{10,... | collective-permute-start | bytes 589832 | tf_op jit(solution)/shard_map/ppermute | solution.py:822
  23.7 0.6 collective-permute-start.6
  24.4 0.5 collective-permute-start.5
  24.8 5.7 %velocity_inner.1 = (f32[4,3,6,64,256]{4,3,2,1,0:T(8,128)S(1)}, f32[4,3,2,64,256]{4,3,2,1,0:T(8,128)S(1)}, f32[4,3,2,64,256]{4,3,2,1,0:T(8,128)S(1)}) custom-call(s32[7]{0:T(128)S(1)} %pad_add_fusion.info_ref, f32[4,3,8,64,256]{4,3,2,1,0:T(8,128)} %refs_0_.1), custom_call_target="tpu_custom_call" | custom-call | bytes 16500000 | tf_op jit(solution)/shard_map/velocity_inner/pallas_call | solution.py:772
  30.5 3.0 %collective-permute-done.7.refs_3_ = f32[2,12,8,256]{3,2,1,0:T(8,128)S(1)} collective-permute-done((f32[2,12,8,256]{3,2,1,0:T(8,128)S(1)}, f32[2,12,8,256]{3,2,1,0:T(8,128)S(1)}, u32[]{:S(2)}, u32[]{:S(2)}) %collective-permute-start.7) | collective-permute-done | bytes 196640 | tf_op jit(solution)/shard_map/ppermute | solution.py:822
  33.5 0.0 collective-permute-done.6.refs_2_
  33.5 0.7 collective-permute-done.5.refs_1_
  34.2 1.0 template_planes.1
  35.3 1.5 %inner_1.1 = (f32[4,6,64,256]{3,2,1,0:T(8,128)S(1)}, f32[4,4,64,256]{3,2,1,0:T(8,128)S(1)}) custom-call(s32[7]{0:T(128)S(1)} %pad_add_fusion.info_ref, f32[4,3,6,64,256]{4,3,2,1,0:T(8,128)S(1)} %get-tuple-element.60.refs_0_.refs_6_.refs_4_, f32[12,64,256]{2,1,0:T(8,128)S(1)} %get-tuple-element.66.refs_1_.refs_4_.refs_24_.refs_8_, ...), custom_call_target="tpu_custom_call" | custom-call | bytes 9900000 | tf_op jit(solution)/shard_map/inner_1/pallas_call | solution.py:772
  36.8 2.1 %collective-permute-done.3.refs_0_ = f32[4,3,2,64,256]{4,3,2,1,0:T(8,128)} collective-permute-done((f32[4,3,2,64,256]{4,3,2,1,0:T(8,128)}, f32[4,3,2,64,256]{4,3,2,1,0:T(8,128)}, u32[]{:S(2)}, u32[]{:S(2)}) %collective-permute-start.3) | collective-permute-done | bytes 1572896 | tf_op jit(solution)/shard_map/ppermute | solution.py:794
  38.8 0.0 collective-permute-done.4.refs_1_
  38.8 3.9 %outer_1.1 = (f32[4,3,2,64,256]{4,3,2,1,0:T(8,128)S(1)}, f32[4,3,2,64,256]{4,3,2,1,0:T(8,128)S(1)}, f32[4,2,64,256]{3,2,1,0:T(8,128)S(1)}, f32[4,2,64,256]{3,2,1...) custom-call(s32[7]{0:T(128)S(1)} %pad_add_fusion.info_ref, ...), custom_call_target="tpu_custom_call" | custom-call | bytes 16500000 | tf_op jit(solution)/shard_map/outer_1/pallas_call | solution.py:772
  42.7 0.0 copy-start.1
  42.8 5.8 %collective-permute-start.8 = (f32[4,2,64,256]{3,2,1,0:T(8,128)S(1)}, f32[4,2,64,256]{3,2,1,0:T(8,128)S(1)}, u32[]{:S(2)}, u32[]{:S(2)}) collective-permute-start(f32[4,2,64,256]{3,2,1,0:T(8,128)S(1)} %get-tuple-element.71.refs_2_.refs_5_.refs_12_.refs_13_.refs_19_), channel_id=1, source_target_pairs={{8,16},{16,8},{24,32},{32,24},{40,48},{48,40},{56,64},{64,56},{72,... | collective-permute-start | bytes 1572872 | tf_op jit(solution)/shard_map/ppermute | solution.py:794
  48.5 0.1 collective-permute-start.9
  48.6 1.3 %inner_2.1 = (f32[4,6,64,256]{3,2,1,0:T(8,128)S(1)}, f32[4,4,64,256]{3,2,1,0:T(8,128)S(1)}, f32[4,4,64,256]{3,2,1,0:T(8,128)S(1)}) custom-call(s32[7]{0:T(128)S(1)} %pad_add_fusion.info_ref, f32[4,3,6,64,256]{4,3,2,1,0:T(8,128)S(1)} %get-tuple-element.60.refs_0_.refs_6_.refs_4_, f32[4,4,64,256]{3,2,1,0:T(8,128)S(1)} %get-tuple-element.73.refs_1_.refs_11_, ...), custom_call_target="tpu_custom_call" | custom-call | bytes 13200000 | tf_op jit(solution)/shard_map/inner_2/pallas_call | solution.py:772
  49.9 5.4 %collective-permute-done.8.refs_0_.refs_11_.refs_17_ = f32[4,2,64,256]{3,2,1,0:T(8,128)S(1)} collective-permute-done((f32[4,2,64,256]{3,2,1,0:T(8,128)S(1)}, f32[4,2,64,256]{3,2,1,0:T(8,128)S(1)}, u32[]{:S(2)}, u32[]{:S(2)}) %collective-permute-start.8) | collective-permute-done | bytes 524320 | tf_op jit(solution)/shard_map/ppermute | solution.py:794
  55.4 0.0 collective-permute-done.9.refs_1_.refs_12_.refs_18_
  55.4 1.1 %outer_2.1 = (f32[4,2,64,256]{3,2,1,0:T(8,128)S(1)}, f32[4,2,64,256]{3,2,1,0:T(8,128)S(1)}, f32[4,2,64,256]{3,2,1,0:T(8,128)S(1)}, f32[4,2,64,256]{3,2,1,0:T(8,1...) custom-call(s32[7]{0:T(128)S(1)} %pad_add_fusion.info_ref, ...), custom_call_target="tpu_custom_call" | custom-call | bytes 9900000 | tf_op jit(solution)/shard_map/outer_2/pallas_call | solution.py:772
  56.5 5.8 %collective-permute-start.10 = (f32[4,2,64,256]{3,2,1,0:T(8,128)S(1)}, f32[4,2,64,256]{3,2,1,0:T(8,128)S(1)}, u32[]{:S(2)}, u32[]{:S(2)}) collective-permute-start(f32[4,2,64,256]{3,2,1,0:T(8,128)S(1)} %get-tuple-element.75.refs_3_.refs_5_.refs_10_), channel_id=1, source_target_pairs={{8,16},{16,8},{24,32},{32,24},{40,48},{48,40},{56,64},{64,56},{72,... | collective-permute-start | bytes 1572872 | tf_op jit(solution)/shard_map/ppermute | solution.py:794
  62.3 0.1 collective-permute-start.11
  62.3 3.8 %inner_3.1 = (f32[4,6,64,256]{3,2,1,0:T(8,128)S(1)}, f32[4,4,64,256]{3,2,1,0:T(8,128)S(1)}, f32[4,3,6,64,256]{4,3,2,1,0:T(8,128)S(1)}, f32[4,8,64,256]{3,2,1,0:T(8,128)}) custom-call(s32[7]{0:T(128)S(1)} %pad_add_fusion.info_ref, f32[4,3,6,64,256]{4,3,2,1,0:T(8,128)S(1)} %get-tuple-element.60.refs_0_.refs_6_.refs_4_, ...), custom_call_target="tpu_custom_call" | custom-call | bytes 23100000 | tf_op jit(solution)/shard_map/inner_3/pallas_call | solution.py:772
  66.2 2.9 %collective-permute-done.10.refs_0_.refs_6_ = f32[4,2,64,256]{3,2,1,0:T(8,128)S(1)} collective-permute-done((f32[4,2,64,256]{3,2,1,0:T(8,128)S(1)}, f32[4,2,64,256]{3,2,1,0:T(8,128)S(1)}, u32[]{:S(2)}, u32[]{:S(2)}) %collective-permute-start.10) | collective-permute-done | bytes 524320 | tf_op jit(solution)/shard_map/ppermute | solution.py:794
  69.1 0.0 collective-permute-done.11.refs_1_.refs_7_
  69.1 1.2 %outer_3.1 = (f32[4,2,64,256]{3,2,1,0:T(8,128)S(1)}, f32[4,2,64,256]{3,2,1,0:T(8,128)S(1)}, f32[4,2,64,256]{3,2,1,0:T(8,128)S(1)}, f32[4,2,64,256]{3,2,1,0:T(8,1...) custom-call(s32[7]{0:T(128)S(1)} %pad_add_fusion.info_ref, ...), custom_call_target="tpu_custom_call" | custom-call | bytes 6600000 | tf_op jit(solution)/shard_map/outer_3/pallas_call | solution.py:772
  70.3 5.8 %collective-permute-start.12 = (f32[4,3,64,256]{3,2,1,0:T(8,128)S(1)}, f32[4,3,64,256]{3,2,1,0:T(8,128)S(1)}, u32[]{:S(2)}, u32[]{:S(2)}) collective-permute-start(f32[4,3,64,256]{3,2,1,0:T(8,128)S(1)} %get-tuple-element.89.refs_12_.refs_5_), channel_id=1, source_target_pairs={{8,16},{16,8},{24,32},{32,24},{40,48},{48,40},{56,64},{64,56},{72,... | collective-permute-start | bytes 2359304 | tf_op jit(solution)/shard_map/ppermute | solution.py:794
  76.0 0.1 collective-permute-start.13
  76.2 4.1 %inner_4.1 = (f32[4,6,64,256]{3,2,1,0:T(8,128)S(1)}, f32[8,4,8,256]{3,2,1,0:T(8,128)S(1)}, f32[4,3,6,64,256]{4,3,2,1,0:T(8,128)S(1)}, f32[4,3,2,64,256]{4,3,2,1,0:T(8,128)S(1)}, f32[4,3,2,64,256]{4,3,2,1,0:T(8,128)S(1)}) custom-call(s32[7]{0:T(128)S(1)} %pad_add_fusion.info_ref, f32[4,3,6,64,256]{4,3,2,1,0:T(8,128)S(1)} %get-tuple-element.60.refs_0_.refs_6_.refs_4_, ...), custom_call_target="tpu_custom_call" | custom-call | bytes 16500000 | tf_op jit(solution)/shard_map/inner_4/pallas_call | solution.py:772
  80.3 1.2 %copy-done.6 = f32[4,3,2,64,256]{4,3,2,1,0:T(8,128)} copy-done((f32[4,3,2,64,256]{4,3,2,1,0:T(8,128)}, f32[4,3,2,64,256]{4,3,2,1,0:T(8,128)S(1)}, u32[]{:S(2)}) %copy-start.6) | copy-done | bytes 1572888
  81.5 4.2 %collective-permute-done.12.refs_0_ = f32[4,3,64,256]{3,2,1,0:T(8,128)S(1)} collective-permute-done((f32[4,3,64,256]{3,2,1,0:T(8,128)S(1)}, f32[4,3,64,256]{3,2,1,0:T(8,128)S(1)}, u32[]{:S(2)}, u32[]{:S(2)}) %collective-permute-start.12) | collective-permute-done | bytes 786464 | tf_op jit(solution)/shard_map/ppermute | solution.py:794
  85.7 0.0 collective-permute-done.13.refs_1_
  85.7 3.2 %outer_4.1 = (f32[8,8,8,256]{3,2,1,0:T(8,128)}, f32[4,2,64,256]{3,2,1,0:T(8,128)}, f32[4,2,64,256]{3,2,1,0:T(8,128)}) custom-call(s32[7]{0:T(128)S(1)} %pad_add_fusion.info_ref, f32[4,3,64,256]{3,2,1,0:T(8,128)S(1)} %collective-permute-done.12.refs_0_, f32[4,3,64,256]{3,2,1,0:T(8,128)S(1)} %collective-permute-done.13.refs_1_, ...), custom_call_target="tpu_custom_call" | custom-call | bytes 9900000 | tf_op jit(solution)/shard_map/outer_4/pallas_call | solution.py:772
  89.0 8.7 %all-to-all-start = ((f32[8,8,8,256]{3,2,1,0:T(8,128)}), f32[8,8,8,256]{3,2,1,0:T(8,128)S(1)}, u32[]{:S(2)}, u32[]{:S(2)}) async-start(f32[8,8,8,256]{3,2,1,0:T(8,128)} %get-tuple-element.99), calls=%async_computation | async-start | bytes 1048576 | tf_op jit(solution)/shard_map/all_to_all | solution.py:920
  97.7 9.2 %finish.1 = f32[4,3,8,64,256]{4,3,2,1,0:T(8,128)} custom-call(s32[7]{0:T(128)S(1)} %pad_add_fusion.info_ref, f32[4,3,64,256]{3,2,1,0:T(8,128)} %copy-done.4, f32[4,3,64,256]{3,2,1,0:T(8,128)} %copy-done.5, f32[4,2,64,256]{3,2,1,0:T(8,128)} %get-tuple-element.100.refs_2_, f32[4,2,64,256]{3,2,1,0:T(8,128)} %get-tuple-element.101.refs_3_, ...), custom_call_target="tpu_custom_call" | custom-call | bytes 19800000 | tf_op jit(solution)/shard_map/finish/pallas_call | solution.py:772
  106.9 0.0 all-to-all-done
  106.9 0.7 reduce_sum.9
  (18 shorter events, 0.0 us)
Async XLA Ops:
  0.6 6.1 %collective-permute-start = (f32[8,8,256]{2,1,0:T(8,128)}, f32[8,8,256]{2,1,0:T(8,128)S(1)}, u32[]{:S(2)}, u32[]{:S(2)}) collective-permute-start(f32[8,8,256]{2,1,0:T(8,128)} %param.4), channel_id=1, source_target_pairs={{0,1},{1,0},{2,3},{3,2},{4,5},{5,4},{6,7},{7,6},{8,9},{9,8},{10,11... | collective-permute-start | bytes 196616 | tf_op jit(solution)/shard_map/ppermute | solution.py:822
  2.1 4.6 %copy-start.8 = (f32[8,8,256]{2,1,0:T(8,128)S(1)}, f32[8,8,256]{2,1,0:T(8,128)}, u32[]{:S(2)}) copy-start(f32[8,8,256]{2,1,0:T(8,128)} %param.4) | copy-start | bytes 196612
  2.1 18.4 %copy-start.9 = (s32[4]{0:T(128)S(1)}, s32[4]{0:T(128)}, u32[]{:S(2)}) copy-start(s32[4]{0:T(128)} %param.7) | copy-start | bytes 52
  6.7 6.4 %collective-permute-start.2 = (f32[2,2,8,256]{3,2,1,0:T(8,128)S(1)}, f32[2,2,8,256]{3,2,1,0:T(8,128)S(1)}, u32[]{:S(2)}, u32[]{:S(2)}) collective-permute-start(f32[2,2,8,256]{3,2,1,0:T(8,128)S(1)} %get-tuple-element.107), channel_id=1, source_target_pairs={{0,8},{8,0},{16,24},{24,16},{32,40},{40,32},{48,56},{56,48},{64,72... | collective-permute-start | bytes 98312 | tf_op jit(solution)/shard_map/ppermute | solution.py:794
  6.8 7.9 %collective-permute-start.1 = (f32[2,2,8,256]{3,2,1,0:T(8,128)S(1)}, f32[2,2,8,256]{3,2,1,0:T(8,128)S(1)}, u32[]{:S(2)}, u32[]{:S(2)}) collective-permute-start(f32[2,2,8,256]{3,2,1,0:T(8,128)S(1)} %get-tuple-element.108), channel_id=1, source_target_pairs={{8,16},{16,8},{24,32},{32,24},{40,48},{48,40},{56,64},{64,56},{72,... | collective-permute-start | bytes 98312 | tf_op jit(solution)/shard_map/ppermute | solution.py:794
  14.7 24.2 %collective-permute-start.3 = (f32[4,3,2,64,256]{4,3,2,1,0:T(8,128)}, f32[4,3,2,64,256]{4,3,2,1,0:T(8,128)}, u32[]{:S(2)}, u32[]{:S(2)}) collective-permute-start(f32[4,3,2,64,256]{4,3,2,1,0:T(8,128)} %get-tuple-element.61), channel_id=1, source_target_pairs={{8,16},{16,8},{24,32},{32,24},{40,48},{48,40},{56,64},{64,56},{72,... | collective-permute-start | bytes 4718600 | tf_op jit(solution)/shard_map/ppermute | solution.py:794
  20.4 18.4 %collective-permute-start.4 = (f32[4,3,2,64,256]{4,3,2,1,0:T(8,128)}, f32[4,3,2,64,256]{4,3,2,1,0:T(8,128)}, u32[]{:S(2)}, u32[]{:S(2)}) collective-permute-start(f32[4,3,2,64,256]{4,3,2,1,0:T(8,128)} %get-tuple-element.62), channel_id=1, source_target_pairs={{0,8},{8,0},{16,24},{24,16},{32,40},{40,32},{48,56},{56,48},{64,72... | collective-permute-start | bytes 4718600 | tf_op jit(solution)/shard_map/ppermute | solution.py:794
  20.7 12.8 %collective-permute-start.7 = (f32[2,12,8,256]{3,2,1,0:T(8,128)S(1)}, f32[2,12,8,256]{3,2,1,0:T(8,128)S(1)}, u32[]{:S(2)}, u32[]{:S(2)}) collective-permute-start(f32[2,12,8,256]{3,2,1,0:T(8,128)S(1)} %pad_maximum_fusion.refs_0_), channel_id=1, source_target_pairs={{0,6},{1,7},{2,4},{3,5},{4,2},{5,3},{6,0},{7,1},{8,14},{9,15},{10,... | collective-permute-start | bytes 589832 | tf_op jit(solution)/shard_map/ppermute | solution.py:822
  23.7 9.8 %collective-permute-start.6 = (f32[2,12,8,256]{3,2,1,0:T(8,128)S(1)}, f32[2,12,8,256]{3,2,1,0:T(8,128)S(1)}, u32[]{:S(2)}, u32[]{:S(2)}) collective-permute-start(f32[2,12,8,256]{3,2,1,0:T(8,128)S(1)} %pad_maximum_fusion.refs_0_), channel_id=1, source_target_pairs={{0,4},{1,5},{2,6},{3,7},{4,0},{5,1},{6,2},{7,3},{8,12},{9,13},{10,... | collective-permute-start | bytes 589832 | tf_op jit(solution)/shard_map/ppermute | solution.py:822
  24.4 9.8 %collective-permute-start.5 = (f32[2,12,8,256]{3,2,1,0:T(8,128)S(1)}, f32[2,12,8,256]{3,2,1,0:T(8,128)S(1)}, u32[]{:S(2)}, u32[]{:S(2)}) collective-permute-start(f32[2,12,8,256]{3,2,1,0:T(8,128)S(1)} %pad_maximum_fusion.refs_0_), channel_id=1, source_target_pairs={{0,2},{1,3},{2,0},{3,1},{4,6},{5,7},{6,4},{7,5},{8,10},{9,11},{10,... | collective-permute-start | bytes 589832 | tf_op jit(solution)/shard_map/ppermute | solution.py:822
  38.8 9.8 %copy-start = (f32[4,8,64,256]{3,2,1,0:T(8,128)S(1)}, f32[4,8,64,256]{3,2,1,0:T(8,128)}, u32[]{:S(2)}) copy-start(f32[4,8,64,256]{3,2,1,0:T(8,128)} %refs_8_.1) | copy-start | bytes 6291460
  42.7 33.4 %copy-start.1 = (f32[4,2,64,256]{3,2,1,0:T(8,128)}, f32[4,2,64,256]{3,2,1,0:T(8,128)S(1)}, u32[]{:S(2)}) copy-start(f32[4,2,64,256]{3,2,1,0:T(8,128)S(1)} %get-tuple-element.87.refs_15_.refs_21_.refs_6_) | copy-start | bytes 1572868
  42.8 33.4 %copy-start.2 = (f32[4,2,64,256]{3,2,1,0:T(8,128)}, f32[4,2,64,256]{3,2,1,0:T(8,128)S(1)}, u32[]{:S(2)}) copy-start(f32[4,2,64,256]{3,2,1,0:T(8,128)S(1)} %get-tuple-element.88.refs_16_.refs_22_.refs_7_) | copy-start | bytes 1572868
  42.8 12.6 %collective-permute-start.8 = (f32[4,2,64,256]{3,2,1,0:T(8,128)S(1)}, f32[4,2,64,256]{3,2,1,0:T(8,128)S(1)}, u32[]{:S(2)}, u32[]{:S(2)}) collective-permute-start(f32[4,2,64,256]{3,2,1,0:T(8,128)S(1)} %get-tuple-element.71.refs_2_.refs_5_.refs_12_.refs_13_.refs_19_), channel_id=1, source_target_pairs={{8,16},{16,8},{24,32},{32,24},{40,48},{48,40},{56,64},{64,56},{72,... | collective-permute-start | bytes 1572872 | tf_op jit(solution)/shard_map/ppermute | solution.py:794
  48.5 6.9 %collective-permute-start.9 = (f32[4,2,64,256]{3,2,1,0:T(8,128)S(1)}, f32[4,2,64,256]{3,2,1,0:T(8,128)S(1)}, u32[]{:S(2)}, u32[]{:S(2)}) collective-permute-start(f32[4,2,64,256]{3,2,1,0:T(8,128)S(1)} %get-tuple-element.72.refs_3_.refs_6_.refs_13_.refs_14_.refs_20_), channel_id=1, source_target_pairs={{0,8},{8,0},{16,24},{24,16},{32,40},{40,32},{48,56},{56,48},{64,72... | collective-permute-start | bytes 1572872 | tf_op jit(solution)/shard_map/ppermute | solution.py:794
  56.5 12.6 %collective-permute-start.10 = (f32[4,2,64,256]{3,2,1,0:T(8,128)S(1)}, f32[4,2,64,256]{3,2,1,0:T(8,128)S(1)}, u32[]{:S(2)}, u32[]{:S(2)}) collective-permute-start(f32[4,2,64,256]{3,2,1,0:T(8,128)S(1)} %get-tuple-element.75.refs_3_.refs_5_.refs_10_), channel_id=1, source_target_pairs={{8,16},{16,8},{24,32},{32,24},{40,48},{48,40},{56,64},{64,56},{72,... | collective-permute-start | bytes 1572872 | tf_op jit(solution)/shard_map/ppermute | solution.py:794
  62.3 6.9 %collective-permute-start.11 = (f32[4,2,64,256]{3,2,1,0:T(8,128)S(1)}, f32[4,2,64,256]{3,2,1,0:T(8,128)S(1)}, u32[]{:S(2)}, u32[]{:S(2)}) collective-permute-start(f32[4,2,64,256]{3,2,1,0:T(8,128)S(1)} %get-tuple-element.76.refs_4_.refs_6_.refs_11_), channel_id=1, source_target_pairs={{0,8},{8,0},{16,24},{24,16},{32,40},{40,32},{48,56},{56,48},{64,72... | collective-permute-start | bytes 1572872 | tf_op jit(solution)/shard_map/ppermute | solution.py:794
  70.3 15.4 %collective-permute-start.12 = (f32[4,3,64,256]{3,2,1,0:T(8,128)S(1)}, f32[4,3,64,256]{3,2,1,0:T(8,128)S(1)}, u32[]{:S(2)}, u32[]{:S(2)}) collective-permute-start(f32[4,3,64,256]{3,2,1,0:T(8,128)S(1)} %get-tuple-element.89.refs_12_.refs_5_), channel_id=1, source_target_pairs={{8,16},{16,8},{24,32},{32,24},{40,48},{48,40},{56,64},{64,56},{72,... | collective-permute-start | bytes 2359304 | tf_op jit(solution)/shard_map/ppermute | solution.py:794
  76.0 9.7 %collective-permute-start.13 = (f32[4,3,64,256]{3,2,1,0:T(8,128)S(1)}, f32[4,3,64,256]{3,2,1,0:T(8,128)S(1)}, u32[]{:S(2)}, u32[]{:S(2)}) collective-permute-start(f32[4,3,64,256]{3,2,1,0:T(8,128)S(1)} %get-tuple-element.90.refs_13_.refs_6_), channel_id=1, source_target_pairs={{0,8},{8,0},{16,24},{24,16},{32,40},{40,32},{48,56},{56,48},{64,72... | collective-permute-start | bytes 2359304 | tf_op jit(solution)/shard_map/ppermute | solution.py:794
  80.3 1.2 %copy-start.6 = (f32[4,3,2,64,256]{4,3,2,1,0:T(8,128)}, f32[4,3,2,64,256]{4,3,2,1,0:T(8,128)S(1)}, u32[]{:S(2)}) copy-start(f32[4,3,2,64,256]{4,3,2,1,0:T(8,128)S(1)} %get-tuple-element.102.refs_4_) | copy-start | bytes 4718596
  81.5 7.4 %copy-start.3 = (f32[4,3,6,64,256]{4,3,2,1,0:T(8,128)}, f32[4,3,6,64,256]{4,3,2,1,0:T(8,128)S(1)}, u32[]{:S(2)}) copy-start(f32[4,3,6,64,256]{4,3,2,1,0:T(8,128)S(1)} %get-tuple-element.104.refs_10_) | copy-start | bytes 14155780
  81.5 7.5 %copy-start.7 = (f32[4,3,2,64,256]{4,3,2,1,0:T(8,128)}, f32[4,3,2,64,256]{4,3,2,1,0:T(8,128)S(1)}, u32[]{:S(2)}) copy-start(f32[4,3,2,64,256]{4,3,2,1,0:T(8,128)S(1)} %get-tuple-element.103.refs_5_) | copy-start | bytes 4718596
  85.7 3.3 %copy-start.4 = (f32[4,3,64,256]{3,2,1,0:T(8,128)}, f32[4,3,64,256]{3,2,1,0:T(8,128)S(1)}, u32[]{:S(2)}) copy-start(f32[4,3,64,256]{3,2,1,0:T(8,128)S(1)} %collective-permute-done.12.refs_0_) | copy-start | bytes 2359300
  85.7 3.3 %copy-start.5 = (f32[4,3,64,256]{3,2,1,0:T(8,128)}, f32[4,3,64,256]{3,2,1,0:T(8,128)S(1)}, u32[]{:S(2)}) copy-start(f32[4,3,64,256]{3,2,1,0:T(8,128)S(1)} %collective-permute-done.13.refs_1_) | copy-start | bytes 2359300
  89.0 17.9 %all-to-all-start = ((f32[8,8,8,256]{3,2,1,0:T(8,128)}), f32[8,8,8,256]{3,2,1,0:T(8,128)S(1)}, u32[]{:S(2)}, u32[]{:S(2)}) async-start(f32[8,8,8,256]{3,2,1,0:T(8,128)} %get-tuple-element.99), calls=%async_computation | async-start | bytes 1048576 | tf_op jit(solution)/shard_map/all_to_all | solution.py:920

commit v3 on v2

--- a/solution.py
+++ b/solution.py
@@ -155,32 +155,45 @@
 
 
 def t_load(t, k, role=0):
-    return load(t, 2 + k if role == 0 else 9 - k)
+    return load(t, k if role == 0 else 7 - k)
 
 
 def t_slopes(dt, k, role=0):
-    return [load(dt, c, 1 + k if role == 0 else 8 - k) for c in (0, 1)]
+    return [load(dt, c, k if role == 0 else 7 - k) for c in (0, 1)]
+
+
+def named(kernel, name, role):
+    kernel.__name__ = name + ("_chip", "_core")[role]
+    return kernel
+
+
+def halo_slopes(s, th, slopes, roles=ROLES):
+    @pl.when(s == 0)
+    def _():
+        for r in roles:
+            mid = load(th[r], 0)
+            store_all([(slopes, dy(mid), (r, 0)), (slopes, dx(mid), (r, 1))])
+
+    return {r: [load(slopes, r, c) for c in (0, 1)] for r in roles}
 
 
 def template_planes(info, s, *refs):
-    *sources, t, dt = refs
+    *sources, t, dt, send_z, send_c = refs
     odd, me = info[4], info[6]
 
     @pl.when(s == 0)
     def _():
-        for j in range(-2, 10):
-            at = 2 + natural(odd, j)
-            if j < 0:
-                at = 1 - odd if j == -1 else odd
-            if j > 7:
-                at = 10 + odd if j == 8 else 11 - odd
+        for j in range(8):
             for i, source in enumerate(sources):
                 for x in (0, 1):
                     row = pl.multiple_of(8 * jnp.bitwise_xor(me, 2 * i + x), 8)
-                    t[j + 2, pl.ds(row, 8)] = source[x, at]
-        for j in range(-1, 9):
-            mid = load(t, j + 2)
-            store_all([(dt, dy(mid), (0, j + 1)), (dt, dx(mid), (1, j + 1))])
+                    t[j, pl.ds(row, 8)] = source[x, natural(odd, j)]
+        for i in (0, 1):
+            send_z[i] = t[i]
+            send_c[i] = t[7 - i]
+        for j in range(8):
+            mid = load(t, j)
+            store_all([(dt, dy(mid), (0, j)), (dt, dx(mid), (1, j))])
 
 
 def velocity_inner(info, s, m, w_in, w_edge, m_edge):
@@ -227,45 +240,51 @@
         i2_in[0] = i1_in[0, 1:5]
 
 
-def outer_1(info, s, *refs):
-    mr, m_edge, w_edge, t, dt, wp, i1p = refs[0:2], *refs[2:6], refs[6:8], refs[8:10]
-    w_out, i1_out, send = refs[10:12], refs[12:14], refs[14:16]
-    odd = info[4]
-    sign = (1 - 2 * odd).astype(f32)
-    for r in ROLES:
-        to = TOWARD[r]
-        h1 = 1 - odd if r == 0 else odd
-        inside = info[5].astype(f32) if r == 0 else 1.0
-        wh, w0 = [], []
-        for c in range(3):
-            turn = sign if c == 0 else 1.0
-            m_h1, m_p0 = load(mr[r], 0, c, h1), load(m_edge, 0, c, r)
-            a, b = half * centre * turn, half * smoothing * turn
-            wh.append(smooth(m_h1, m_p0, load(mr[r], 0, c, 1 - h1), a * inside, b * inside))
-            w0.append(add(load(w_edge, 0, c, r), scale(m_h1, b)))
-        at = lambda k: t_load(t, k, r)
-        i_h1 = forward_by(at(-1), at(0), at(-2), t_slopes(dt, -1, r), wh, to)
-        i_p0 = forward_by(at(0), at(1), at(-1), t_slopes(dt, 0, r), w0, to)
-        targets = [(i1_out[r], i_h1, (0, 0)), (i1_out[r], i_p0, (0, 1))]
-        targets += [(w_out[r], w[c], (0, c, i)) for i, w in enumerate((wh, w0)) for c in range(3)]
-        store_all(targets)
-
-    @pl.when(info[s] > 1)
-    def _():
-        for r in ROLES:
-            to, near, far = TOWARD[r], r, 1 - r
-            i_h1, i_p0 = load(i1_out[r], 0, 0), load(i1_out[r], 0, 1)
-            i_p1, i_p2 = load(i1p[r], 0, near), load(i1p[r], 0, far)
-            w0 = [load(w_out[r], 0, c, 1) for c in range(3)]
-            w1 = [load(wp[r], 0, c, near) for c in range(3)]
-            store(send[r], forward(i_p0, i_p1, i_h1, w0, to), 0, 0)
-            store(send[r], forward(i_p1, i_p2, i_p0, w1, to), 0, 1)
-
-    @pl.when(info[s] <= 1)
-    def _():
-        for r in ROLES:
-            send[r][0, 0] = i1_out[r][0, 1]
-            send[r][0, 1] = i1p[r][0, r]
+def outer_1(role):
+    roles = (role,)
+
+    def kernel(info, s, *refs):
+        m_edge, w_edge, t, dt = refs[:4]
+        mr, th, wp, i1p, w_out, i1_out, send = ({role: ref} for ref in refs[4:11])
+        slopes = halo_slopes(s, th, refs[11], roles)
+        odd = info[4]
+        sign = (1 - 2 * odd).astype(f32)
+        for r in roles:
+            to = TOWARD[r]
+            h1 = 1 - odd if r == 0 else odd
+            inside = info[5].astype(f32) if r == 0 else 1.0
+            wh, w0 = [], []
+            for c in range(3):
+                turn = sign if c == 0 else 1.0
+                m_h1, m_p0 = load(mr[r], 0, c, h1), load(m_edge, 0, c, r)
+                a, b = half * centre * turn, half * smoothing * turn
+                wh.append(smooth(m_h1, m_p0, load(mr[r], 0, c, 1 - h1), a * inside, b * inside))
+                w0.append(add(load(w_edge, 0, c, r), scale(m_h1, b)))
+            th1, th2, tp0, tp1 = load(th[r], 0), load(th[r], 1), t_load(t, 0, r), t_load(t, 1, r)
+            i_h1 = forward_by(th1, tp0, th2, slopes[r], wh, to)
+            i_p0 = forward_by(tp0, tp1, th1, t_slopes(dt, 0, r), w0, to)
+            targets = [(i1_out[r], i_h1, (0, 0)), (i1_out[r], i_p0, (0, 1))]
+            targets += [(w_out[r], w[c], (0, c, i)) for i, w in enumerate((wh, w0)) for c in range(3)]
+            store_all(targets)
+
+        @pl.when(info[s] > 1)
+        def _():
+            for r in roles:
+                to, near, far = TOWARD[r], r, 1 - r
+                i_h1, i_p0 = load(i1_out[r], 0, 0), load(i1_out[r], 0, 1)
+                i_p1, i_p2 = load(i1p[r], 0, near), load(i1p[r], 0, far)
+                w0 = [load(w_out[r], 0, c, 1) for c in range(3)]
+                w1 = [load(wp[r], 0, c, near) for c in range(3)]
+                store(send[r], forward(i_p0, i_p1, i_h1, w0, to), 0, 0)
+                store(send[r], forward(i_p1, i_p2, i_p0, w1, to), 0, 1)
+
+        @pl.when(info[s] <= 1)
+        def _():
+            for r in roles:
+                send[r][0, 0] = i1_out[r][0, 1]
+                send[r][0, 1] = i1p[r][0, r]
+
+    return named(kernel, "outer_1", role)
 
 
 def gather_planes(x, sides, inner):
@@ -316,49 +335,53 @@
         unrolled(2, 6, step)
 
 
-def outer_2(info, s, *refs):
-    r1, wb, wp, s1, i3p = (refs[2 * i : 2 * i + 2] for i in range(5))
-    targets = refs[10]
-    i3_out, i4_out, a4_out, send = (refs[11 + 2 * i : 13 + 2 * i] for i in range(4))
-    odd = info[4]
-
-    @pl.when(info[s] > 2)
-    def _():
-        for r in ROLES:
-            i_h1, i_h2 = load(r1[r], 0, 0), load(r1[r], 0, 1)
-            i_p0, i_p1 = load(s1[r], 0, 0), load(s1[r], 0, 1)
-            wh = [load(wb[r], 0, c, 0) for c in range(3)]
-            w0 = [load(wb[r], 0, c, 1) for c in range(3)]
-            store(i3_out[r], forward(i_h1, i_p0, i_h2, wh, TOWARD[r]), 0, 0)
-            store(i3_out[r], forward(i_p0, i_p1, i_h1, w0, TOWARD[r]), 0, 1)
-
-    @pl.when(info[s] <= 2)
-    def _():
-        for r in ROLES:
-            i3_out[r][0, 0] = r1[r][0, 0]
-            i3_out[r][0, 1] = s1[r][0, 0]
-
-    def late(r, i4_p0, i4_p1):
-        n = [natural(odd, k if r == 0 else 7 - k) for k in (0, 1)]
-        a_p0, a_p1 = sub(i4_p0, load(targets, 0, n[0])), sub(i4_p1, load(targets, 0, n[1]))
-        store_all([(i4_out[r], i4_p0, (0, 0)), (send[r], a_p0, (0, 0))])
-        f_p1 = mul(load(wp[r], 0, 0, r), a_p1)
-        store_all([(i4_out[r], i4_p1, (0, 1)), (a4_out[r], a_p1, (0, 0)), (send[r], f_p1, (0, 1))])
-
-    @pl.when(info[s] > 3)
-    def _():
-        for r in ROLES:
-            to, near, far = TOWARD[r], r, 1 - r
-            i_h1, i_p0 = load(i3_out[r], 0, 0), load(i3_out[r], 0, 1)
-            i_p1, i_p2 = load(i3p[r], 0, near), load(i3p[r], 0, far)
-            w0 = [load(wb[r], 0, c, 1) for c in range(3)]
-            w1 = [load(wp[r], 0, c, near) for c in range(3)]
-            late(r, forward(i_p0, i_p1, i_h1, w0, to), forward(i_p1, i_p2, i_p0, w1, to))
-
-    @pl.when(info[s] <= 3)
-    def _():
-        for r in ROLES:
-            late(r, load(i3_out[r], 0, 1), load(i3p[r], 0, r))
+def outer_2(role):
+    roles = (role,)
+
+    def kernel(info, s, *refs):
+        targets = refs[0]
+        r1, wb, wp, s1, i3p, i3_out, i4_out, a4_out, send = ({role: ref} for ref in refs[1:])
+        odd = info[4]
+
+        @pl.when(info[s] > 2)
+        def _():
+            for r in roles:
+                i_h1, i_h2 = load(r1[r], 0, 0), load(r1[r], 0, 1)
+                i_p0, i_p1 = load(s1[r], 0, 0), load(s1[r], 0, 1)
+                wh = [load(wb[r], 0, c, 0) for c in range(3)]
+                w0 = [load(wb[r], 0, c, 1) for c in range(3)]
+                store(i3_out[r], forward(i_h1, i_p0, i_h2, wh, TOWARD[r]), 0, 0)
+                store(i3_out[r], forward(i_p0, i_p1, i_h1, w0, TOWARD[r]), 0, 1)
+
+        @pl.when(info[s] <= 2)
+        def _():
+            for r in roles:
+                i3_out[r][0, 0] = r1[r][0, 0]
+                i3_out[r][0, 1] = s1[r][0, 0]
+
+        def late(r, i4_p0, i4_p1):
+            n = [natural(odd, k if r == 0 else 7 - k) for k in (0, 1)]
+            a_p0, a_p1 = sub(i4_p0, load(targets, 0, n[0])), sub(i4_p1, load(targets, 0, n[1]))
+            store_all([(i4_out[r], i4_p0, (0, 0)), (send[r], a_p0, (0, 0))])
+            f_p1 = mul(load(wp[r], 0, 0, r), a_p1)
+            store_all([(i4_out[r], i4_p1, (0, 1)), (a4_out[r], a_p1, (0, 0)), (send[r], f_p1, (0, 1))])
+
+        @pl.when(info[s] > 3)
+        def _():
+            for r in roles:
+                to, near, far = TOWARD[r], r, 1 - r
+                i_h1, i_p0 = load(i3_out[r], 0, 0), load(i3_out[r], 0, 1)
+                i_p1, i_p2 = load(i3p[r], 0, near), load(i3p[r], 0, far)
+                w0 = [load(wb[r], 0, c, 1) for c in range(3)]
+                w1 = [load(wp[r], 0, c, near) for c in range(3)]
+                late(r, forward(i_p0, i_p1, i_h1, w0, to), forward(i_p1, i_p2, i_p0, w1, to))
+
+        @pl.when(info[s] <= 3)
+        def _():
+            for r in roles:
+                late(r, load(i3_out[r], 0, 1), load(i3p[r], 0, r))
+
+    return named(kernel, "outer_2", role)
 
 
 def inner_3(info, s, *refs):
@@ -446,65 +469,69 @@
         copy.wait()
 
 
-def outer_3(info, s, *refs):
-    r2, wb, wp, s2, a3p, i3b, i3p, r1, s1, i1b, i1p = (refs[2 * i : 2 * i + 2] for i in range(11))
-    a3, a2_out, send = (refs[22 + 2 * i : 24 + 2 * i] for i in range(3))
-
-    def gz(r, adj, inner, outer):
-        return (send[r], add(load(send[r], 0, 2), mul(adj, dz(inner, outer, TOWARD[r]))), (0, 2))
-
-
-    @pl.when(info[s] > 3)
-    def _():
-        for r in ROLES:
-            to = TOWARD[r]
-            a_h1, a_p0 = load(r2[r], 0, 0), load(s2[r], 0, 0)
-            f_h2, f_p1 = scale(load(r2[r], 0, 1), -1.0), load(s2[r], 0, 1)
-            wh = [load(wb[r], 0, c, 0) for c in range(3)]
-            w0 = [load(wb[r], 0, c, 1) for c in range(3)]
-            store(a3[r], backward(a_h1, mul(w0[0], a_p0), f_h2, wh[1], wh[2], to), 0, 0)
-            b_p0 = backward(a_p0, f_p1, mul(wh[0], a_h1), w0[1], w0[2], to)
-            g = mul(a_p0, dz(load(i3p[r], 0, r), load(i3b[r], 0, 0), to))
-            store_all([(a3[r], b_p0, (0, 1)), (send[r], g, (0, 2))])
-
-    @pl.when(info[s] <= 3)
-    def _():
-        for r in ROLES:
-            a3[r][0, 0] = r2[r][0, 0]
-            a3[r][0, 1] = s2[r][0, 0]
-            send[r][0, 2] = jnp.zeros(send[r].shape[2:], f32)
-
-    def late(r, a2_p0, a2_p1):
-        f_p1 = mul(load(wp[r], 0, 0, r), a2_p1)
-        store_all([(a2_out[r], a2_p0, (0, 0)), (send[r], a2_p0, (0, 0))])
-        store_all([(a2_out[r], a2_p1, (0, 1)), (send[r], f_p1, (0, 1))])
-
-    @pl.when(info[s] > 2)
-    def _():
-        for r in ROLES:
-            to, near, far = TOWARD[r], r, 1 - r
-            a_h1, a_p0 = load(a3[r], 0, 0), load(a3[r], 0, 1)
-            a_p1, a_p2 = load(a3p[r], 0, near), load(a3p[r], 0, far)
-            wh0 = load(wb[r], 0, 0, 0)
-            w0 = [load(wb[r], 0, c, 1) for c in range(3)]
-            w1 = [load(wp[r], 0, c, near) for c in range(3)]
-            f_p2 = mul(load(wp[r], 0, 0, far), a_p2)
-            store_all([gz(r, a_p0, load(s1[r], 0, 1), load(r1[r], 0, 0))])
-            late(
-                r,
-                backward(a_p0, mul(w1[0], a_p1), mul(wh0, a_h1), w0[1], w0[2], to),
-                backward(a_p1, f_p2, mul(w0[0], a_p0), w1[1], w1[2], to),
-            )
-
-    @pl.when(info[s] <= 2)
-    def _():
-        for r in ROLES:
-            late(r, load(a3[r], 0, 1), load(a3p[r], 0, r))
-
-    @pl.when(info[s] > 1)
-    def _():
-        for r in ROLES:
-            store_all([gz(r, load(a2_out[r], 0, 0), load(i1p[r], 0, r), load(i1b[r], 0, 0))])
+def outer_3(role):
+    roles = (role,)
+
+    def kernel(info, s, *refs):
+        r2, wb, wp, s2, a3p, i3b, i3p, r1, s1, i1b, i1p, a3, a2_out, send = ({role: ref} for ref in refs)
+
+        def gz(r, adj, inner, outer):
+            return (send[r], add(load(send[r], 0, 2), mul(adj, dz(inner, outer, TOWARD[r]))), (0, 2))
+
+
+        @pl.when(info[s] > 3)
+        def _():
+            for r in roles:
+                to = TOWARD[r]
+                a_h1, a_p0 = load(r2[r], 0, 0), load(s2[r], 0, 0)
+                f_h2, f_p1 = scale(load(r2[r], 0, 1), -1.0), load(s2[r], 0, 1)
+                wh = [load(wb[r], 0, c, 0) for c in range(3)]
+                w0 = [load(wb[r], 0, c, 1) for c in range(3)]
+                store(a3[r], backward(a_h1, mul(w0[0], a_p0), f_h2, wh[1], wh[2], to), 0, 0)
+                b_p0 = backward(a_p0, f_p1, mul(wh[0], a_h1), w0[1], w0[2], to)
+                g = mul(a_p0, dz(load(i3p[r], 0, r), load(i3b[r], 0, 0), to))
+                store_all([(a3[r], b_p0, (0, 1)), (send[r], g, (0, 2))])
+
+        @pl.when(info[s] <= 3)
+        def _():
+            for r in roles:
+                a3[r][0, 0] = r2[r][0, 0]
+                a3[r][0, 1] = s2[r][0, 0]
+                send[r][0, 2] = jnp.zeros(send[r].shape[2:], f32)
+
+        def late(r, a2_p0, a2_p1):
+            f_p1 = mul(load(wp[r], 0, 0, r), a2_p1)
+            store_all([(a2_out[r], a2_p0, (0, 0)), (send[r], a2_p0, (0, 0))])
+            store_all([(a2_out[r], a2_p1, (0, 1)), (send[r], f_p1, (0, 1))])
+
+        @pl.when(info[s] > 2)
+        def _():
+            for r in roles:
+                to, near, far = TOWARD[r], r, 1 - r
+                a_h1, a_p0 = load(a3[r], 0, 0), load(a3[r], 0, 1)
+                a_p1, a_p2 = load(a3p[r], 0, near), load(a3p[r], 0, far)
+                wh0 = load(wb[r], 0, 0, 0)
+                w0 = [load(wb[r], 0, c, 1) for c in range(3)]
+                w1 = [load(wp[r], 0, c, near) for c in range(3)]
+                f_p2 = mul(load(wp[r], 0, 0, far), a_p2)
+                store_all([gz(r, a_p0, load(s1[r], 0, 1), load(r1[r], 0, 0))])
+                late(
+                    r,
+                    backward(a_p0, mul(w1[0], a_p1), mul(wh0, a_h1), w0[1], w0[2], to),
+                    backward(a_p1, f_p2, mul(w0[0], a_p0), w1[1], w1[2], to),
+                )
+
+        @pl.when(info[s] <= 2)
+        def _():
+            for r in roles:
+                late(r, load(a3[r], 0, 1), load(a3p[r], 0, r))
+
+        @pl.when(info[s] > 1)
+        def _():
+            for r in roles:
+                store_all([gz(r, load(a2_out[r], 0, 0), load(i1p[r], 0, r), load(i1b[r], 0, 0))])
+
+    return named(kernel, "outer_3", role)
 
 
 def inner_4(info, s, *refs):
@@ -596,49 +623,62 @@
         g[0, 0, 1] = s3[r][0, 2]
 
 
-def outer_4(info, s, *refs):
-    r3, wb, wp, s3, a1p = (refs[2 * i : 2 * i + 2] for i in range(5))
-    total_in, total_out, *outs = refs[10:14]
-    total, a1s, sems = refs[14:]
-    odd = info[4]
-
-    def sent(r):
-        return pltpu.make_async_copy(a1s.at[s, r], outs[r].at[s], sems.at[s, r])
-
-    @pl.when(s == 0)
-    def _():
-        for j in range(2, 6):
-            total[:, natural(odd, j)] = total_in[:, j - 2]
-        for j in (0, 1, 6, 7):
-            total[:, j] = jnp.zeros((8, 8, COLS), f32)
-
-    for r in ROLES:
-        to, near, far = TOWARD[r], r, 1 - r
+def outer_4(role):
+    to, near, far = TOWARD[role], role, 1 - role
+
+    def kernel(info, s, *refs):
+        r3, wb, wp, s3, a1p, total_in, total_out, a1_out = refs[:8]
+        total, a1s, sems = refs[8:]
+        odd = info[4]
+        first = 2 - 2 * odd
+
+        def sent(at):
+            return pltpu.make_async_copy(a1s.at[at], a1_out.at[at], sems.at[at])
+
+        def six():
+            return pltpu.make_async_copy(total_in, total_out.at[:, pl.ds(first, 6)], sems.at[4])
+
+        @pl.when(s == 0)
+        def _():
+            if role == 0:
+                six().start()
+                total[...] = jnp.zeros(total.shape, f32)
+            else:
+                for j in range(2, 6):
+                    total_out[:, natural(odd, j) - first] = total_in[:, j - 2]
+                for j in (6, 7):
+                    total_out[:, natural(odd, j) - first] = jnp.zeros((8, 8, COLS), f32)
 
         active = (info[s] > 1).astype(f32)
-        a_h1, a_p0 = load(r3[r], 0, 0), load(s3[r], 0, 0)
-        f_h2, f_p1 = scale(load(r3[r], 0, 1), -1.0), load(s3[r], 0, 1)
-        wh = [load(wb[r], 0, c, 0) for c in range(3)]
-        w0 = [load(wb[r], 0, c, 1) for c in range(3)]
+        a_h1, a_p0 = load(r3, 0, 0), load(s3, 0, 0)
+        f_h2, f_p1 = scale(load(r3, 0, 1), -1.0), load(s3, 0, 1)
+        wh = [load(wb, 0, c, 0) for c in range(3)]
+        w0 = [load(wb, 0, c, 1) for c in range(3)]
         b_h1 = backward(a_h1, mul(w0[0], a_p0), f_h2, wh[1], wh[2], to, active)
         b_p0 = backward(a_p0, f_p1, mul(wh[0], a_h1), w0[1], w0[2], to, active)
-        store_all([(a1s, b_h1, (s, r, 0)), (a1s, b_p0, (s, r, 1))])
-        w1 = [load(wp[r], 0, c, near) for c in range(3)]
-        b_p1, b_p2 = load(a1p[r], 0, near), load(a1p[r], 0, far)
+        store_all([(a1s, b_h1, (s, 0)), (a1s, b_p0, (s, 1))])
+        sent(s).start()
+        w1 = [load(wp, 0, c, near) for c in range(3)]
+        b_p1, b_p2 = load(a1p, 0, near), load(a1p, 0, far)
         c_p0 = backward(b_p0, mul(w1[0], b_p1), mul(wh[0], b_h1), w0[1], w0[2], to)
-        c_p1 = backward(b_p1, mul(load(wp[r], 0, 0, far), b_p2), mul(w0[0], b_p0), w1[1], w1[2], to)
+        c_p1 = backward(b_p1, mul(load(wp, 0, 0, far), b_p2), mul(w0[0], b_p0), w1[1], w1[2], to)
         for k, value in enumerate((c_p0, c_p1)):
-            add_t(total, value, natural(odd, k if r == 0 else 7 - k))
-        sent(r).start()
-
-    @pl.when(s == 3)
-    def _():
-        last = pltpu.make_async_copy(total, total_out, sems.at[4, 0])
-        last.start()
-        for at in range(4):
-            for r in ROLES:
-                pltpu.make_async_copy(a1s.at[at, r], outs[r].at[at], sems.at[at, r]).wait()
-        last.wait()
+            if role == 0:
+                add_t(total, value, natural(odd, k) - 6 * odd)
+            else:
+                add_t(total_out, value, natural(odd, 7 - k) - first)
+
+        @pl.when(s == 3)
+        def _():
+            if role == 0:
+                last = pltpu.make_async_copy(total, total_out.at[:, pl.ds(6 * odd, 2)], sems.at[5])
+                last.start()
+                last.wait()
+                six().wait()
+            for at in range(4):
+                sent(at).wait()
+
+    return named(kernel, "outer_4", role)
 
 
 def final(mid, inner, outer, turn):
@@ -647,7 +687,8 @@
 
 def finish(info, s, *refs):
     r3, a1b, gb, i1b = (refs[2 * i : 2 * i + 2] for i in range(4))
-    t, dt, g_full, mg, made, sems = refs[8:]
+    th, (t, dt, g_full, mg, made, sems, halo) = refs[8:10], refs[10:]
+    slopes_h1 = halo_slopes(s, th, halo)
     odd = info[4]
     sign = (1 - 2 * odd).astype(f32)
     slot = lax.rem(s, 2)
@@ -672,8 +713,8 @@
         n0, n1 = (natural(odd, k if r == 0 else 7 - k) for k in (0, 1))
         inside = info[5].astype(f32) if r == 0 else 1.0
         step_one = (info[s] > 1).astype(f32)
-        th2, th1, tp0, tp1 = (t_load(t, k, r) for k in (-2, -1, 0, 1))
-        slopes = t_slopes(dt, -1, r)
+        th1, th2, tp0, tp1 = load(th[r], 0), load(th[r], 1), t_load(t, 0, r), t_load(t, 1, r)
+        slopes = slopes_h1[r]
         a_one = scale(load(r3[r], 0, 0), step_one)
         i_h1 = load(i1b[r], 0, 0)
         b_h1, b_p0 = load(a1b[r], 0, 0), load(a1b[r], 0, 1)
@@ -790,16 +831,13 @@
     core_pairs = [(i, i ^ 1) for i in range(count)]
     chip_pairs = [(i, ((i + 1) ^ 1) - 1) for i in range(1, count - 1)]
 
-    def swap(sides):
-        return lax.ppermute(sides[0], "space", chip_pairs), lax.ppermute(sides[1], "space", core_pairs)
+    def swap(array, role):
+        return lax.ppermute(array, "space", (chip_pairs, core_pairs)[role])
 
     group = lax.axis_index("subj")
     inside = jnp.logical_and(place > 0, place < count - 1)
     info = jnp.concatenate([step_count, jnp.stack([odd, inside, group]).astype(jnp.int32)])
 
-    def ends(array, dim):
-        return tuple(lax.dynamic_slice_in_dim(array, at, 2, dim) for at in (6 * odd, 6 - 6 * odd))
-
     def shape(*lead):
         return (step_count.shape[0],) + lead + PLANE
 
@@ -821,31 +859,49 @@
     def partner(array, by):
         return lax.ppermute(array, "subj", [(i, i ^ by) for i in range(groups)])
 
-    across, ms = lax.optimization_barrier((partner(template, 1), ends(momentum, 2)))
-    own = jnp.stack([template, across])
-    t_halo, ms = lax.optimization_barrier((swap(ends(own, 1)), ms))
-    mr = swap(ms)
-    wide = jnp.concatenate([t_halo[0], own, t_halo[1]], axis=1)
-    wide, late_info = lax.optimization_barrier((wide, info))
-    rows = [wide] + [partner(wide, by) for by in (2, 4, 6)]
+    ends = [lax.dynamic_slice_in_dim(momentum, at, 2, 2) for at in (6 * odd, 6 - 6 * odd)]
+    across, ends = lax.optimization_barrier((partner(template, 1), ends))
+    mr = [swap(ends[r], r) for r in ROLES]
+    own, later = lax.optimization_barrier((jnp.stack([template, across]), momentum))
+    rows = [own] + [partner(own, by) for by in (2, 4, 6)]
     w_in, w_edge, m_edge = call(
-        velocity_inner, late_info, [(momentum, stream)], [out(3, 6), out(3, 2), out(3, 2)], us=5
+        velocity_inner, info, [(later, stream)], [out(3, 6), out(3, 2), out(3, 2)], us=5
     )
-    t, dt = call(
-        template_planes, info, [(x, whole) for x in rows], [((12,) + PLANE, whole), ((2, 10) + PLANE, whole)], us=1
+    rows, w_in, w_edge, m_edge = lax.optimization_barrier((rows, w_in, w_edge, m_edge))
+    two_planes = ((2,) + PLANE, whole)
+    t, dt, *t_sides = call(
+        template_planes,
+        info,
+        [(x, whole) for x in rows],
+        [((8,) + PLANE, whole), ((2, 8) + PLANE, whole), two_planes, two_planes],
+        us=1,
     )
     tdt = [(t, whole), (dt, whole)]
+    th = [swap(t_sides[r], r) for r in ROLES]
+    slopes = pltpu.VMEM((2, 2) + PLANE, f32)
     i1_in, i2_in = call(inner_1, info, [(w_in, one)] + tdt, [out(6), out(4)], us=3)
-    *made, s1z, s1c = call(
-        outer_1,
-        info,
-        both(mr, stream) + [(m_edge, one), (w_edge, one)] + tdt + near(w_in) + near(i1_in),
-        out2(3, 2) + out2(2) + out2(2),
-        us=5,
-    )
-    wb, i1b = made[:2], made[2:]
-    s1 = (s1z, s1c)
-    r1 = swap(s1)
+
+    def side(r, *arrays):
+        return [(x[r], one) if isinstance(x, (list, tuple)) else (x, pair((0, 4)[r])) for x in arrays]
+
+    def sides(kernel, shared, arrays, *more, waits=None):
+        made = [None, None]
+        for r in (1, 0):
+            made[r] = list(call(kernel(r), info, shared(r) + side(r, *arrays), *more))
+            if r == 1 and waits is not None:
+                arrays[waits][0], made[1][0] = lax.optimization_barrier((arrays[waits][0], made[1][0]))
+        return [list(pair) for pair in zip(*made)]
+
+    def exchange(pair):
+        return [swap(pair[r], r) for r in ROLES]
+
+    wb, i1b, s1 = [None, None], [None, None], [None, None]
+    for r in (1, 0):
+        given = [(m_edge, one), (w_edge, one)] + tdt + [(mr[r], stream), (th[r], whole)] + side(r, w_in, i1_in)
+        wb[r], i1b[r], s1[r] = call(outer_1(r), info, given, [out(3, 2), out(2), out(2)], [slopes], 3)
+        if r == 1:
+            mr[0], s1[1] = lax.optimization_barrier((mr[0], s1[1]))
+    r1 = exchange(s1)
     i3_in, i4_in, a4_in = call(
         inner_2,
         info,
@@ -854,15 +910,10 @@
         [planes(8)],
         us=4,
     )
-    made = call(
-        outer_2,
-        info,
-        both(r1, one) + both(wb, one) + near(w_in) + both(s1, one) + near(i3_in) + [(targets, one)],
-        out2(2) + out2(2) + out2(1) + out2(2),
-        us=3,
+    i3b, i4b, a4b, s2 = sides(
+        outer_2, lambda r: [(targets, one)], [r1, wb, w_in, s1, i3_in], [out(2), out(2), out(1), out(2)], [], 2, waits=0
     )
-    i3b, i4b, a4b, s2 = (made[2 * i : 2 * i + 2] for i in range(4))
-    r2 = swap(s2)
+    r2 = exchange(s2)
     a3_in, a2_in, g_in, warped = call(
         inner_3,
         info,
@@ -880,17 +931,12 @@
         [planes(8)] * 3 + [pltpu.SemaphoreType.DMA((8,))],
         us=7,
     )
-    images = both(i3b, one) + near(i3_in) + both(r1, one) + both(s1, one) + both(i1b, one) + near(i1_in)
-    made = call(
-        outer_3,
-        info,
-        both(r2, one) + both(wb, one) + near(w_in) + both(s2, one) + near(a3_in) + images,
-        out2(2) + out2(2) + out2(3),
-        us=2,
+    images = [i3b, i3_in, r1, s1, i1b, i1_in]
+    a3b, a2b, s3 = sides(
+        outer_3, lambda r: [], [r2, wb, w_in, s2, a3_in] + images, [out(2), out(2), out(3)], [], 2, waits=0
     )
-    a3b, a2b, s3 = (made[2 * i : 2 * i + 2] for i in range(3))
-    r3 = swap(s3)
-    small, tile = (groups, 4, 8, COLS), (groups, 8, 8, COLS)
+    r3 = exchange(s3)
+    small, six, tile = ((groups, n, 8, COLS) for n in (4, 6, 8))
     a1_in, total, g_full, *gb = call(
         inner_4,
         info,
@@ -902,28 +948,37 @@
         + both(a3b, one)
         + both(s2, one)
         + both(s3, one)
-        + images
+        + both(i3b, one)
+        + near(i3_in)
+        + both(r1, one)
+        + both(s1, one)
+        + both(i1b, one)
+        + near(i1_in)
         + tdt
         + [(g_in, one)],
         [out(6), (small, whole), out(3, 6)] + out2(3, 2),
         [planes(8)] * 2,
         us=5,
     )
-    total, *a1b = call(
-        outer_4,
-        info,
-        both(r3, one) + both(wb, one) + near(w_in) + both(s3, one) + near(a1_in) + [(total, whole)],
-        [(tile, None)] + [(shape(2), None)] * 2,
-        [pltpu.VMEM(tile, f32), pltpu.VMEM((4, 2, 2) + PLANE, f32), pltpu.SemaphoreType.DMA((5, 2))],
-        us=3,
-    )
+    a1b = [None, None]
+    for r in (1, 0):
+        total, a1b[r] = call(
+            outer_4(r),
+            info,
+            side(r, r3, wb, w_in, s3, a1_in) + [(total, whole)],
+            [(six, whole) if r else (tile, None), (shape(2), None)],
+            [pltpu.VMEM((groups, 2, 8, COLS), f32), pltpu.VMEM((4, 2) + PLANE, f32), pltpu.SemaphoreType.DMA((6,))],
+            2,
+        )
+        if r == 1:
+            r3[0], total = lax.optimization_barrier((r3[0], total))
     parts = lax.all_to_all(total, "subj", 0, 0)
     (momentum_gradient,) = call(
         finish,
         info,
-        both(r3, stream) + both(a1b, stream) + both(gb, stream) + both(i1b, stream) + tdt + [(g_full, stream)],
+        both(r3, stream) + both(a1b, stream) + both(gb, stream) + both(i1b, stream) + both(th, whole) + tdt + [(g_full, stream)],
         [(shape(3, 8), None)],
-        [pltpu.VMEM((2, 3, 8) + PLANE, f32), pltpu.SemaphoreType.DMA((2,))],
+        [pltpu.VMEM((2, 3, 8) + PLANE, f32), pltpu.SemaphoreType.DMA((2,)), slopes],
         us=6,
         mib=14,
     )

time: 108 us -> 100 us (0.926)
  waiting for transfers between devices: 20.6 us -> 9.33 us
  Pallas kernels: 36.1 us -> 43.9 us
  starting transfers between devices: 44.1 us -> 39.2 us
    pallas_call x11 -> x15, Pallas kernels: 36.1 us -> 43.9 us  [call(): pl.pallas_call(body, grid=(subjects,) if streams else (), in_specs=[pl.Bl...]
    ppermute x10, waiting for transfers between devices: 16.2 us -> 8.68 us  [swap(): return lax.ppermute(array, 'space', (chip_pairs, core_pairs)[role])]
    ppermute x4, waiting for transfers between devices: 4.34 us -> 0.65 us  [partner(): return lax.ppermute(array, 'subj', [(i, i ^ by) for i in range(groups)])]
    ppermute x10, starting transfers between devices: 29.7 us -> 26.2 us  [swap(): return lax.ppermute(array, 'space', (chip_pairs, core_pairs)[role])]
    all_to_all x1, starting transfers between devices: 8.67 us -> 7.34 us  [shards(): parts = lax.all_to_all(total, 'subj', 0, 0)]
  transfers between devices with their start and end apart: 15 -> 15, of which waited for: 8 -> 5; matrix products, arithmetic and copies ran while one was open for 4% -> 4% of each run, Pallas kernels for 25% -> 42%
where the time goes in v3:
time: 100 us; the launch traced here: 98.7 us
  Pallas kernels  43.9 us (44%)
  starting transfers between devices  39.2 us (39%)
  waiting for transfers between devices  9.33 us (9%)
  local copies, waits for them, and re-layouts  4.53 us (5%)
  between operations  1.02 us (1%)
    pallas_call x15, Pallas kernels, call(): pl.pallas_call(body, grid=(subjects,) if streams else (), in_specs=[pl.Bl...  43.9 us
    ppermute x10, starting transfers between devices, swap(): return lax.ppermute(array, 'space', (chip_pairs, core_pairs)[role])  26.2 us
    ppermute x10, waiting for transfers between devices, swap(): return lax.ppermute(array, 'space', (chip_pairs, core_pairs)[role])  8.68 us
    all_to_all x1, starting transfers between devices, shards(): parts = lax.all_to_all(total, 'subj', 0, 0)  7.34 us
    ppermute x4, starting transfers between devices, partner(): return lax.ppermute(array, 'subj', [(i, i ^ by) for i in range(groups)])  5.66 us
    dynamic_slice x1, local copies, waits for them, and re-layouts, shards(): lax.dynamic_slice_in_dim(momentum, at, 2, 2)  3.93 us
  transfers between devices with their start and end apart: 15, of which 5 were waited for; matrix products, arithmetic and copies ran while one was open for 4% of the time, Pallas kernels for 42%

profile of v3, /device:TPU:6, one launch (start us, length us, event | category | flops | bytes accessed | tf_op | source)
XLA Modules:
  0.0 98.7 jit_solution(4448998970591815385)
XLA Ops:
  0.6 1.5 %collective-permute-start = (f32[8,8,256]{2,1,0:T(8,128)}, f32[8,8,256]{2,1,0:T(8,128)S(1)}, u32[]{:S(2)}, u32[]{:S(2)}) collective-permute-start(f32[8,8,256]{2,1,0:T(8,128)} %param.4), channel_id=1, source_target_pairs={{0,1},{1,0},{2,3},{3,2},{4,5},{5,4},{6,7},{7,6},{8,9},{9,8},{10,11... | collective-permute-start | bytes 196616 | tf_op jit(solution)/shard_map/ppermute | solution.py:860
  2.1 3.9 %constant_dynamic-slice_fusion = (f32[4,3,2,64,256]{4,3,2,1,0:T(8,128)}, f32[4,3,2,64,256]{4,3,2,1,0:T(8,128)}) fusion(f32[4,3,8,64,256]{4,3,2,1,0:T(8,128)} %refs_0_.2, s32[]{:T(128)S(6)} %select_n.15, s32[]{:T(128)S(6)} %select_n.14), kind=kLoop, calls=%fused_computation.2 | loop fusion | bytes 6291464 | tf_op jit(solution)/shard_map/dynamic_slice | solution.py:862
  6.0 0.6 collective-permute-done
  6.7 0.0 collective-permute-start.5
  6.7 6.3 %collective-permute-start.4 = (f32[4,3,2,64,256]{4,3,2,1,0:T(8,128)}, f32[4,3,2,64,256]{4,3,2,1,0:T(8,128)}, u32[]{:S(2)}, u32[]{:S(2)}) collective-permute-start(f32[4,3,2,64,256]{4,3,2,1,0:T(8,128)} %get-tuple-element.83), channel_id=1, source_target_pairs={{8,16},{16,8},{24,32},{32,24},{40,48},{48,40},{56,64},{64,56},{72,... | collective-permute-start | bytes 4718600 | tf_op jit(solution)/shard_map/ppermute | solution.py:835
  13.0 3.1 %collective-permute-start.3 = (f32[2,8,8,256]{3,2,1,0:T(8,128)S(1)}, f32[2,8,8,256]{3,2,1,0:T(8,128)S(1)}, u32[]{:S(2)}, u32[]{:S(2)}) collective-permute-start(f32[2,8,8,256]{3,2,1,0:T(8,128)S(1)} %pad_maximum_fusion.refs_0_), channel_id=1, source_target_pairs={{0,6},{1,7},{2,4},{3,5},{4,2},{5,3},{6,0},{7,1},{8,14},{9,15},{10,... | collective-permute-start | bytes 393224 | tf_op jit(solution)/shard_map/ppermute | solution.py:860
  16.1 0.6 collective-permute-start.2
  16.8 0.5 collective-permute-start.1
  17.2 0.1 pad_add_fusion.info_ref
  17.3 5.7 %velocity_inner.1 = (f32[4,3,6,64,256]{4,3,2,1,0:T(8,128)S(1)}, f32[4,3,2,64,256]{4,3,2,1,0:T(8,128)S(1)}, f32[4,3,2,64,256]{4,3,2,1,0:T(8,128)S(1)}) custom-call(s32[7]{0:T(128)S(1)} %pad_add_fusion.info_ref, f32[4,3,8,64,256]{4,3,2,1,0:T(8,128)} %refs_0_.2), custom_call_target="tpu_custom_call" | custom-call | bytes 16500000 | tf_op jit(solution)/shard_map/velocity_inner/pallas_call | solution.py:813
  23.0 0.0 collective-permute-done.3.refs_3_
  23.0 0.0 collective-permute-done.2.refs_2_
  23.0 0.0 collective-permute-done.1.refs_1_
  23.0 1.0 template_planes.1
  24.0 0.1 collective-permute-start.6
  24.1 3.4 %collective-permute-start.7 = (f32[2,64,256]{2,1,0:T(8,128)S(1)}, f32[2,64,256]{2,1,0:T(8,128)S(1)}, u32[]{:S(2)}, u32[]{:S(2)}) collective-permute-start(f32[2,64,256]{2,1,0:T(8,128)S(1)} %get-tuple-element.89), channel_id=1, source_target_pairs={{8,16},{16,8},{24,32},{32,24},{40,48},{48,40},{56,64},{64,56},{72,... | collective-permute-start | bytes 393224 | tf_op jit(solution)/shard_map/ppermute | solution.py:835
  27.5 1.7 %inner_1.1 = (f32[4,6,64,256]{3,2,1,0:T(8,128)S(1)}, f32[4,4,64,256]{3,2,1,0:T(8,128)S(1)}) custom-call(s32[7]{0:T(128)S(1)} %pad_add_fusion.info_ref, f32[4,3,6,64,256]{4,3,2,1,0:T(8,128)S(1)} %get-tuple-element.74.refs_0_.refs_6_.refs_3_.refs_2_, f32[8,64,256]{2,1,0:T(8,128)S(1)} %get-tuple-element.81.refs_1_.refs_2_.refs_24_.refs_10_, ...), custom_call_target="tpu_custom_call" | custom-call | bytes 9900000 | tf_op jit(solution)/shard_map/inner_1/pallas_call | solution.py:813
  29.3 0.0 collective-permute-done.6.refs_5_.refs_9_
  29.3 0.0 collective-permute-done.5.refs_4_
  29.3 3.1 %outer_1_core.1 = (f32[4,3,2,64,256]{4,3,2,1,0:T(8,128)S(1)}, f32[4,2,64,256]{3,2,1,0:T(8,128)S(1)}, f32[4,2,64,256]{3,2,1,0:T(8,128)S(1)}) custom-call(s32[7]{0:T(128)S(1)} %pad_add_fusion.info_ref, f32[4,3,2,64,256]{4,3,2,1,0:T(8,128)S(1)} %get-tuple-element.75.refs_0_, f32[4,3,2,64,256]{4,3,2,1,0:T(8,128)S(1)} %get-tuple-element.76.refs_1_, ...), custom_call_target="tpu_custom_call" | custom-call | bytes 9900000 | tf_op jit(solution)/shard_map/outer_1_core/pallas_call | solution.py:813
  32.4 0.0 collective-permute-done.4.refs_4_
  32.4 0.0 copy-start
  32.4 0.1 collective-permute-start.9
  32.5 0.2 collective-permute-done.7.refs_5_.refs_8_
  32.7 3.5 %outer_1_chip.1 = (f32[4,3,2,64,256]{4,3,2,1,0:T(8,128)S(1)}, f32[4,2,64,256]{3,2,1,0:T(8,128)S(1)}, f32[4,2,64,256]{3,2,1,0:T(8,128)S(1)}) custom-call(s32[7]{0:T(128)S(1)} %pad_add_fusion.info_ref, f32[4,3,2,64,256]{4,3,2,1,0:T(8,128)S(1)} %get-tuple-element.75.refs_0_, f32[4,3,2,64,256]{4,3,2,1,0:T(8,128)S(1)} %get-tuple-element.76.refs_1_, ...), custom_call_target="tpu_custom_call" | custom-call | bytes 9900000 | tf_op jit(solution)/shard_map/outer_1_chip/pallas_call | solution.py:813
  36.2 5.4 %collective-permute-start.8 = (f32[4,2,64,256]{3,2,1,0:T(8,128)S(1)}, f32[4,2,64,256]{3,2,1,0:T(8,128)S(1)}, u32[]{:S(2)}, u32[]{:S(2)}) collective-permute-start(f32[4,2,64,256]{3,2,1,0:T(8,128)S(1)} %get-tuple-element.92.refs_2_.refs_4_.refs_12_.refs_8_.refs_19_), channel_id=1, source_target_pairs={{8,16},{16,8},{24,32},{32,24},{40,48},{48,40},{56,64},{64,56},{72,... | collective-permute-start | bytes 1572872 | tf_op jit(solution)/shard_map/ppermute | solution.py:835
  41.7 1.4 %inner_2.1 = (f32[4,6,64,256]{3,2,1,0:T(8,128)S(1)}, f32[4,4,64,256]{3,2,1,0:T(8,128)S(1)}, f32[4,4,64,256]{3,2,1,0:T(8,128)S(1)}) custom-call(s32[7]{0:T(128)S(1)} %pad_add_fusion.info_ref, f32[4,3,6,64,256]{4,3,2,1,0:T(8,128)S(1)} %get-tuple-element.74.refs_0_.refs_6_.refs_3_.refs_2_, f32[4,4,64,256]{3,2,1,0:T(8,128)S(1)} %get-tuple-element.94.refs_1_.refs_11_, ...), custom_call_target="tpu_custom_call" | custom-call | bytes 13200000 | tf_op jit(solution)/shard_map/inner_2/pallas_call | solution.py:813
  43.1 1.0 %outer_2_core.1 = (f32[4,2,64,256]{3,2,1,0:T(8,128)S(1)}, f32[4,2,64,256]{3,2,1,0:T(8,128)S(1)}, f32[4,1,64,256]{3,2,1,0:T(8,128)S(1)}, f32[4,2,64,256]{3,2,1,0:T(8,128)S(1)}) custom-call(s32[7]{0:T(128)S(1)} %pad_add_fusion.info_ref, f32[4,8,64,256]{3,2,1,0:T(8,128)S(1)} %copy-done, f32[4,2,64,256]{3,2,1,0:T(8,128)S(1)} %collective-permute-done.9.refs_1_.refs_7_.refs_18_, ...), custom_call_target="tpu_custom_call" | custom-call | bytes 6600000 | tf_op jit(solution)/shard_map/outer_2_core/pallas_call | solution.py:813
  44.2 4.7 %collective-permute-done.8.refs_1_.refs_7_.refs_17_ = f32[4,2,64,256]{3,2,1,0:T(8,128)S(1)} collective-permute-done((f32[4,2,64,256]{3,2,1,0:T(8,128)S(1)}, f32[4,2,64,256]{3,2,1,0:T(8,128)S(1)}, u32[]{:S(2)}, u32[]{:S(2)}) %collective-permute-start.8) | collective-permute-done | bytes 524320 | tf_op jit(solution)/shard_map/ppermute | solution.py:835
  48.8 0.0 collective-permute-start.11
  48.8 1.0 %outer_2_chip.1 = (f32[4,2,64,256]{3,2,1,0:T(8,128)S(1)}, f32[4,2,64,256]{3,2,1,0:T(8,128)S(1)}, f32[4,1,64,256]{3,2,1,0:T(8,128)S(1)}, f32[4,2,64,256]{3,2,1,0:T(8,128)S(1)}) custom-call(s32[7]{0:T(128)S(1)} %pad_add_fusion.info_ref, f32[4,8,64,256]{3,2,1,0:T(8,128)S(1)} %copy-done, f32[4,2,64,256]{3,2,1,0:T(8,128)S(1)} %collective-permute-done.8.refs_1_.refs_7_.refs_17_, ...), custom_call_target="tpu_custom_call" | custom-call | bytes 6600000 | tf_op jit(solution)/shard_map/outer_2_chip/pallas_call | solution.py:813
  49.9 5.4 %collective-permute-start.10 = (f32[4,2,64,256]{3,2,1,0:T(8,128)S(1)}, f32[4,2,64,256]{3,2,1,0:T(8,128)S(1)}, u32[]{:S(2)}, u32[]{:S(2)}) collective-permute-start(f32[4,2,64,256]{3,2,1,0:T(8,128)S(1)} %get-tuple-element.98.refs_3_.refs_10_), channel_id=1, source_target_pairs={{8,16},{16,8},{24,32},{32,24},{40,48},{48,40},{56,64},{64,56},{72,... | collective-permute-start | bytes 1572872 | tf_op jit(solution)/shard_map/ppermute | solution.py:835
  55.3 4.1 %inner_3.1 = (f32[4,6,64,256]{3,2,1,0:T(8,128)S(1)}, f32[4,4,64,256]{3,2,1,0:T(8,128)S(1)}, f32[4,3,6,64,256]{4,3,2,1,0:T(8,128)S(1)}, f32[4,8,64,256]{3,2,1,0:T(8,128)}) custom-call(s32[7]{0:T(128)S(1)} %pad_add_fusion.info_ref, f32[4,3,6,64,256]{4,3,2,1,0:T(8,128)S(1)} %get-tuple-element.74.refs_0_.refs_6_.refs_3_.refs_2_, ...), custom_call_target="tpu_custom_call" | custom-call | bytes 23100000 | tf_op jit(solution)/shard_map/inner_3/pallas_call | solution.py:813
  59.5 1.1 %outer_3_core.1 = (f32[4,2,64,256]{3,2,1,0:T(8,128)S(1)}, f32[4,2,64,256]{3,2,1,0:T(8,128)S(1)}, f32[4,3,64,256]{3,2,1,0:T(8,128)S(1)}) custom-call(s32[7]{0:T(128)S(1)} %pad_add_fusion.info_ref, f32[4,2,64,256]{3,2,1,0:T(8,128)S(1)} %collective-permute-done.11.refs_0_.refs_7_, f32[4,3,2,64,256]{4,3,2,1,0:T(8,128)S(1)} %get-tuple-element.91.refs_2_.refs_1_, ...), custom_call_target="tpu_custom_call" | custom-call | bytes 6600000 | tf_op jit(solution)/shard_map/outer_3_core/pallas_call | solution.py:813
  60.6 1.9 %collective-permute-done.10.refs_0_.refs_6_ = f32[4,2,64,256]{3,2,1,0:T(8,128)S(1)} collective-permute-done((f32[4,2,64,256]{3,2,1,0:T(8,128)S(1)}, f32[4,2,64,256]{3,2,1,0:T(8,128)S(1)}, u32[]{:S(2)}, u32[]{:S(2)}) %collective-permute-start.10) | collective-permute-done | bytes 524320 | tf_op jit(solution)/shard_map/ppermute | solution.py:835
  62.5 0.0 collective-permute-start.13
  62.5 1.1 %outer_3_chip.1 = (f32[4,2,64,256]{3,2,1,0:T(8,128)S(1)}, f32[4,2,64,256]{3,2,1,0:T(8,128)S(1)}, f32[4,3,64,256]{3,2,1,0:T(8,128)S(1)}) custom-call(s32[7]{0:T(128)S(1)} %pad_add_fusion.info_ref, f32[4,2,64,256]{3,2,1,0:T(8,128)S(1)} %collective-permute-done.10.refs_0_.refs_6_, f32[4,3,2,64,256]{4,3,2,1,0:T(8,128)S(1)} %get-tuple-element.90.refs_2_.refs_1_, ...), custom_call_target="tpu_custom_call" | custom-call | bytes 6600000 | tf_op jit(solution)/shard_map/outer_3_chip/pallas_call | solution.py:813
  63.6 5.4 %collective-permute-start.12 = (f32[4,3,64,256]{3,2,1,0:T(8,128)S(1)}, f32[4,3,64,256]{3,2,1,0:T(8,128)S(1)}, u32[]{:S(2)}, u32[]{:S(2)}) collective-permute-start(f32[4,3,64,256]{3,2,1,0:T(8,128)S(1)} %get-tuple-element.114.refs_12_.refs_3_), channel_id=1, source_target_pairs={{8,16},{16,8},{24,32},{32,24},{40,48},{48,40},{56,64},{64,56},{72,... | collective-permute-start | bytes 2359304 | tf_op jit(solution)/shard_map/ppermute | solution.py:835
  69.0 4.5 %inner_4.1 = (f32[4,6,64,256]{3,2,1,0:T(8,128)S(1)}, f32[8,4,8,256]{3,2,1,0:T(8,128)S(1)}, f32[4,3,6,64,256]{4,3,2,1,0:T(8,128)S(1)}, f32[4,3,2,64,256]{4,3,2,1,0:T(8,128)S(1)}, f32[4,3,2,64,256]{4,3,2,1,0:T(8,128)S(1)}) custom-call(s32[7]{0:T(128)S(1)} %pad_add_fusion.info_ref, f32[4,3,6,64,256]{4,3,2,1,0:T(8,128)S(1)} %get-tuple-element.74.refs_0_.refs_6_.refs_3_.refs_2_, ...), custom_call_target="tpu_custom_call" | custom-call | bytes 16500000 | tf_op jit(solution)/shard_map/inner_4/pallas_call | solution.py:813
  73.6 0.0 collective-permute-done.13.refs_0_.refs_1_
  73.6 2.9 %outer_4_core.1 = (f32[8,6,8,256]{3,2,1,0:T(8,128)S(1)}, f32[4,2,64,256]{3,2,1,0:T(8,128)}) custom-call(s32[7]{0:T(128)S(1)} %pad_add_fusion.info_ref, f32[4,3,64,256]{3,2,1,0:T(8,128)S(1)} %collective-permute-done.13.refs_0_.refs_1_, f32[4,3,2,64,256]{4,3,2,1,0:T(8,128)S(1)} %get-tuple-element.91.refs_2_.refs_1_, ...), custom_call_target="tpu_custom_call" | custom-call | bytes 6600000 | tf_op jit(solution)/shard_map/outer_4_core/pallas_call | solution.py:813
  76.6 0.3 copy-done.7
  76.9 0.2 copy-done.4
  77.1 1.9 %collective-permute-done.12.refs_0_ = f32[4,3,64,256]{3,2,1,0:T(8,128)S(1)} collective-permute-done((f32[4,3,64,256]{3,2,1,0:T(8,128)S(1)}, f32[4,3,64,256]{3,2,1,0:T(8,128)S(1)}, u32[]{:S(2)}, u32[]{:S(2)}) %collective-permute-start.12) | collective-permute-done | bytes 786464 | tf_op jit(solution)/shard_map/ppermute | solution.py:835
  79.0 2.3 %outer_4_chip.1 = (f32[8,8,8,256]{3,2,1,0:T(8,128)}, f32[4,2,64,256]{3,2,1,0:T(8,128)}) custom-call(s32[7]{0:T(128)S(1)} %pad_add_fusion.info_ref, f32[4,3,64,256]{3,2,1,0:T(8,128)S(1)} %collective-permute-done.12.refs_0_, f32[4,3,2,64,256]{4,3,2,1,0:T(8,128)S(1)} %get-tuple-element.90.refs_2_.refs_1_, ...), custom_call_target="tpu_custom_call" | custom-call | bytes 6600000 | tf_op jit(solution)/shard_map/outer_4_chip/pallas_call | solution.py:813
  81.3 7.3 %all-to-all-start = ((f32[8,8,8,256]{3,2,1,0:T(8,128)}), f32[8,8,8,256]{3,2,1,0:T(8,128)S(1)}, u32[]{:S(2)}, u32[]{:S(2)}) async-start(f32[8,8,8,256]{3,2,1,0:T(8,128)} %get-tuple-element.127), calls=%async_computation | async-start | bytes 1048576 | tf_op jit(solution)/shard_map/all_to_all | solution.py:975
  88.7 9.4 %finish.1 = f32[4,3,8,64,256]{4,3,2,1,0:T(8,128)} custom-call(s32[7]{0:T(128)S(1)} %pad_add_fusion.info_ref, f32[4,3,64,256]{3,2,1,0:T(8,128)} %copy-done.5, f32[4,3,64,256]{3,2,1,0:T(8,128)} %copy-done.4, f32[4,2,64,256]{3,2,1,0:T(8,128)} %get-tuple-element.128.refs_2_, f32[4,2,64,256]{3,2,1,0:T(8,128)} %get-tuple-element.129.refs_3_, ...), custom_call_target="tpu_custom_call" | custom-call | bytes 19800000 | tf_op jit(solution)/shard_map/finish/pallas_call | solution.py:813
  98.1 0.7 reduce_sum.9
  (25 shorter events, 0.1 us)
Async XLA Ops:
  0.6 6.1 %collective-permute-start = (f32[8,8,256]{2,1,0:T(8,128)}, f32[8,8,256]{2,1,0:T(8,128)S(1)}, u32[]{:S(2)}, u32[]{:S(2)}) collective-permute-start(f32[8,8,256]{2,1,0:T(8,128)} %param.4), channel_id=1, source_target_pairs={{0,1},{1,0},{2,3},{3,2},{4,5},{5,4},{6,7},{7,6},{8,9},{9,8},{10,11... | collective-permute-start | bytes 196616 | tf_op jit(solution)/shard_map/ppermute | solution.py:860
  2.1 10.9 %copy-start.10 = (f32[8,8,256]{2,1,0:T(8,128)S(1)}, f32[8,8,256]{2,1,0:T(8,128)}, u32[]{:S(2)}) copy-start(f32[8,8,256]{2,1,0:T(8,128)} %param.4) | copy-start | bytes 196612
  2.1 15.1 %copy-start.11 = (s32[4]{0:T(128)S(1)}, s32[4]{0:T(128)}, u32[]{:S(2)}) copy-start(s32[4]{0:T(128)} %param.7) | copy-start | bytes 52
  6.7 22.6 %collective-permute-start.5 = (f32[4,3,2,64,256]{4,3,2,1,0:T(8,128)}, f32[4,3,2,64,256]{4,3,2,1,0:T(8,128)}, u32[]{:S(2)}, u32[]{:S(2)}) collective-permute-start(f32[4,3,2,64,256]{4,3,2,1,0:T(8,128)} %get-tuple-element.84), channel_id=1, source_target_pairs={{0,8},{8,0},{16,24},{24,16},{32,40},{40,32},{48,56},{56,48},{64,72... | collective-permute-start | bytes 4718600 | tf_op jit(solution)/shard_map/ppermute | solution.py:835
  6.7 25.7 %collective-permute-start.4 = (f32[4,3,2,64,256]{4,3,2,1,0:T(8,128)}, f32[4,3,2,64,256]{4,3,2,1,0:T(8,128)}, u32[]{:S(2)}, u32[]{:S(2)}) collective-permute-start(f32[4,3,2,64,256]{4,3,2,1,0:T(8,128)} %get-tuple-element.83), channel_id=1, source_target_pairs={{8,16},{16,8},{24,32},{32,24},{40,48},{48,40},{56,64},{64,56},{72,... | collective-permute-start | bytes 4718600 | tf_op jit(solution)/shard_map/ppermute | solution.py:835
  13.0 9.9 %collective-permute-start.3 = (f32[2,8,8,256]{3,2,1,0:T(8,128)S(1)}, f32[2,8,8,256]{3,2,1,0:T(8,128)S(1)}, u32[]{:S(2)}, u32[]{:S(2)}) collective-permute-start(f32[2,8,8,256]{3,2,1,0:T(8,128)S(1)} %pad_maximum_fusion.refs_0_), channel_id=1, source_target_pairs={{0,6},{1,7},{2,4},{3,5},{4,2},{5,3},{6,0},{7,1},{8,14},{9,15},{10,... | collective-permute-start | bytes 393224 | tf_op jit(solution)/shard_map/ppermute | solution.py:860
  16.1 6.9 %collective-permute-start.2 = (f32[2,8,8,256]{3,2,1,0:T(8,128)S(1)}, f32[2,8,8,256]{3,2,1,0:T(8,128)S(1)}, u32[]{:S(2)}, u32[]{:S(2)}) collective-permute-start(f32[2,8,8,256]{3,2,1,0:T(8,128)S(1)} %pad_maximum_fusion.refs_0_), channel_id=1, source_target_pairs={{0,4},{1,5},{2,6},{3,7},{4,0},{5,1},{6,2},{7,3},{8,12},{9,13},{10,... | collective-permute-start | bytes 393224 | tf_op jit(solution)/shard_map/ppermute | solution.py:860
  16.8 6.2 %collective-permute-start.1 = (f32[2,8,8,256]{3,2,1,0:T(8,128)S(1)}, f32[2,8,8,256]{3,2,1,0:T(8,128)S(1)}, u32[]{:S(2)}, u32[]{:S(2)}) collective-permute-start(f32[2,8,8,256]{3,2,1,0:T(8,128)S(1)} %pad_maximum_fusion.refs_0_), channel_id=1, source_target_pairs={{0,2},{1,3},{2,0},{3,1},{4,6},{5,7},{6,4},{7,5},{8,10},{9,11},{10,... | collective-permute-start | bytes 393224 | tf_op jit(solution)/shard_map/ppermute | solution.py:860
  24.0 5.3 %collective-permute-start.6 = (f32[2,64,256]{2,1,0:T(8,128)S(1)}, f32[2,64,256]{2,1,0:T(8,128)S(1)}, u32[]{:S(2)}, u32[]{:S(2)}) collective-permute-start(f32[2,64,256]{2,1,0:T(8,128)S(1)} %get-tuple-element.85), channel_id=1, source_target_pairs={{0,8},{8,0},{16,24},{24,16},{32,40},{40,32},{48,56},{56,48},{64,72... | collective-permute-start | bytes 393224 | tf_op jit(solution)/shard_map/ppermute | solution.py:835
  24.1 8.6 %collective-permute-start.7 = (f32[2,64,256]{2,1,0:T(8,128)S(1)}, f32[2,64,256]{2,1,0:T(8,128)S(1)}, u32[]{:S(2)}, u32[]{:S(2)}) collective-permute-start(f32[2,64,256]{2,1,0:T(8,128)S(1)} %get-tuple-element.89), channel_id=1, source_target_pairs={{8,16},{16,8},{24,32},{32,24},{40,48},{48,40},{56,64},{64,56},{72,... | collective-permute-start | bytes 393224 | tf_op jit(solution)/shard_map/ppermute | solution.py:835
  32.4 36.6 %copy-start.2 = (f32[4,2,64,256]{3,2,1,0:T(8,128)}, f32[4,2,64,256]{3,2,1,0:T(8,128)S(1)}, u32[]{:S(2)}) copy-start(f32[4,2,64,256]{3,2,1,0:T(8,128)S(1)} %get-tuple-element.110.refs_9_.refs_22_.refs_7_) | copy-start | bytes 1572868
  32.4 9.2 %copy-start = (f32[4,8,64,256]{3,2,1,0:T(8,128)S(1)}, f32[4,8,64,256]{3,2,1,0:T(8,128)}, u32[]{:S(2)}) copy-start(f32[4,8,64,256]{3,2,1,0:T(8,128)} %refs_0_.4) | copy-start | bytes 6291460
  32.4 10.7 %collective-permute-start.9 = (f32[4,2,64,256]{3,2,1,0:T(8,128)S(1)}, f32[4,2,64,256]{3,2,1,0:T(8,128)S(1)}, u32[]{:S(2)}, u32[]{:S(2)}) collective-permute-start(f32[4,2,64,256]{3,2,1,0:T(8,128)S(1)} %get-tuple-element.93.refs_3_.refs_4_.refs_13_.refs_8_.refs_20_), channel_id=1, source_target_pairs={{0,8},{8,0},{16,24},{24,16},{32,40},{40,32},{48,56},{56,48},{64,72... | collective-permute-start | bytes 1572872 | tf_op jit(solution)/shard_map/ppermute | solution.py:835
  32.7 3.5 %copy-start.8 = (f32[2,64,256]{2,1,0:T(8,128)}, f32[2,64,256]{2,1,0:T(8,128)S(1)}, u32[]{:S(2)}) copy-start(f32[2,64,256]{2,1,0:T(8,128)S(1)} %collective-permute-done.7.refs_5_.refs_8_) | copy-start | bytes 393220
  36.2 32.8 %copy-start.3 = (f32[4,2,64,256]{3,2,1,0:T(8,128)}, f32[4,2,64,256]{3,2,1,0:T(8,128)S(1)}, u32[]{:S(2)}) copy-start(f32[4,2,64,256]{3,2,1,0:T(8,128)S(1)} %get-tuple-element.113.refs_9_.refs_21_.refs_6_) | copy-start | bytes 1572868
  36.2 12.6 %collective-permute-start.8 = (f32[4,2,64,256]{3,2,1,0:T(8,128)S(1)}, f32[4,2,64,256]{3,2,1,0:T(8,128)S(1)}, u32[]{:S(2)}, u32[]{:S(2)}) collective-permute-start(f32[4,2,64,256]{3,2,1,0:T(8,128)S(1)} %get-tuple-element.92.refs_2_.refs_4_.refs_12_.refs_8_.refs_19_), channel_id=1, source_target_pairs={{8,16},{16,8},{24,32},{32,24},{40,48},{48,40},{56,64},{64,56},{72,... | collective-permute-start | bytes 1572872 | tf_op jit(solution)/shard_map/ppermute | solution.py:835
  48.8 10.6 %collective-permute-start.11 = (f32[4,2,64,256]{3,2,1,0:T(8,128)S(1)}, f32[4,2,64,256]{3,2,1,0:T(8,128)S(1)}, u32[]{:S(2)}, u32[]{:S(2)}) collective-permute-start(f32[4,2,64,256]{3,2,1,0:T(8,128)S(1)} %get-tuple-element.99.refs_4_.refs_3_.refs_11_), channel_id=1, source_target_pairs={{0,8},{8,0},{16,24},{24,16},{32,40},{40,32},{48,56},{56,48},{64,72... | collective-permute-start | bytes 1572872 | tf_op jit(solution)/shard_map/ppermute | solution.py:835
  49.9 12.6 %collective-permute-start.10 = (f32[4,2,64,256]{3,2,1,0:T(8,128)S(1)}, f32[4,2,64,256]{3,2,1,0:T(8,128)S(1)}, u32[]{:S(2)}, u32[]{:S(2)}) collective-permute-start(f32[4,2,64,256]{3,2,1,0:T(8,128)S(1)} %get-tuple-element.98.refs_3_.refs_10_), channel_id=1, source_target_pairs={{8,16},{16,8},{24,32},{32,24},{40,48},{48,40},{56,64},{64,56},{72,... | collective-permute-start | bytes 1572872 | tf_op jit(solution)/shard_map/ppermute | solution.py:835
  62.5 11.1 %collective-permute-start.13 = (f32[4,3,64,256]{3,2,1,0:T(8,128)S(1)}, f32[4,3,64,256]{3,2,1,0:T(8,128)S(1)}, u32[]{:S(2)}, u32[]{:S(2)}) collective-permute-start(f32[4,3,64,256]{3,2,1,0:T(8,128)S(1)} %get-tuple-element.115.refs_13_.refs_3_), channel_id=1, source_target_pairs={{0,8},{8,0},{16,24},{24,16},{32,40},{40,32},{48,56},{56,48},{64,72... | collective-permute-start | bytes 2359304 | tf_op jit(solution)/shard_map/ppermute | solution.py:835
  63.6 15.4 %collective-permute-start.12 = (f32[4,3,64,256]{3,2,1,0:T(8,128)S(1)}, f32[4,3,64,256]{3,2,1,0:T(8,128)S(1)}, u32[]{:S(2)}, u32[]{:S(2)}) collective-permute-start(f32[4,3,64,256]{3,2,1,0:T(8,128)S(1)} %get-tuple-element.114.refs_12_.refs_3_), channel_id=1, source_target_pairs={{8,16},{16,8},{24,32},{32,24},{40,48},{48,40},{56,64},{64,56},{72,... | collective-permute-start | bytes 2359304 | tf_op jit(solution)/shard_map/ppermute | solution.py:835
  73.6 3.0 %copy-start.1 = (f32[4,3,6,64,256]{4,3,2,1,0:T(8,128)}, f32[4,3,6,64,256]{4,3,2,1,0:T(8,128)S(1)}, u32[]{:S(2)}) copy-start(f32[4,3,6,64,256]{4,3,2,1,0:T(8,128)S(1)} %get-tuple-element.132.refs_12_) | copy-start | bytes 14155780
  73.6 3.0 %copy-start.6 = (f32[4,3,2,64,256]{4,3,2,1,0:T(8,128)}, f32[4,3,2,64,256]{4,3,2,1,0:T(8,128)S(1)}, u32[]{:S(2)}) copy-start(f32[4,3,2,64,256]{4,3,2,1,0:T(8,128)S(1)} %get-tuple-element.130.refs_4_) | copy-start | bytes 4718596
  73.6 3.3 %copy-start.7 = (f32[4,3,2,64,256]{4,3,2,1,0:T(8,128)}, f32[4,3,2,64,256]{4,3,2,1,0:T(8,128)S(1)}, u32[]{:S(2)}) copy-start(f32[4,3,2,64,256]{4,3,2,1,0:T(8,128)S(1)} %get-tuple-element.131.refs_5_) | copy-start | bytes 4718596
  73.6 3.5 %copy-start.4 = (f32[4,3,64,256]{3,2,1,0:T(8,128)}, f32[4,3,64,256]{3,2,1,0:T(8,128)S(1)}, u32[]{:S(2)}) copy-start(f32[4,3,64,256]{3,2,1,0:T(8,128)S(1)} %collective-permute-done.13.refs_0_.refs_1_) | copy-start | bytes 2359300
  79.0 2.3 %copy-start.5 = (f32[4,3,64,256]{3,2,1,0:T(8,128)}, f32[4,3,64,256]{3,2,1,0:T(8,128)S(1)}, u32[]{:S(2)}) copy-start(f32[4,3,64,256]{3,2,1,0:T(8,128)S(1)} %collective-permute-done.12.refs_0_) | copy-start | bytes 2359300
  79.0 9.7 %copy-start.9 = (f32[2,64,256]{2,1,0:T(8,128)S(1)}, f32[2,64,256]{2,1,0:T(8,128)}, u32[]{:S(2)}) copy-start(f32[2,64,256]{2,1,0:T(8,128)} %copy-done.8) | copy-start | bytes 393220
  81.3 16.7 %all-to-all-start = ((f32[8,8,8,256]{3,2,1,0:T(8,128)}), f32[8,8,8,256]{3,2,1,0:T(8,128)S(1)}, u32[]{:S(2)}, u32[]{:S(2)}) async-start(f32[8,8,8,256]{3,2,1,0:T(8,128)} %get-tuple-element.127), calls=%async_computation | async-start | bytes 1048576 | tf_op jit(solution)/shard_map/all_to_all | solution.py:975

commit v4 on v3

--- a/solution.py
+++ b/solution.py
@@ -194,6 +194,22 @@
         for j in range(8):
             mid = load(t, j)
             store_all([(dt, dy(mid), (0, j)), (dt, dx(mid), (1, j))])
+
+
+def momentum_ends(info, s, m, chip, core, sems):
+    odd = info[4]
+    copies = [
+        pltpu.make_async_copy(m.at[at, :, pl.ds(first, 2)], end.at[at], sems.at[at, i])
+        for i, (end, first) in enumerate(((chip, 6 * odd), (core, 6 - 6 * odd)))
+        for at in range(4)
+    ]
+
+    @pl.when(s == 0)
+    def _():
+        for copy in copies:
+            copy.start()
+        for copy in copies:
+            copy.wait()
 
 
 def velocity_inner(info, s, m, w_in, w_edge, m_edge):
@@ -755,6 +771,10 @@
     return ref
 
 
+def far_off(ref, s):
+    return ref
+
+
 def flows(view):
     return view is stream or getattr(view, "streamed", False)
 
@@ -807,13 +827,19 @@
         return vmem, jax.ShapeDtypeStruct(dims, f32)
 
     streamed = [any(flows(view) for other, view in ins if other is array) for array in arrays]
-    operands = [pltpu.with_memory_space_constraint(a, pltpu.HBM) if st else a for a, st in zip(arrays, streamed)]
+    remote = [any(view is far_off for other, view in ins if other is array) for array in arrays]
+    operands = [
+        pltpu.with_memory_space_constraint(a, pltpu.HBM) if st or re else a for a, st, re in zip(arrays, streamed, remote)
+    ]
     out_specs, out_shapes = zip(*(made_of(*o) for o in outs))
 
     return pl.pallas_call(
         body,
         grid=(subjects,) if streams else (),
-        in_specs=[pl.BlockSpec(memory_space=pltpu.SMEM)] + [block(a.shape) if st else vmem for a, st in zip(arrays, streamed)],
+        in_specs=[pl.BlockSpec(memory_space=pltpu.SMEM)] + [
+            pl.BlockSpec(memory_space=pl.ANY) if re else block(a.shape) if st else vmem
+            for a, st, re in zip(arrays, streamed, remote)
+        ],
         out_specs=list(out_specs),
         out_shape=list(out_shapes),
         scratch_shapes=list(scratch),
@@ -859,7 +885,13 @@
     def partner(array, by):
         return lax.ppermute(array, "subj", [(i, i ^ by) for i in range(groups)])
 
-    ends = [lax.dynamic_slice_in_dim(momentum, at, 2, 2) for at in (6 * odd, 6 - 6 * odd)]
+    ends = call(
+        momentum_ends,
+        info,
+        [(momentum, far_off)],
+        [(shape(3, 2), whole), (shape(3, 2), whole)],
+        [pltpu.SemaphoreType.DMA((4, 2))],
+    )
     across, ends = lax.optimization_barrier((partner(template, 1), ends))
     mr = [swap(ends[r], r) for r in ROLES]
     own, later = lax.optimization_barrier((jnp.stack([template, across]), momentum))
@@ -897,7 +929,7 @@
 
     wb, i1b, s1 = [None, None], [None, None], [None, None]
     for r in (1, 0):
-        given = [(m_edge, one), (w_edge, one)] + tdt + [(mr[r], stream), (th[r], whole)] + side(r, w_in, i1_in)
+        given = [(m_edge, one), (w_edge, one)] + tdt + [(mr[r], one), (th[r], whole)] + side(r, w_in, i1_in)
         wb[r], i1b[r], s1[r] = call(outer_1(r), info, given, [out(3, 2), out(2), out(2)], [slopes], 3)
         if r == 1:
             mr[0], s1[1] = lax.optimization_barrier((mr[0], s1[1]))

time: 100 us -> 98.9 us (0.989)
  Pallas kernels: 43.9 us -> 51.1 us
  waiting for transfers between devices: 9.33 us -> 4.71 us
  local copies, waits for them, and re-layouts: 4.53 us -> 0.56 us
    pallas_call x15 -> x16, Pallas kernels: 43.9 us -> 51.1 us  [call(): pl.pallas_call(body, grid=(subjects,) if streams else (), in_specs=[pl.Bl...]
    ppermute x10, waiting for transfers between devices: 8.68 us -> 3.3 us  [swap(): return lax.ppermute(array, 'space', (chip_pairs, core_pairs)[role])]
    dynamic_slice x1 -> x0, local copies, waits for them, and re-layouts: 3.93 us -> none  [shards(): lax.dynamic_slice_in_dim(momentum, at, 2, 2)]
  transfers between devices with their start and end apart: 15 -> 15, of which waited for: 5 -> 3; matrix products, arithmetic and copies ran while one was open for 4% -> 1% of each run, Pallas kernels for 42% -> 50%
where the time goes in v4:
time: 98.9 us; the launch traced here: 98.4 us
  Pallas kernels  51.1 us (52%)
  starting transfers between devices  39.5 us (40%)
  waiting for transfers between devices  4.71 us (5%)
  other arithmetic  1.41 us (1%)
  between operations  1.04 us (1%)
    pallas_call x16, Pallas kernels, call(): pl.pallas_call(body, grid=(subjects,) if streams else (), in_specs=[pl.Bl...  51.1 us
    ppermute x10, starting transfers between devices, swap(): return lax.ppermute(array, 'space', (chip_pairs, core_pairs)[role])  27.1 us
    all_to_all x1, starting transfers between devices, shards(): parts = lax.all_to_all(total, 'subj', 0, 0)  6.81 us
    ppermute x4, starting transfers between devices, partner(): return lax.ppermute(array, 'subj', [(i, i ^ by) for i in range(groups)])  5.66 us
    ppermute x10, waiting for transfers between devices, swap(): return lax.ppermute(array, 'space', (chip_pairs, core_pairs)[role])  3.3 us
  transfers between devices with their start and end apart: 15, of which 3 were waited for; matrix products, arithmetic and copies ran while one was open for 1% of the time, Pallas kernels for 50%

profile of v4, /device:TPU:6, one launch (start us, length us, event | category | flops | bytes accessed | tf_op | source)
XLA Modules:
  0.0 98.4 jit_solution(14157268196699401080)
XLA Ops:
  0.6 1.5 %collective-permute-start = (f32[8,8,256]{2,1,0:T(8,128)}, f32[8,8,256]{2,1,0:T(8,128)S(1)}, u32[]{:S(2)}, u32[]{:S(2)}) collective-permute-start(f32[8,8,256]{2,1,0:T(8,128)} %param.4), channel_id=1, source_target_pairs={{0,1},{1,0},{2,3},{3,2},{4,5},{5,4},{6,7},{7,6},{8,9},{9,8},{10,11... | collective-permute-start | bytes 196616 | tf_op jit(solution)/shard_map/ppermute | solution.py:886
  2.1 0.7 pad_add_fusion.info_ref
  2.8 2.4 %momentum_ends.1 = (f32[4,3,2,64,256]{4,3,2,1,0:T(8,128)S(1)}, f32[4,3,2,64,256]{4,3,2,1,0:T(8,128)S(1)}) custom-call(s32[7]{0:T(128)S(1)} %pad_add_fusion.info_ref, f32[4,3,8,64,256]{4,3,2,1,0:T(8,128)} %refs_0_.4), custom_call_target="tpu_custom_call" | custom-call | bytes 3300000 | tf_op jit(solution)/shard_map/momentum_ends/pallas_call | solution.py:836
  5.3 1.4 %collective-permute-done = f32[8,8,256]{2,1,0:T(8,128)S(1)} collective-permute-done((f32[8,8,256]{2,1,0:T(8,128)}, f32[8,8,256]{2,1,0:T(8,128)S(1)}, u32[]{:S(2)}, u32[]{:S(2)}) %collective-permute-start) | collective-permute-done | bytes 65568 | tf_op jit(solution)/shard_map/ppermute | solution.py:886
  6.7 0.0 collective-permute-start.5
  6.7 6.3 %collective-permute-start.4 = (f32[4,3,2,64,256]{4,3,2,1,0:T(8,128)S(1)}, f32[4,3,2,64,256]{4,3,2,1,0:T(8,128)S(1)}, u32[]{:S(2)}, u32[]{:S(2)}) collective-permute-start(f32[4,3,2,64,256]{4,3,2,1,0:T(8,128)S(1)} %get-tuple-element.87), channel_id=1, source_target_pairs={{8,16},{16,8},{24,32},{32,24},{40,48},{48,40},{56,64},{64,56},{72,... | collective-permute-start | bytes 4718600 | tf_op jit(solution)/shard_map/ppermute | solution.py:861
  13.0 3.1 %collective-permute-start.3 = (f32[2,8,8,256]{3,2,1,0:T(8,128)S(1)}, f32[2,8,8,256]{3,2,1,0:T(8,128)S(1)}, u32[]{:S(2)}, u32[]{:S(2)}) collective-permute-start(f32[2,8,8,256]{3,2,1,0:T(8,128)S(1)} %pad_maximum_fusion.refs_0_), channel_id=1, source_target_pairs={{0,6},{1,7},{2,4},{3,5},{4,2},{5,3},{6,0},{7,1},{8,14},{9,15},{10,... | collective-permute-start | bytes 393224 | tf_op jit(solution)/shard_map/ppermute | solution.py:886
  16.1 0.6 collective-permute-start.2
  16.8 0.5 collective-permute-start.1
  17.2 5.7 %velocity_inner.1 = (f32[4,3,6,64,256]{4,3,2,1,0:T(8,128)S(1)}, f32[4,3,2,64,256]{4,3,2,1,0:T(8,128)S(1)}, f32[4,3,2,64,256]{4,3,2,1,0:T(8,128)S(1)}) custom-call(s32[7]{0:T(128)S(1)} %pad_add_fusion.info_ref, f32[4,3,8,64,256]{4,3,2,1,0:T(8,128)} %refs_0_.4), custom_call_target="tpu_custom_call" | custom-call | bytes 16500000 | tf_op jit(solution)/shard_map/velocity_inner/pallas_call | solution.py:836
  22.9 0.0 collective-permute-done.3.refs_3_
  22.9 0.0 collective-permute-done.2.refs_2_
  22.9 1.0 template_planes.1
  23.9 0.1 collective-permute-start.6
  24.0 3.5 %collective-permute-start.7 = (f32[2,64,256]{2,1,0:T(8,128)S(1)}, f32[2,64,256]{2,1,0:T(8,128)S(1)}, u32[]{:S(2)}, u32[]{:S(2)}) collective-permute-start(f32[2,64,256]{2,1,0:T(8,128)S(1)} %get-tuple-element.93), channel_id=1, source_target_pairs={{8,16},{16,8},{24,32},{32,24},{40,48},{48,40},{56,64},{64,56},{72,... | collective-permute-start | bytes 393224 | tf_op jit(solution)/shard_map/ppermute | solution.py:861
  27.5 2.0 %inner_1.1 = (f32[4,6,64,256]{3,2,1,0:T(8,128)S(1)}, f32[4,4,64,256]{3,2,1,0:T(8,128)S(1)}) custom-call(s32[7]{0:T(128)S(1)} %pad_add_fusion.info_ref, f32[4,3,6,64,256]{4,3,2,1,0:T(8,128)S(1)} %get-tuple-element.78.refs_0_.refs_6_.refs_3_.refs_2_, f32[8,64,256]{2,1,0:T(8,128)S(1)} %get-tuple-element.85.refs_1_.refs_2_.refs_24_.refs_10_, ...), custom_call_target="tpu_custom_call" | custom-call | bytes 9900000 | tf_op jit(solution)/shard_map/inner_1/pallas_call | solution.py:836
  29.6 0.0 collective-permute-done.6.refs_5_.refs_9_
  29.6 0.0 collective-permute-done.5.refs_4_
  29.6 2.1 %outer_1_core.1 = (f32[4,3,2,64,256]{4,3,2,1,0:T(8,128)S(1)}, f32[4,2,64,256]{3,2,1,0:T(8,128)S(1)}, f32[4,2,64,256]{3,2,1,0:T(8,128)S(1)}) custom-call(s32[7]{0:T(128)S(1)} %pad_add_fusion.info_ref, f32[4,3,2,64,256]{4,3,2,1,0:T(8,128)S(1)} %get-tuple-element.79.refs_0_, f32[4,3,2,64,256]{4,3,2,1,0:T(8,128)S(1)} %get-tuple-element.80.refs_1_, ...), custom_call_target="tpu_custom_call" | custom-call | bytes 9900000 | tf_op jit(solution)/shard_map/outer_1_core/pallas_call | solution.py:836
  31.7 0.0 collective-permute-done.4.refs_4_
  31.7 0.0 copy-start
  31.7 0.1 collective-permute-start.9
  31.8 0.7 collective-permute-done.7.refs_5_.refs_8_
  32.5 2.0 %outer_1_chip.1 = (f32[4,3,2,64,256]{4,3,2,1,0:T(8,128)S(1)}, f32[4,2,64,256]{3,2,1,0:T(8,128)S(1)}, f32[4,2,64,256]{3,2,1,0:T(8,128)S(1)}) custom-call(s32[7]{0:T(128)S(1)} %pad_add_fusion.info_ref, f32[4,3,2,64,256]{4,3,2,1,0:T(8,128)S(1)} %get-tuple-element.79.refs_0_, f32[4,3,2,64,256]{4,3,2,1,0:T(8,128)S(1)} %get-tuple-element.80.refs_1_, ...), custom_call_target="tpu_custom_call" | custom-call | bytes 9900000 | tf_op jit(solution)/shard_map/outer_1_chip/pallas_call | solution.py:836
  34.6 5.8 %collective-permute-start.8 = (f32[4,2,64,256]{3,2,1,0:T(8,128)S(1)}, f32[4,2,64,256]{3,2,1,0:T(8,128)S(1)}, u32[]{:S(2)}, u32[]{:S(2)}) collective-permute-start(f32[4,2,64,256]{3,2,1,0:T(8,128)S(1)} %get-tuple-element.96.refs_2_.refs_4_.refs_12_.refs_8_.refs_19_), channel_id=1, source_target_pairs={{8,16},{16,8},{24,32},{32,24},{40,48},{48,40},{56,64},{64,56},{72,... | collective-permute-start | bytes 1572872 | tf_op jit(solution)/shard_map/ppermute | solution.py:861
  40.3 2.6 %inner_2.1 = (f32[4,6,64,256]{3,2,1,0:T(8,128)S(1)}, f32[4,4,64,256]{3,2,1,0:T(8,128)S(1)}, f32[4,4,64,256]{3,2,1,0:T(8,128)S(1)}) custom-call(s32[7]{0:T(128)S(1)} %pad_add_fusion.info_ref, f32[4,3,6,64,256]{4,3,2,1,0:T(8,128)S(1)} %get-tuple-element.78.refs_0_.refs_6_.refs_3_.refs_2_, f32[4,4,64,256]{3,2,1,0:T(8,128)S(1)} %get-tuple-element.98.refs_1_.refs_11_, ...), custom_call_target="tpu_custom_call" | custom-call | bytes 13200000 | tf_op jit(solution)/shard_map/inner_2/pallas_call | solution.py:836
  43.0 1.6 %outer_2_core.1 = (f32[4,2,64,256]{3,2,1,0:T(8,128)S(1)}, f32[4,2,64,256]{3,2,1,0:T(8,128)S(1)}, f32[4,1,64,256]{3,2,1,0:T(8,128)S(1)}, f32[4,2,64,256]{3,2,1,0:T(8,128)S(1)}) custom-call(s32[7]{0:T(128)S(1)} %pad_add_fusion.info_ref, f32[4,8,64,256]{3,2,1,0:T(8,128)S(1)} %copy-done, f32[4,2,64,256]{3,2,1,0:T(8,128)S(1)} %collective-permute-done.9.refs_1_.refs_7_.refs_18_, ...), custom_call_target="tpu_custom_call" | custom-call | bytes 6600000 | tf_op jit(solution)/shard_map/outer_2_core/pallas_call | solution.py:836
  44.6 2.5 %collective-permute-done.8.refs_1_.refs_7_.refs_17_ = f32[4,2,64,256]{3,2,1,0:T(8,128)S(1)} collective-permute-done((f32[4,2,64,256]{3,2,1,0:T(8,128)S(1)}, f32[4,2,64,256]{3,2,1,0:T(8,128)S(1)}, u32[]{:S(2)}, u32[]{:S(2)}) %collective-permute-start.8) | collective-permute-done | bytes 524320 | tf_op jit(solution)/shard_map/ppermute | solution.py:861
  47.2 1.6 %outer_2_chip.1 = (f32[4,2,64,256]{3,2,1,0:T(8,128)S(1)}, f32[4,2,64,256]{3,2,1,0:T(8,128)S(1)}, f32[4,1,64,256]{3,2,1,0:T(8,128)S(1)}, f32[4,2,64,256]{3,2,1,0:T(8,128)S(1)}) custom-call(s32[7]{0:T(128)S(1)} %pad_add_fusion.info_ref, f32[4,8,64,256]{3,2,1,0:T(8,128)S(1)} %copy-done, f32[4,2,64,256]{3,2,1,0:T(8,128)S(1)} %collective-permute-done.8.refs_1_.refs_7_.refs_17_, ...), custom_call_target="tpu_custom_call" | custom-call | bytes 6600000 | tf_op jit(solution)/shard_map/outer_2_chip/pallas_call | solution.py:836
  48.8 5.8 %collective-permute-start.10 = (f32[4,2,64,256]{3,2,1,0:T(8,128)S(1)}, f32[4,2,64,256]{3,2,1,0:T(8,128)S(1)}, u32[]{:S(2)}, u32[]{:S(2)}) collective-permute-start(f32[4,2,64,256]{3,2,1,0:T(8,128)S(1)} %get-tuple-element.102.refs_3_.refs_10_), channel_id=1, source_target_pairs={{8,16},{16,8},{24,32},{32,24},{40,48},{48,40},{56,64},{64,56},{72,... | collective-permute-start | bytes 1572872 | tf_op jit(solution)/shard_map/ppermute | solution.py:861
  54.6 5.3 %inner_3.1 = (f32[4,6,64,256]{3,2,1,0:T(8,128)S(1)}, f32[4,4,64,256]{3,2,1,0:T(8,128)S(1)}, f32[4,3,6,64,256]{4,3,2,1,0:T(8,128)S(1)}, f32[4,8,64,256]{3,2,1,0:T(8,128)}) custom-call(s32[7]{0:T(128)S(1)} %pad_add_fusion.info_ref, f32[4,3,6,64,256]{4,3,2,1,0:T(8,128)S(1)} %get-tuple-element.78.refs_0_.refs_6_.refs_3_.refs_2_, ...), custom_call_target="tpu_custom_call" | custom-call | bytes 23100000 | tf_op jit(solution)/shard_map/inner_3/pallas_call | solution.py:836
  59.9 0.0 collective-permute-done.11.refs_0_.refs_7_
  59.9 1.7 %outer_3_core.1 = (f32[4,2,64,256]{3,2,1,0:T(8,128)S(1)}, f32[4,2,64,256]{3,2,1,0:T(8,128)S(1)}, f32[4,3,64,256]{3,2,1,0:T(8,128)S(1)}) custom-call(s32[7]{0:T(128)S(1)} %pad_add_fusion.info_ref, f32[4,2,64,256]{3,2,1,0:T(8,128)S(1)} %collective-permute-done.11.refs_0_.refs_7_, f32[4,3,2,64,256]{4,3,2,1,0:T(8,128)S(1)} %get-tuple-element.95.refs_2_.refs_1_, ...), custom_call_target="tpu_custom_call" | custom-call | bytes 6600000 | tf_op jit(solution)/shard_map/outer_3_core/pallas_call | solution.py:836
  61.6 0.0 collective-permute-done.10.refs_0_.refs_6_
  61.6 0.1 collective-permute-start.13
  61.7 1.7 %outer_3_chip.1 = (f32[4,2,64,256]{3,2,1,0:T(8,128)S(1)}, f32[4,2,64,256]{3,2,1,0:T(8,128)S(1)}, f32[4,3,64,256]{3,2,1,0:T(8,128)S(1)}) custom-call(s32[7]{0:T(128)S(1)} %pad_add_fusion.info_ref, f32[4,2,64,256]{3,2,1,0:T(8,128)S(1)} %collective-permute-done.10.refs_0_.refs_6_, f32[4,3,2,64,256]{4,3,2,1,0:T(8,128)S(1)} %get-tuple-element.94.refs_2_.refs_1_, ...), custom_call_target="tpu_custom_call" | custom-call | bytes 6600000 | tf_op jit(solution)/shard_map/outer_3_chip/pallas_call | solution.py:836
  63.4 5.5 %collective-permute-start.12 = (f32[4,3,64,256]{3,2,1,0:T(8,128)S(1)}, f32[4,3,64,256]{3,2,1,0:T(8,128)S(1)}, u32[]{:S(2)}, u32[]{:S(2)}) collective-permute-start(f32[4,3,64,256]{3,2,1,0:T(8,128)S(1)} %get-tuple-element.118.refs_12_.refs_3_), channel_id=1, source_target_pairs={{8,16},{16,8},{24,32},{32,24},{40,48},{48,40},{56,64},{64,56},{72,... | collective-permute-start | bytes 2359304 | tf_op jit(solution)/shard_map/ppermute | solution.py:861
  68.9 6.8 %inner_4.1 = (f32[4,6,64,256]{3,2,1,0:T(8,128)S(1)}, f32[8,4,8,256]{3,2,1,0:T(8,128)S(1)}, f32[4,3,6,64,256]{4,3,2,1,0:T(8,128)S(1)}, f32[4,3,2,64,256]{4,3,2,1,0:T(8,128)S(1)}, f32[4,3,2,64,256]{4,3,2,1,0:T(8,128)S(1)}) custom-call(s32[7]{0:T(128)S(1)} %pad_add_fusion.info_ref, f32[4,3,6,64,256]{4,3,2,1,0:T(8,128)S(1)} %get-tuple-element.78.refs_0_.refs_6_.refs_3_.refs_2_, ...), custom_call_target="tpu_custom_call" | custom-call | bytes 16500000 | tf_op jit(solution)/shard_map/inner_4/pallas_call | solution.py:836
  75.8 0.0 collective-permute-done.13.refs_0_.refs_1_
  75.8 2.9 %outer_4_core.1 = (f32[8,6,8,256]{3,2,1,0:T(8,128)S(1)}, f32[4,2,64,256]{3,2,1,0:T(8,128)}) custom-call(s32[7]{0:T(128)S(1)} %pad_add_fusion.info_ref, f32[4,3,64,256]{3,2,1,0:T(8,128)S(1)} %collective-permute-done.13.refs_0_.refs_1_, f32[4,3,2,64,256]{4,3,2,1,0:T(8,128)S(1)} %get-tuple-element.95.refs_2_.refs_1_, ...), custom_call_target="tpu_custom_call" | custom-call | bytes 6600000 | tf_op jit(solution)/shard_map/outer_4_core/pallas_call | solution.py:836
  78.8 0.3 copy-done.7
  79.0 0.2 copy-done.4
  79.3 0.0 collective-permute-done.12.refs_0_
  79.3 2.3 %outer_4_chip.1 = (f32[8,8,8,256]{3,2,1,0:T(8,128)}, f32[4,2,64,256]{3,2,1,0:T(8,128)}) custom-call(s32[7]{0:T(128)S(1)} %pad_add_fusion.info_ref, f32[4,3,64,256]{3,2,1,0:T(8,128)S(1)} %collective-permute-done.12.refs_0_, f32[4,3,2,64,256]{4,3,2,1,0:T(8,128)S(1)} %get-tuple-element.94.refs_2_.refs_1_, ...), custom_call_target="tpu_custom_call" | custom-call | bytes 6600000 | tf_op jit(solution)/shard_map/outer_4_chip/pallas_call | solution.py:836
  81.6 6.8 %all-to-all-start = ((f32[8,8,8,256]{3,2,1,0:T(8,128)}), f32[8,8,8,256]{3,2,1,0:T(8,128)S(1)}, u32[]{:S(2)}, u32[]{:S(2)}) async-start(f32[8,8,8,256]{3,2,1,0:T(8,128)} %get-tuple-element.131), calls=%async_computation | async-start | bytes 1048576 | tf_op jit(solution)/shard_map/all_to_all | solution.py:1007
  88.4 9.3 %finish.1 = f32[4,3,8,64,256]{4,3,2,1,0:T(8,128)} custom-call(s32[7]{0:T(128)S(1)} %pad_add_fusion.info_ref, f32[4,3,64,256]{3,2,1,0:T(8,128)} %copy-done.5, f32[4,3,64,256]{3,2,1,0:T(8,128)} %copy-done.4, f32[4,2,64,256]{3,2,1,0:T(8,128)} %get-tuple-element.132.refs_2_, f32[4,2,64,256]{3,2,1,0:T(8,128)} %get-tuple-element.133.refs_3_, ...), custom_call_target="tpu_custom_call" | custom-call | bytes 19800000 | tf_op jit(solution)/shard_map/finish/pallas_call | solution.py:836
  97.7 0.0 all-to-all-done
  97.7 0.7 reduce_sum.9
  (23 shorter events, 0.1 us)
Async XLA Ops:
  0.6 6.1 %collective-permute-start = (f32[8,8,256]{2,1,0:T(8,128)}, f32[8,8,256]{2,1,0:T(8,128)S(1)}, u32[]{:S(2)}, u32[]{:S(2)}) collective-permute-start(f32[8,8,256]{2,1,0:T(8,128)} %param.4), channel_id=1, source_target_pairs={{0,1},{1,0},{2,3},{3,2},{4,5},{5,4},{6,7},{7,6},{8,9},{9,8},{10,11... | collective-permute-start | bytes 196616 | tf_op jit(solution)/shard_map/ppermute | solution.py:886
  2.8 10.2 %copy-start.10 = (f32[8,8,256]{2,1,0:T(8,128)S(1)}, f32[8,8,256]{2,1,0:T(8,128)}, u32[]{:S(2)}) copy-start(f32[8,8,256]{2,1,0:T(8,128)} %param.4) | copy-start | bytes 196612
  6.7 22.9 %collective-permute-start.5 = (f32[4,3,2,64,256]{4,3,2,1,0:T(8,128)S(1)}, f32[4,3,2,64,256]{4,3,2,1,0:T(8,128)S(1)}, u32[]{:S(2)}, u32[]{:S(2)}) collective-permute-start(f32[4,3,2,64,256]{4,3,2,1,0:T(8,128)S(1)} %get-tuple-element.88), channel_id=1, source_target_pairs={{0,8},{8,0},{16,24},{24,16},{32,40},{40,32},{48,56},{56,48},{64,72... | collective-permute-start | bytes 4718600 | tf_op jit(solution)/shard_map/ppermute | solution.py:861
  6.7 25.0 %collective-permute-start.4 = (f32[4,3,2,64,256]{4,3,2,1,0:T(8,128)S(1)}, f32[4,3,2,64,256]{4,3,2,1,0:T(8,128)S(1)}, u32[]{:S(2)}, u32[]{:S(2)}) collective-permute-start(f32[4,3,2,64,256]{4,3,2,1,0:T(8,128)S(1)} %get-tuple-element.87), channel_id=1, source_target_pairs={{8,16},{16,8},{24,32},{32,24},{40,48},{48,40},{56,64},{64,56},{72,... | collective-permute-start | bytes 4718600 | tf_op jit(solution)/shard_map/ppermute | solution.py:861
  13.0 9.9 %collective-permute-start.3 = (f32[2,8,8,256]{3,2,1,0:T(8,128)S(1)}, f32[2,8,8,256]{3,2,1,0:T(8,128)S(1)}, u32[]{:S(2)}, u32[]{:S(2)}) collective-permute-start(f32[2,8,8,256]{3,2,1,0:T(8,128)S(1)} %pad_maximum_fusion.refs_0_), channel_id=1, source_target_pairs={{0,6},{1,7},{2,4},{3,5},{4,2},{5,3},{6,0},{7,1},{8,14},{9,15},{10,... | collective-permute-start | bytes 393224 | tf_op jit(solution)/shard_map/ppermute | solution.py:886
  16.1 6.8 %collective-permute-start.2 = (f32[2,8,8,256]{3,2,1,0:T(8,128)S(1)}, f32[2,8,8,256]{3,2,1,0:T(8,128)S(1)}, u32[]{:S(2)}, u32[]{:S(2)}) collective-permute-start(f32[2,8,8,256]{3,2,1,0:T(8,128)S(1)} %pad_maximum_fusion.refs_0_), channel_id=1, source_target_pairs={{0,4},{1,5},{2,6},{3,7},{4,0},{5,1},{6,2},{7,3},{8,12},{9,13},{10,... | collective-permute-start | bytes 393224 | tf_op jit(solution)/shard_map/ppermute | solution.py:886
  16.8 6.2 %collective-permute-start.1 = (f32[2,8,8,256]{3,2,1,0:T(8,128)S(1)}, f32[2,8,8,256]{3,2,1,0:T(8,128)S(1)}, u32[]{:S(2)}, u32[]{:S(2)}) collective-permute-start(f32[2,8,8,256]{3,2,1,0:T(8,128)S(1)} %pad_maximum_fusion.refs_0_), channel_id=1, source_target_pairs={{0,2},{1,3},{2,0},{3,1},{4,6},{5,7},{6,4},{7,5},{8,10},{9,11},{10,... | collective-permute-start | bytes 393224 | tf_op jit(solution)/shard_map/ppermute | solution.py:886
  23.9 5.7 %collective-permute-start.6 = (f32[2,64,256]{2,1,0:T(8,128)S(1)}, f32[2,64,256]{2,1,0:T(8,128)S(1)}, u32[]{:S(2)}, u32[]{:S(2)}) collective-permute-start(f32[2,64,256]{2,1,0:T(8,128)S(1)} %get-tuple-element.89), channel_id=1, source_target_pairs={{0,8},{8,0},{16,24},{24,16},{32,40},{40,32},{48,56},{56,48},{64,72... | collective-permute-start | bytes 393224 | tf_op jit(solution)/shard_map/ppermute | solution.py:861
  24.0 8.5 %collective-permute-start.7 = (f32[2,64,256]{2,1,0:T(8,128)S(1)}, f32[2,64,256]{2,1,0:T(8,128)S(1)}, u32[]{:S(2)}, u32[]{:S(2)}) collective-permute-start(f32[2,64,256]{2,1,0:T(8,128)S(1)} %get-tuple-element.93), channel_id=1, source_target_pairs={{8,16},{16,8},{24,32},{32,24},{40,48},{48,40},{56,64},{64,56},{72,... | collective-permute-start | bytes 393224 | tf_op jit(solution)/shard_map/ppermute | solution.py:861
  31.6 37.3 %copy-start.2 = (f32[4,2,64,256]{3,2,1,0:T(8,128)}, f32[4,2,64,256]{3,2,1,0:T(8,128)S(1)}, u32[]{:S(2)}) copy-start(f32[4,2,64,256]{3,2,1,0:T(8,128)S(1)} %get-tuple-element.114.refs_9_.refs_22_.refs_7_) | copy-start | bytes 1572868
  31.7 8.7 %copy-start = (f32[4,8,64,256]{3,2,1,0:T(8,128)S(1)}, f32[4,8,64,256]{3,2,1,0:T(8,128)}, u32[]{:S(2)}) copy-start(f32[4,8,64,256]{3,2,1,0:T(8,128)} %refs_0_.6) | copy-start | bytes 6291460
  31.7 11.3 %collective-permute-start.9 = (f32[4,2,64,256]{3,2,1,0:T(8,128)S(1)}, f32[4,2,64,256]{3,2,1,0:T(8,128)S(1)}, u32[]{:S(2)}, u32[]{:S(2)}) collective-permute-start(f32[4,2,64,256]{3,2,1,0:T(8,128)S(1)} %get-tuple-element.97.refs_3_.refs_4_.refs_13_.refs_8_.refs_20_), channel_id=1, source_target_pairs={{0,8},{8,0},{16,24},{24,16},{32,40},{40,32},{48,56},{56,48},{64,72... | collective-permute-start | bytes 1572872 | tf_op jit(solution)/shard_map/ppermute | solution.py:861
  32.5 2.0 %copy-start.8 = (f32[2,64,256]{2,1,0:T(8,128)}, f32[2,64,256]{2,1,0:T(8,128)S(1)}, u32[]{:S(2)}) copy-start(f32[2,64,256]{2,1,0:T(8,128)S(1)} %collective-permute-done.7.refs_5_.refs_8_) | copy-start | bytes 393220
  34.5 34.4 %copy-start.3 = (f32[4,2,64,256]{3,2,1,0:T(8,128)}, f32[4,2,64,256]{3,2,1,0:T(8,128)S(1)}, u32[]{:S(2)}) copy-start(f32[4,2,64,256]{3,2,1,0:T(8,128)S(1)} %get-tuple-element.117.refs_9_.refs_21_.refs_6_) | copy-start | bytes 1572868
  34.6 12.6 %collective-permute-start.8 = (f32[4,2,64,256]{3,2,1,0:T(8,128)S(1)}, f32[4,2,64,256]{3,2,1,0:T(8,128)S(1)}, u32[]{:S(2)}, u32[]{:S(2)}) collective-permute-start(f32[4,2,64,256]{3,2,1,0:T(8,128)S(1)} %get-tuple-element.96.refs_2_.refs_4_.refs_12_.refs_8_.refs_19_), channel_id=1, source_target_pairs={{8,16},{16,8},{24,32},{32,24},{40,48},{48,40},{56,64},{64,56},{72,... | collective-permute-start | bytes 1572872 | tf_op jit(solution)/shard_map/ppermute | solution.py:861
  47.2 12.7 %collective-permute-start.11 = (f32[4,2,64,256]{3,2,1,0:T(8,128)S(1)}, f32[4,2,64,256]{3,2,1,0:T(8,128)S(1)}, u32[]{:S(2)}, u32[]{:S(2)}) collective-permute-start(f32[4,2,64,256]{3,2,1,0:T(8,128)S(1)} %get-tuple-element.103.refs_4_.refs_3_.refs_11_), channel_id=1, source_target_pairs={{0,8},{8,0},{16,24},{24,16},{32,40},{40,32},{48,56},{56,48},{64,72... | collective-permute-start | bytes 1572872 | tf_op jit(solution)/shard_map/ppermute | solution.py:861
  48.8 12.8 %collective-permute-start.10 = (f32[4,2,64,256]{3,2,1,0:T(8,128)S(1)}, f32[4,2,64,256]{3,2,1,0:T(8,128)S(1)}, u32[]{:S(2)}, u32[]{:S(2)}) collective-permute-start(f32[4,2,64,256]{3,2,1,0:T(8,128)S(1)} %get-tuple-element.102.refs_3_.refs_10_), channel_id=1, source_target_pairs={{8,16},{16,8},{24,32},{32,24},{40,48},{48,40},{56,64},{64,56},{72,... | collective-permute-start | bytes 1572872 | tf_op jit(solution)/shard_map/ppermute | solution.py:861
  61.6 14.2 %collective-permute-start.13 = (f32[4,3,64,256]{3,2,1,0:T(8,128)S(1)}, f32[4,3,64,256]{3,2,1,0:T(8,128)S(1)}, u32[]{:S(2)}, u32[]{:S(2)}) collective-permute-start(f32[4,3,64,256]{3,2,1,0:T(8,128)S(1)} %get-tuple-element.119.refs_13_.refs_3_), channel_id=1, source_target_pairs={{0,8},{8,0},{16,24},{24,16},{32,40},{40,32},{48,56},{56,48},{64,72... | collective-permute-start | bytes 2359304 | tf_op jit(solution)/shard_map/ppermute | solution.py:861
  63.4 15.8 %collective-permute-start.12 = (f32[4,3,64,256]{3,2,1,0:T(8,128)S(1)}, f32[4,3,64,256]{3,2,1,0:T(8,128)S(1)}, u32[]{:S(2)}, u32[]{:S(2)}) collective-permute-start(f32[4,3,64,256]{3,2,1,0:T(8,128)S(1)} %get-tuple-element.118.refs_12_.refs_3_), channel_id=1, source_target_pairs={{8,16},{16,8},{24,32},{32,24},{40,48},{48,40},{56,64},{64,56},{72,... | collective-permute-start | bytes 2359304 | tf_op jit(solution)/shard_map/ppermute | solution.py:861
  75.8 2.9 %copy-start.1 = (f32[4,3,6,64,256]{4,3,2,1,0:T(8,128)}, f32[4,3,6,64,256]{4,3,2,1,0:T(8,128)S(1)}, u32[]{:S(2)}) copy-start(f32[4,3,6,64,256]{4,3,2,1,0:T(8,128)S(1)} %get-tuple-element.136.refs_12_) | copy-start | bytes 14155780
  75.8 2.9 %copy-start.6 = (f32[4,3,2,64,256]{4,3,2,1,0:T(8,128)}, f32[4,3,2,64,256]{4,3,2,1,0:T(8,128)S(1)}, u32[]{:S(2)}) copy-start(f32[4,3,2,64,256]{4,3,2,1,0:T(8,128)S(1)} %get-tuple-element.134.refs_4_) | copy-start | bytes 4718596
  75.8 3.2 %copy-start.7 = (f32[4,3,2,64,256]{4,3,2,1,0:T(8,128)}, f32[4,3,2,64,256]{4,3,2,1,0:T(8,128)S(1)}, u32[]{:S(2)}) copy-start(f32[4,3,2,64,256]{4,3,2,1,0:T(8,128)S(1)} %get-tuple-element.135.refs_5_) | copy-start | bytes 4718596
  75.8 3.4 %copy-start.4 = (f32[4,3,64,256]{3,2,1,0:T(8,128)}, f32[4,3,64,256]{3,2,1,0:T(8,128)S(1)}, u32[]{:S(2)}) copy-start(f32[4,3,64,256]{3,2,1,0:T(8,128)S(1)} %collective-permute-done.13.refs_0_.refs_1_) | copy-start | bytes 2359300
  79.3 2.3 %copy-start.5 = (f32[4,3,64,256]{3,2,1,0:T(8,128)}, f32[4,3,64,256]{3,2,1,0:T(8,128)S(1)}, u32[]{:S(2)}) copy-start(f32[4,3,64,256]{3,2,1,0:T(8,128)S(1)} %collective-permute-done.12.refs_0_) | copy-start | bytes 2359300
  79.3 9.1 %copy-start.9 = (f32[2,64,256]{2,1,0:T(8,128)S(1)}, f32[2,64,256]{2,1,0:T(8,128)}, u32[]{:S(2)}) copy-start(f32[2,64,256]{2,1,0:T(8,128)} %copy-done.8) | copy-start | bytes 393220
  81.6 16.1 %all-to-all-start = ((f32[8,8,8,256]{3,2,1,0:T(8,128)}), f32[8,8,8,256]{3,2,1,0:T(8,128)S(1)}, u32[]{:S(2)}, u32[]{:S(2)}) async-start(f32[8,8,8,256]{3,2,1,0:T(8,128)} %get-tuple-element.131), calls=%async_computation | async-start | bytes 1048576 | tf_op jit(solution)/shard_map/all_to_all | solution.py:1007
